TPU v7x, 32 devices: a whole 2x2x4 slice. The times are simulated.
32 devices in a mesh: grp: 2 (over x), row: 16 (over z, y, core).
Axes of the slice: x: 2, y: 2, z: 4, core: 2. Of those that a mesh axis runs over, the one named last changes fastest.
Arguments:
- excitations: bfloat16 [32, 8192, 128], P('grp', 'row'), parts along dimension 0, may hold values from -0.005859375 to 0.005859375
- valence_orb: bfloat16 [2048, 128], P(('grp', 'row')), parts along dimension 0, may hold values from -6 to 6
- conduction_orb: bfloat16 [2048, 8192], P(('grp', 'row')), parts along dimension 0, may hold values from -6 to 6
- screened: bfloat16 [2048, 1024], P(('grp', 'row')), parts along dimension 0, may hold values from -0.005859375 to 0.005859375
Outputs:
- action: bfloat16 [32, 8192, 128], P('grp', 'row'), parts along dimension 0
There are 2 independent parts, one for each index of `grp`. A program takes and returns all parts, laid end to end along the dimension named above; each array names one. Nothing has to cross between parts.
All inputs are finite; a program needn't handle non-finite values.
Results may differ from a plain program's by a relative error of at most 0.0064.
Values may be sent and summed in bfloat16 or wider, within the bound.
No kernel may reach another device: no remote copies, remote signals or barrier semaphores. Data moves between devices by JAX's collectives and lax.ppermute only.
A program may use at most 64 MiB of HBM per device.

v0:
```python
import math

import jax
import jax.numpy as jnp
from jax import lax
from jax.sharding import PartitionSpec as P


def over_blocks(total_rows, step_fn, initial):
    span_size = math.gcd(total_rows, 2048)
    block_count = total_rows // span_size
    if block_count == 1:
        return step_fn(initial, 0, span_size)
    return lax.fori_loop(
        0, block_count, lambda index, carry: step_fn(carry, index * span_size, span_size), initial
    )


def density_rows(flat_exc, batch, valence_rows, cond_rows):
    total_rows = valence_rows.shape[0]
    cond_local = cond_rows.shape[1]
    initial = jnp.zeros((batch, total_rows), jnp.float32)

    def step_fn(carry, offset, span_size):
        val_block = lax.dynamic_slice_in_dim(valence_rows, offset, span_size, 0)
        cond_block = lax.dynamic_slice_in_dim(cond_rows, offset, span_size, 0)
        mixed = lax.dot_general(
            flat_exc, val_block, (((1,), (1,)), ((), ())), preferred_element_type=jnp.float32
        )
        mixed = mixed.reshape(batch, cond_local, span_size)
        summed = jnp.sum(mixed * cond_block.T.astype(jnp.float32)[None], axis=1)
        return lax.dynamic_update_slice_in_dim(carry, summed, offset, 1)

    return over_blocks(total_rows, step_fn, initial)


def projection(carry, valence_rows, cond_rows, field_cols):
    total_rows = valence_rows.shape[0]
    batch = field_cols.shape[0]
    cond_local = cond_rows.shape[1]

    def step_fn(inner, offset, span_size):
        val_block = lax.dynamic_slice_in_dim(valence_rows, offset, span_size, 0)
        cond_block = lax.dynamic_slice_in_dim(cond_rows, offset, span_size, 0)
        field_block = lax.dynamic_slice_in_dim(field_cols, offset, span_size, 1)
        pair = (
            cond_block.T.astype(jnp.float32)[None] * field_block.astype(jnp.float32)[:, None, :]
        ).astype(jnp.bfloat16)
        pair = pair.reshape(batch * cond_local, span_size)
        return inner + jnp.dot(pair, val_block, preferred_element_type=jnp.float32)

    return over_blocks(total_rows, step_fn, carry)


def body(excitations, valence_orb, conduction_orb, screened):
    batch, cond_local, valence = excitations.shape
    flat_exc = excitations.reshape(batch * cond_local, valence)
    valence_whole = lax.all_gather(valence_orb, "row", axis=0, tiled=True)
    cond_rows = lax.all_to_all(conduction_orb, "row", split_axis=1, concat_axis=0, tiled=True)
    partial_density = density_rows(flat_exc, batch, valence_whole, cond_rows)
    density_whole = lax.psum(partial_density, "row").astype(jnp.bfloat16)
    field_mine = lax.dot_general(
        density_whole, screened, (((1,), (1,)), ((), ())), preferred_element_type=jnp.float32
    ).astype(jnp.bfloat16)
    initial = jnp.zeros((batch * cond_local, valence), jnp.float32)
    summed = projection(
        initial, valence_whole, cond_rows, lax.all_gather(field_mine, "row", axis=1, tiled=True)
    )
    return summed.reshape(batch, cond_local, valence).astype(jnp.bfloat16)


def solution(mesh):
    in_specs = (
        P("grp", "row", None),
        P(("grp", "row"), None),
        P(("grp", "row"), None),
        P(("grp", "row"), None),
    )
    out_specs = P("grp", "row", None)
    return jax.shard_map(body, mesh=mesh, in_specs=in_specs, out_specs=out_specs, check_vma=False)
```

profile of v0, /device:TPU:0, one launch (start us, length us, event | category | flops | bytes accessed | tf_op | source)
XLA Modules:
  0.0 141.2 jit_solution(12085013585132656083)
XLA Ops:
  0.0 0.0 copy-start
  0.0 0.0 copy-start.2
  0.0 2.5 %copy.15 = bf16[8,16,8,512]{3,2,0,1:T(8,128)(2,1)} copy(bf16[8,16,8,512]{3,2,1,0:T(8,128)(2,1)} %bitcast.26) | data formatting | bytes 2097152 | tf_op jit(solution)/shard_map/all_to_all | solution.py:59
  2.5 7.4 %all-to-all-start = ((bf16[64,16,512]{2,0,1:T(8,128)(2,1)}), bf16[64,16,512]{2,0,1:T(8,128)(2,1)S(1)}, u32[]{:S(2)}, u32[]{:S(2)}) async-start(bf16[64,16,512]{2,0,1:T(8,128)(2,1)} %bitcast.25), calls=%async_computation | async-start | bytes 2097152 | tf_op jit(solution)/shard_map/all_to_all | solution.py:59
  9.9 0.0 copy-done.2
  9.9 34.5 %all_gather.6 = bf16[1024,128]{1,0:T(8,128)(2,1)S(1)} all-gather(bf16[64,128]{1,0:T(8,128)(2,1)S(1)} %copy-done.2), channel_id=1, replica_groups=mesh['grp'=2,'row'=16] {'row'}, dimensions={0}, use_global_device_ids=true | all-gather | bytes 278528 | tf_op jit(solution)/shard_map/all_gather | solution.py:58
  44.4 0.0 all-to-all-done
  44.4 1.6 %convert_element_type.41 = f32[64,16,512]{2,0,1:T(8,128)} convert(bf16[64,16,512]{2,0,1:T(8,128)(2,1)S(1)} %all-to-all-done) | non-fusion elementwise | flops 524288 | bytes 3145728 | tf_op jit(solution)/shard_map/convert_element_type | solution.py:47
  46.0 2.9 %copy.11 = f32[512,1024]{1,0:T(8,128)} copy(f32[512,1024]{0,1:T(8,128)} %bitcast.24) | data formatting | bytes 4194304 | tf_op jit(solution)/shard_map/convert_element_type | solution.py:47
  48.9 0.0 copy-done
  48.9 0.0 copy-start.1
  48.9 6.0 %multiply_reduce_fusion = f32[16,1024]{1,0:T(8,128)S(1)} fusion(f32[512,1024]{1,0:T(8,128)} %copy.11, bf16[16,512,128]{2,1,0:T(8,128)(2,1)S(1)} %copy-done, bf16[1024,128]{1,0:T(8,128)(2,1)S(1)} %all_gather.6), kind=kOutput, calls=%fused_computation.1 | convolution fusion | flops 2164244480 | bytes 4521984 | tf_op jit(solution)/shard_map/dot_general | solution.py:27
  54.9 61.8 %psum.7 = bf16[16,1024]{1,0:T(8,128)(2,1)S(1)} all-reduce(f32[16,1024]{1,0:T(8,128)S(1)} %multiply_reduce_fusion), channel_id=1, replica_groups=mesh['grp'=2,'row'=16] {'row'}, use_global_device_ids=true, to_apply=%region_1.0 | all-reduce | flops 16384 | bytes 98304 | tf_op jit(solution)/shard_map/psum | solution.py:61
  116.7 0.0 copy-done.1
  116.8 0.1 fusion.4
  116.9 17.3 %all-gather = bf16[16,64,16]{1,2,0:T(8,128)(2,1)S(1)} all-gather(bf16[1,64,16]{1,2,0:T(8,128)(2,1)S(1)} %fusion.4), channel_id=1, replica_groups=mesh['grp'=2,'row'=16] {'row'}, dimensions={0}, use_global_device_ids=true | all-gather | bytes 34816 | tf_op jit(solution)/shard_map/all_gather | solution.py:67
  134.2 0.1 reshape.19
  134.3 6.9 %fusion.3 = bf16[16,512,128]{2,1,0:T(8,128)(2,1)} fusion(f32[16,1024]{1,0:T(8,128)S(1)} %bitcast.27, f32[512,1024]{1,0:T(8,128)} %copy.11, bf16[1024,128]{1,0:T(8,128)(2,1)S(1)} %all_gather.6), kind=kOutput, calls=%fused_computation.5 | convolution fusion | flops 2165309440 | bytes 4521984 | tf_op jit(solution)/shard_map/dot_general | solution.py:50
  (1 shorter events, 0.0 us)
Async XLA Ops:
  0.0 48.9 %copy-start = (bf16[16,512,128]{2,1,0:T(8,128)(2,1)S(1)}, bf16[16,512,128]{2,1,0:T(8,128)(2,1)}, u32[]{:S(2)}) copy-start(bf16[16,512,128]{2,1,0:T(8,128)(2,1)} %param.4) | copy-start | bytes 6291460
  0.0 9.9 %copy-start.2 = (bf16[64,128]{1,0:T(8,128)(2,1)S(1)}, bf16[64,128]{1,0:T(8,128)(2,1)}, u32[]{:S(2)}) copy-start(bf16[64,128]{1,0:T(8,128)(2,1)} %param.5) | copy-start | bytes 49156
  2.5 41.9 %all-to-all-start = ((bf16[64,16,512]{2,0,1:T(8,128)(2,1)}), bf16[64,16,512]{2,0,1:T(8,128)(2,1)S(1)}, u32[]{:S(2)}, u32[]{:S(2)}) async-start(bf16[64,16,512]{2,0,1:T(8,128)(2,1)} %bitcast.25), calls=%async_computation | async-start | bytes 2097152 | tf_op jit(solution)/shard_map/all_to_all | solution.py:59
  48.9 67.8 %copy-start.1 = (bf16[64,1024]{1,0:T(8,128)(2,1)S(1)}, bf16[64,1024]{1,0:T(8,128)(2,1)}, u32[]{:S(2)}) copy-start(bf16[64,1024]{1,0:T(8,128)(2,1)} %param.7) | copy-start | bytes 393220
where the time goes:
time: 142 us; the launch traced here: 141 us
  blocking collectives  114 us (80%)
  matrix products  13.1 us (9%)
  starting transfers between devices  7.39 us (5%)
  local copies, waits for them, and re-layouts  5.54 us (4%)
  other arithmetic  1.6 us (1%)
    psum x1, blocking collectives, body(): density_whole = lax.psum(partial_density, 'row').astype(jnp.bfloat16)  61.8 us
    all_gather x1, blocking collectives, body(): valence_whole = lax.all_gather(valence_orb, 'row', axis=0, tiled=True)  34.5 us
    all_gather x1, blocking collectives, body(): lax.all_gather(field_mine, 'row', axis=1, tiled=True)  17.3 us
    all_to_all x1, starting transfers between devices, body(): lax.all_to_all(conduction_orb, 'row', split_axis=1, concat_axis=0, tiled=...  7.39 us
    dot_general x1, matrix products, step_fn(): return inner + jnp.dot(pair, val_block, preferred_element_type=jnp.float32)  6.93 us
    dot_general x1, matrix products, step_fn(): lax.dot_general(flat_exc, val_block, (((1,), (1,)), ((), ())), preferred_...  6.01 us
    convert_element_type x1, local copies, waits for them, and re-layouts, step_fn(): cond_block.T.astype(jnp.float32)[None]  2.94 us
  transfers between devices with their start and end apart: 1, of which 0 were waited for; matrix products, arithmetic and copies ran while one was open for 0% of the time, Pallas kernels for 0%

commit v1 on v0

v1 whole, which is shorter than its diff:
```python
import functools
import math

import jax
import jax.numpy as jnp
from jax import lax
from jax.experimental import pallas as pl
from jax.experimental.pallas import tpu as pltpu
from jax.sharding import PartitionSpec as P

AXIS = "row"
VMEM = pltpu.VMEM
NT = (((1,), (1,)), ((), ()))


def swap(x, bits, size):
    return lax.ppermute(x, AXIS, [(i, i ^ bits) for i in range(size)])


def exchange(x, step, count, size):
    return [x] + [swap(x, k * step, size) for k in range(1, count)]


def density_kernel(exc_ref, val_ref, cond_ref, out_ref):
    batch, valence, _ = exc_ref.shape
    cond, val = cond_ref[...], val_ref[...].astype(jnp.float32)
    group = math.gcd(batch, 4)
    sums = []
    for first in range(0, batch, group):
        exc = exc_ref[first : first + group].reshape(group * valence, -1)
        mixed = lax.dot_general(exc, cond, NT, preferred_element_type=jnp.float32)
        mixed = mixed.reshape(group, valence, -1) * val[None]
        sums.append(jnp.sum(mixed, axis=1))
    out_ref[...] = jnp.concatenate(sums, axis=0).astype(out_ref.dtype)


def partial_density(exc_t, val_t, cond_all):
    batch, valence, cond_local = exc_t.shape
    points = cond_all.shape[0]
    width = math.gcd(points, 1024)
    return pl.pallas_call(
        density_kernel,
        grid=(points // width,),
        in_specs=[
            pl.BlockSpec(memory_space=VMEM),
            pl.BlockSpec((valence, width), lambda i: (0, i)),
            pl.BlockSpec((width, cond_local), lambda i: (i, 0)),
        ],
        out_specs=pl.BlockSpec((batch, width), lambda i: (0, i)),
        out_shape=jax.ShapeDtypeStruct((batch, points), jnp.bfloat16),
        compiler_params=pltpu.CompilerParams(vmem_limit_bytes=24 << 20),
        cost_estimate=pl.CostEstimate(
            flops=2 * exc_t.size * points,
            bytes_accessed=2 * (exc_t.size + cond_all.size + val_t.size),
            transcendentals=0,
        ),
    )(exc_t, val_t, cond_all)


def action_kernel(z_ref, cond_ref, val_ref, *refs, layers, span):
    fields, (out_ref, held_ref, total_ref, sems) = refs[:layers], refs[layers:]
    batch = held_ref.shape[1]
    valence = val_ref.shape[0]
    for k, field in enumerate(fields):
        held_ref[z_ref[0] ^ k] = field[...].astype(jnp.float32)
    copies = []
    for first in range(0, batch, span):
        sides = []
        for b in range(first, first + span):
            row = jnp.concatenate([held_ref[k, b : b + 1, :] for k in range(layers)], axis=1)
            sides.append((val_ref[...].astype(jnp.float32) * row).astype(jnp.bfloat16))
        weights = jnp.concatenate(sides, axis=0)
        total = lax.dot_general(cond_ref[...], weights, NT, preferred_element_type=jnp.float32)
        for part in range(span):
            total_ref[first + part] = total[:, part * valence : (part + 1) * valence].astype(total_ref.dtype)
        piece = pl.ds(first, span)
        copies.append(pltpu.make_async_copy(total_ref.at[piece], out_ref.at[piece], sems.at[first // span]))
        copies[-1].start()
    for copy in copies:
        copy.wait()


def action_of(z, cond_t, val_t, fields):
    cond_local, points = cond_t.shape
    valence = val_t.shape[0]
    layers, (batch, chunk) = len(fields), fields[0].shape
    span = batch
    while span > 1 and span * valence * points * 2 > 1 << 20:
        span //= 2
    span = math.gcd(batch, span)
    whole = pl.BlockSpec(memory_space=VMEM)
    shape = (batch, cond_local, valence)
    return pl.pallas_call(
        functools.partial(action_kernel, layers=layers, span=span),
        in_specs=[pl.BlockSpec(memory_space=pltpu.SMEM)] + [whole] * (2 + layers),
        out_specs=pl.BlockSpec(memory_space=pl.ANY),
        out_shape=jax.ShapeDtypeStruct(shape, jnp.bfloat16),
        scratch_shapes=[
            pltpu.VMEM((layers, batch, chunk), jnp.float32),
            pltpu.VMEM(shape, jnp.bfloat16),
            pltpu.SemaphoreType.DMA((batch // span,)),
        ],
        compiler_params=pltpu.CompilerParams(vmem_limit_bytes=32 << 20),
        cost_estimate=pl.CostEstimate(
            flops=2 * batch * valence * cond_local * points,
            bytes_accessed=2 * (cond_t.size + val_t.size + batch * cond_local * valence),
            transcendentals=0,
        ),
    )(z, cond_t, val_t, *fields)


def body(size, excitations, valence_orb, conduction_orb, screened):
    batch, cond_local, valence = excitations.shape
    rows = valence_orb.shape[0]
    points = rows * size
    q_size = 1 << ((size.bit_length() - 1) // 2)
    z_size = size // q_size
    index = lax.axis_index(AXIS)
    z, q = index // q_size, index % q_size

    blocks = conduction_orb.reshape(rows, size, cond_local).transpose(1, 0, 2)
    blocks, valence_orb, screened = lax.optimization_barrier((blocks, valence_orb, screened))
    cond_all = lax.all_to_all(blocks, AXIS, split_axis=0, concat_axis=0, tiled=True)
    cond_all = cond_all.reshape(points, cond_local)

    val = jnp.concatenate(exchange(valence_orb, q_size, z_size, size), axis=0)
    val = jnp.stack(exchange(val, 1, q_size, size)).reshape(size, rows, valence)
    val = jnp.concatenate(
        [val[((i % q_size) ^ q) * z_size + ((i // q_size) ^ z)] for i in range(size)], axis=0
    )
    val_t = val.T
    scr = jnp.stack(exchange(screened, 1, q_size, size))
    scr = jnp.concatenate([scr[k ^ q] for k in range(q_size)], axis=0)
    exc_t = excitations.transpose(0, 2, 1)

    density = partial_density(exc_t, val_t, cond_all)
    density = sum(d.astype(jnp.float32) for d in exchange(density, q_size, z_size, size))
    partial = lax.dot_general(
        density.astype(jnp.bfloat16), scr, NT, preferred_element_type=jnp.float32
    )
    sent = partial.astype(jnp.bfloat16)
    field = partial + sum(f.astype(jnp.float32) for f in exchange(sent, 1, q_size, size)[1:])
    fields = exchange(field.astype(jnp.bfloat16), q_size, z_size, size)
    return action_of(z.reshape(1), cond_all.T, val_t, fields)


def solution(mesh):
    in_specs = (
        P("grp", "row", None),
        P(("grp", "row"), None),
        P(("grp", "row"), None),
        P(("grp", "row"), None),
    )
    out_specs = P("grp", "row", None)
    size = mesh.shape[AXIS]
    return jax.shard_map(
        functools.partial(body, size),
        mesh=mesh,
        in_specs=in_specs,
        out_specs=out_specs,
        check_vma=False,
    )
```

time: 142 us -> 84.7 us (0.60)
  blocking collectives: 114 us -> 0 us
  waiting for transfers between devices: 0.01 us -> 32.8 us
  starting transfers between devices: 7.39 us -> 26.4 us
  matrix products: 13.1 us -> 0.23 us
  local copies, waits for them, and re-layouts: 5.54 us -> 16.9 us
  Pallas kernels: 0 us -> 5.6 us
    psum x1 -> x0, blocking collectives: 61.8 us -> none  [body(): density_whole = lax.psum(partial_density, 'row').astype(jnp.bfloat16)]
    all_gather x2 -> x0, blocking collectives: 51.8 us -> none  [the longest x1 34.5 us: body(): valence_whole = lax.all_gather(valence_orb, 'row', axis=0, tiled=True)]
    ppermute x0 -> x18, waiting for transfers between devices: none -> 32.8 us  [swap(): return lax.ppermute(x, AXIS, [(i, i ^ bits) for i in range(size)])]
    ppermute x0 -> x18, starting transfers between devices: none -> 19 us  [swap(): return lax.ppermute(x, AXIS, [(i, i ^ bits) for i in range(size)])]
    unnamed x6 -> x25, local copies, waits for them, and re-layouts: 0.01 us -> 13.6 us
    dot_general x3 -> x1, matrix products: 13.1 us -> 0.23 us  [body(): lax.dot_general(density.astype(jnp.bfloat16), scr, NT, preferred_element_...]
    pallas_call x0 -> x2, Pallas kernels: none -> 5.6 us  [the longest x1 3.21 us: action_of(): pl.pallas_call(functools.partial(action_kernel, layers=layers, span=span)...]
    convert_element_type x3 -> x0, local copies, waits for them, and re-layouts: 3.06 us -> none  [the longest x1 2.94 us: step_fn(): cond_block.T.astype(jnp.float32)[None]]
  transfers between devices with their start and end apart: 1 -> 19, of which waited for: 0 -> 7; matrix products, arithmetic and copies ran while one was open for 0% -> 19% of each run, Pallas kernels for 0% -> 0%
where the time goes in v1:
time: 84.7 us; the launch traced here: 84.3 us
  waiting for transfers between devices  32.8 us (39%)
  starting transfers between devices  26.4 us (31%)
  local copies, waits for them, and re-layouts  16.9 us (20%)
  Pallas kernels  5.6 us (7%)
  other arithmetic  2.02 us (2%)
    ppermute x18, waiting for transfers between devices, swap(): return lax.ppermute(x, AXIS, [(i, i ^ bits) for i in range(size)])  32.8 us
    ppermute x18, starting transfers between devices, swap(): return lax.ppermute(x, AXIS, [(i, i ^ bits) for i in range(size)])  19 us
    unnamed x25, local copies, waits for them, and re-layouts  13.6 us
    all_to_all x1, starting transfers between devices, body(): lax.all_to_all(blocks, AXIS, split_axis=0, concat_axis=0, tiled=True)  7.39 us
    pallas_call x1, Pallas kernels, action_of(): pl.pallas_call(functools.partial(action_kernel, layers=layers, span=span)...  3.21 us
    pallas_call x1, Pallas kernels, partial_density(): pl.pallas_call(density_kernel, grid=(points // width,), in_specs=[pl.Bloc...  2.38 us
    another operation x1, other arithmetic, body(): scr = jnp.stack(exchange(screened, 1, q_size, size))  1.97 us
  transfers between devices with their start and end apart: 19, of which 7 were waited for; matrix products, arithmetic and copies ran while one was open for 19% of the time, Pallas kernels for 0%

profile of v1, /device:TPU:0, one launch (start us, length us, event | category | flops | bytes accessed | tf_op | source)
XLA Modules:
  0.0 84.3 jit_solution(3954786729155490112)
XLA Ops:
  0.0 1.6 %copy.96 = bf16[8,8,16,512]{3,2,1,0:T(8,128)(2,1)S(1)} copy(bf16[8,8,16,512]{3,1,2,0:T(8,128)(2,1)} %bitcast.49) | data formatting | bytes 2097152
  1.6 1.5 %copy.61 = bf16[16,64,512]{2,1,0:T(8,128)(2,1)} copy(bf16[16,64,512]{2,0,1:T(8,128)(2,1)S(1)} %bitcast.48) | data formatting | bytes 2097152 | tf_op jit(solution)/shard_map/optimization_barrier | solution.py:122
  3.1 7.4 %all-to-all-start = ((bf16[16,64,512]{2,1,0:T(8,128)(2,1)}), bf16[16,64,512]{2,1,0:T(8,128)(2,1)S(1)}, u32[]{:S(2)}, u32[]{:S(2)}) async-start(bf16[16,64,512]{2,1,0:T(8,128)(2,1)} %copy.61), calls=%async_computation | async-start | bytes 2097152 | tf_op jit(solution)/shard_map/all_to_all | solution.py:123
  10.5 2.0 %collective-permute-start = (bf16[64,128]{1,0:T(8,128)(2,1)S(1)}, bf16[64,128]{1,0:T(8,128)(2,1)S(1)}, u32[]{:S(2)}, u32[]{:S(2)}) collective-permute-start(bf16[64,128]{1,0:T(8,128)(2,1)S(1)} %copy-done.1), channel_id=1, source_target_pairs={{0,4},{1,5},{2,6},{3,7},{4,0},{5,1},{6,2},{7,3},{8,12},{9,13},{10,... | collective-permute-start | bytes 49160 | tf_op jit(solution)/shard_map/ppermute | solution.py:17
  12.5 2.4 %collective-permute-start.1 = (bf16[64,128]{1,0:T(8,128)(2,1)S(1)}, bf16[64,128]{1,0:T(8,128)(2,1)S(1)}, u32[]{:S(2)}, u32[]{:S(2)}) collective-permute-start(bf16[64,128]{1,0:T(8,128)(2,1)S(1)} %copy-done.1), channel_id=1, source_target_pairs={{0,8},{1,9},{2,10},{3,11},{4,12},{5,13},{6,14},{7,15},{8,0},{9,1},... | collective-permute-start | bytes 49160 | tf_op jit(solution)/shard_map/ppermute | solution.py:17
  15.0 14.1 %collective-permute-done = bf16[64,128]{1,0:T(8,128)(2,1)S(1)} collective-permute-done((bf16[64,128]{1,0:T(8,128)(2,1)S(1)}, bf16[64,128]{1,0:T(8,128)(2,1)S(1)}, u32[]{:S(2)}, u32[]{:S(2)}) %collective-permute-start) | collective-permute-done | bytes 16416 | tf_op jit(solution)/shard_map/ppermute | solution.py:17
  29.1 9.2 %collective-permute-done.1 = bf16[64,128]{1,0:T(8,128)(2,1)S(1)} collective-permute-done((bf16[64,128]{1,0:T(8,128)(2,1)S(1)}, bf16[64,128]{1,0:T(8,128)(2,1)S(1)}, u32[]{:S(2)}, u32[]{:S(2)}) %collective-permute-start.1) | collective-permute-done | bytes 16416 | tf_op jit(solution)/shard_map/ppermute | solution.py:17
  38.4 1.5 %collective-permute-start.4 = (bf16[256,128]{1,0:T(8,128)(2,1)S(1)}, bf16[256,128]{1,0:T(8,128)(2,1)S(1)}, u32[]{:S(2)}, u32[]{:S(2)}) collective-permute-start(bf16[256,128]{1,0:T(8,128)(2,1)S(1)} %constant_dynamic-update-slice_fusion), channel_id=1, source_target_pairs={{0,2},{1,3},{2,0},{3,1},{4,6},{5,7},{6,4},{7,5},{8,10},{9,11},{10,... | collective-permute-start | bytes 196616 | tf_op jit(solution)/shard_map/ppermute | solution.py:17
  40.6 1.5 %collective-permute-start.10 = (bf16[64,1024]{1,0:T(8,128)(2,1)}, bf16[64,1024]{1,0:T(8,128)(2,1)}, u32[]{:S(2)}, u32[]{:S(2)}) collective-permute-start(bf16[64,1024]{1,0:T(8,128)(2,1)} %param.7), channel_id=1, source_target_pairs={{0,2},{1,3},{2,0},{3,1},{4,6},{5,7},{6,4},{7,5},{8,10},{9,11},{10,... | collective-permute-start | bytes 393224 | tf_op jit(solution)/shard_map/ppermute | solution.py:17
  42.1 2.9 %copy.79 = bf16[16,512,128]{1,2,0:T(8,128)(2,1)S(1)} copy(bf16[16,512,128]{2,1,0:T(8,128)(2,1)} %param.4) | data formatting | bytes 4194304 | tf_op args[0]
  45.9 0.7 copy.85
  48.0 0.7 copy.88
  48.7 0.7 copy.89
  49.5 0.7 copy.90
  50.2 0.7 copy.91
  52.3 0.7 copy.94
  53.8 0.7 copy.80
  54.5 1.1 %concatenate.10 = bf16[1024,128]{0,1:T(8,128)(2,1)S(1)} concatenate(bf16[64,128]{0,1:T(8,128)(2,1)} %bitcast.66, bf16[64,128]{0,1:T(8,128)(2,1)S(1)} %bitcast.51, bf16[64,128]{0,1:T(8,128)(2,1)S(1)} %bitcast.52, bf16[64,128]{0,1:T(8,128)(2,1)S(1)} %bitcast.53, bf16[64,128]{0,1:T(8,128)(2,1)S(1)} %bitcast.54, bf16[64,128]{0,1:T(8,128)(2,1)} %bitcast.55, bf16[64,128]{0,1:T(8,128)(2,1)} %bitcast.56, ...), dimensions={0} | concatenate | bytes 524288 | tf_op jit(solution)/shard_map/concatenate | solution.py:128
  55.7 2.0 %pad_maximum_fusion = bf16[4,64,1024]{2,1,0:T(8,128)(2,1)} fusion(bf16[1,64,1024]{2,1,0:T(8,128)(2,1)} %bitcast.30, bf16[1,64,1024]{2,1,0:T(8,128)(2,1)} %bitcast.29, bf16[1,64,1024]{2,1,0:T(8,128)(2,1)} %bitcast.28, bf16[1,64,1024]{2,1,0:T(8,128)(2,1)} %bitcast.27), kind=kLoop, calls=%fused_computation | loop fusion | flops 786432 | bytes 1048576 | tf_op jit(solution)/shard_map/stack | solution.py:132
  57.6 2.4 %shard_map.46 = bf16[16,1024]{1,0:T(8,128)(2,1)S(1)} custom-call(bf16[16,128,512]{2,1,0:T(8,128)(2,1)S(1)} %bitcast.44, bf16[128,1024]{1,0:T(8,128)(2,1)S(1)} %bitcast.46, bf16[1024,512]{1,0:T(8,128)(2,1)S(1)} %bitcast.42), custom_call_target="tpu_custom_call" | custom-call | flops 2147483648 | bytes 3407872 | tf_op jit(solution)/shard_map/pallas_call | solution.py:41
  60.0 0.7 collective-permute-start.6
  60.8 1.4 %collective-permute-start.7 = (bf16[16,1024]{1,0:T(8,128)(2,1)S(1)}, bf16[16,1024]{1,0:T(8,128)(2,1)S(1)}, u32[]{:S(2)}, u32[]{:S(2)}) collective-permute-start(bf16[16,1024]{1,0:T(8,128)(2,1)S(1)} %shard_map.46), channel_id=1, source_target_pairs={{0,8},{1,9},{2,10},{3,11},{4,12},{5,13},{6,14},{7,15},{8,0},{9,1},... | collective-permute-start | bytes 98312 | tf_op jit(solution)/shard_map/ppermute | solution.py:17
  62.1 2.4 %collective-permute-start.8 = (bf16[16,1024]{1,0:T(8,128)(2,1)S(1)}, bf16[16,1024]{1,0:T(8,128)(2,1)S(1)}, u32[]{:S(2)}, u32[]{:S(2)}) collective-permute-start(bf16[16,1024]{1,0:T(8,128)(2,1)S(1)} %shard_map.46), channel_id=1, source_target_pairs={{0,12},{1,13},{2,14},{3,15},{4,8},{5,9},{6,10},{7,11},{8,4},{9,5},... | collective-permute-start | bytes 98312 | tf_op jit(solution)/shard_map/ppermute | solution.py:17
  64.5 1.4 %collective-permute-done.7 = bf16[16,1024]{1,0:T(8,128)(2,1)S(1)} collective-permute-done((bf16[16,1024]{1,0:T(8,128)(2,1)S(1)}, bf16[16,1024]{1,0:T(8,128)(2,1)S(1)}, u32[]{:S(2)}, u32[]{:S(2)}) %collective-permute-start.7) | collective-permute-done | bytes 32800 | tf_op jit(solution)/shard_map/ppermute | solution.py:17
  66.0 1.8 %collective-permute-done.8 = bf16[16,1024]{1,0:T(8,128)(2,1)S(1)} collective-permute-done((bf16[16,1024]{1,0:T(8,128)(2,1)S(1)}, bf16[16,1024]{1,0:T(8,128)(2,1)S(1)}, u32[]{:S(2)}, u32[]{:S(2)}) %collective-permute-start.8) | collective-permute-done | bytes 32800 | tf_op jit(solution)/shard_map/ppermute | solution.py:17
  68.1 1.5 %collective-permute-start.13 = (bf16[16,256]{1,0:T(8,128)(2,1)S(1)}, bf16[16,256]{1,0:T(8,128)(2,1)S(1)}, u32[]{:S(2)}, u32[]{:S(2)}) collective-permute-start(bf16[16,256]{1,0:T(8,128)(2,1)S(1)} %get-tuple-element.31), channel_id=1, source_target_pairs={{0,2},{1,3},{2,0},{3,1},{4,6},{5,7},{6,4},{7,5},{8,10},{9,11},{10,... | collective-permute-start | bytes 24584 | tf_op jit(solution)/shard_map/ppermute | solution.py:17
  70.0 1.8 %collective-permute-done.13 = bf16[16,256]{1,0:T(8,128)(2,1)S(1)} collective-permute-done((bf16[16,256]{1,0:T(8,128)(2,1)S(1)}, bf16[16,256]{1,0:T(8,128)(2,1)S(1)}, u32[]{:S(2)}, u32[]{:S(2)}) %collective-permute-start.13) | collective-permute-done | bytes 8224 | tf_op jit(solution)/shard_map/ppermute | solution.py:17
  71.8 0.9 %collective-permute-done.14 = bf16[16,256]{1,0:T(8,128)(2,1)S(1)} collective-permute-done((bf16[16,256]{1,0:T(8,128)(2,1)S(1)}, bf16[16,256]{1,0:T(8,128)(2,1)S(1)}, u32[]{:S(2)}, u32[]{:S(2)}) %collective-permute-start.14) | collective-permute-done | bytes 8224 | tf_op jit(solution)/shard_map/ppermute | solution.py:17
  72.7 2.9 %collective-permute-start.16 = (bf16[16,256]{1,0:T(8,128)(2,1)S(1)}, bf16[16,256]{1,0:T(8,128)(2,1)S(1)}, u32[]{:S(2)}, u32[]{:S(2)}) collective-permute-start(bf16[16,256]{1,0:T(8,128)(2,1)S(1)} %add_convert_fusion.2.refs_0_), channel_id=1, source_target_pairs={{0,8},{1,9},{2,10},{3,11},{4,12},{5,13},{6,14},{7,15},{8,0},{9,1},... | collective-permute-start | bytes 24584 | tf_op jit(solution)/shard_map/ppermute | solution.py:17
  75.6 1.4 %collective-permute-start.17 = (bf16[16,256]{1,0:T(8,128)(2,1)S(1)}, bf16[16,256]{1,0:T(8,128)(2,1)S(1)}, u32[]{:S(2)}, u32[]{:S(2)}) collective-permute-start(bf16[16,256]{1,0:T(8,128)(2,1)S(1)} %add_convert_fusion.2.refs_0_), channel_id=1, source_target_pairs={{0,12},{1,13},{2,14},{3,15},{4,8},{5,9},{6,10},{7,11},{8,4},{9,5},... | collective-permute-start | bytes 24584 | tf_op jit(solution)/shard_map/ppermute | solution.py:17
  77.6 3.5 %collective-permute-done.17.refs_3_ = bf16[16,256]{1,0:T(8,128)(2,1)S(1)} collective-permute-done((bf16[16,256]{1,0:T(8,128)(2,1)S(1)}, bf16[16,256]{1,0:T(8,128)(2,1)S(1)}, u32[]{:S(2)}, u32[]{:S(2)}) %collective-permute-start.17) | collective-permute-done | bytes 8224 | tf_op jit(solution)/shard_map/ppermute | solution.py:17
  81.1 3.2 %shard_map.47 = bf16[16,512,128]{2,1,0:T(8,128)(2,1)} custom-call(s32[1]{0:T(128)} %bitcast.z_ref, bf16[512,1024]{1,0:T(8,128)(2,1)S(1)} %bitcast.45, bf16[128,1024]{1,0:T(8,128)(2,1)S(1)} %bitcast.47, bf16[16,256]{1,0:T(8,128)(2,1)S(1)} %add_convert_fusion.2.refs_0_, bf16[16,256]{1,0:T(8,128)(2,1)S(1)} %collective-permute-done.15.refs_1_, ...), custom_call_target="tpu_custom_call" | custom-call | flops 2147483648 | bytes 3407872 | tf_op jit(solution)/shard_map/pallas_call | solution.py:93
  (43 shorter events, 6.3 us)
Async XLA Ops:
  1.6 9.0 %copy-start.1 = (bf16[64,128]{1,0:T(8,128)(2,1)S(1)}, bf16[64,128]{1,0:T(8,128)(2,1)}, u32[]{:S(2)}) copy-start(bf16[64,128]{1,0:T(8,128)(2,1)} %param.5) | copy-start | bytes 49156
  3.1 54.5 %all-to-all-start = ((bf16[16,64,512]{2,1,0:T(8,128)(2,1)}), bf16[16,64,512]{2,1,0:T(8,128)(2,1)S(1)}, u32[]{:S(2)}, u32[]{:S(2)}) async-start(bf16[16,64,512]{2,1,0:T(8,128)(2,1)} %copy.61), calls=%async_computation | async-start | bytes 2097152 | tf_op jit(solution)/shard_map/all_to_all | solution.py:123
  10.5 18.6 %collective-permute-start = (bf16[64,128]{1,0:T(8,128)(2,1)S(1)}, bf16[64,128]{1,0:T(8,128)(2,1)S(1)}, u32[]{:S(2)}, u32[]{:S(2)}) collective-permute-start(bf16[64,128]{1,0:T(8,128)(2,1)S(1)} %copy-done.1), channel_id=1, source_target_pairs={{0,4},{1,5},{2,6},{3,7},{4,0},{5,1},{6,2},{7,3},{8,12},{9,13},{10,... | collective-permute-start | bytes 49160 | tf_op jit(solution)/shard_map/ppermute | solution.py:17
  12.5 25.8 %collective-permute-start.1 = (bf16[64,128]{1,0:T(8,128)(2,1)S(1)}, bf16[64,128]{1,0:T(8,128)(2,1)S(1)}, u32[]{:S(2)}, u32[]{:S(2)}) collective-permute-start(bf16[64,128]{1,0:T(8,128)(2,1)S(1)} %copy-done.1), channel_id=1, source_target_pairs={{0,8},{1,9},{2,10},{3,11},{4,12},{5,13},{6,14},{7,15},{8,0},{9,1},... | collective-permute-start | bytes 49160 | tf_op jit(solution)/shard_map/ppermute | solution.py:17
  14.9 23.4 %collective-permute-start.2 = (bf16[64,128]{1,0:T(8,128)(2,1)S(1)}, bf16[64,128]{1,0:T(8,128)(2,1)S(1)}, u32[]{:S(2)}, u32[]{:S(2)}) collective-permute-start(bf16[64,128]{1,0:T(8,128)(2,1)S(1)} %copy-done.1), channel_id=1, source_target_pairs={{0,12},{1,13},{2,14},{3,15},{4,8},{5,9},{6,10},{7,11},{8,4},{9,5},... | collective-permute-start | bytes 49160 | tf_op jit(solution)/shard_map/ppermute | solution.py:17
  38.3 6.7 %collective-permute-start.3 = (bf16[256,128]{1,0:T(8,128)(2,1)S(1)}, bf16[256,128]{1,0:T(8,128)(2,1)S(1)}, u32[]{:S(2)}, u32[]{:S(2)}) collective-permute-start(bf16[256,128]{1,0:T(8,128)(2,1)S(1)} %constant_dynamic-update-slice_fusion), channel_id=1, source_target_pairs={{0,1},{1,0},{2,3},{3,2},{4,5},{5,4},{6,7},{7,6},{8,9},{9,8},{10,11... | collective-permute-start | bytes 196616 | tf_op jit(solution)/shard_map/ppermute | solution.py:17
  38.4 6.8 %collective-permute-start.4 = (bf16[256,128]{1,0:T(8,128)(2,1)S(1)}, bf16[256,128]{1,0:T(8,128)(2,1)S(1)}, u32[]{:S(2)}, u32[]{:S(2)}) collective-permute-start(bf16[256,128]{1,0:T(8,128)(2,1)S(1)} %constant_dynamic-update-slice_fusion), channel_id=1, source_target_pairs={{0,2},{1,3},{2,0},{3,1},{4,6},{5,7},{6,4},{7,5},{8,10},{9,11},{10,... | collective-permute-start | bytes 196616 | tf_op jit(solution)/shard_map/ppermute | solution.py:17
  40.0 5.2 %collective-permute-start.5 = (bf16[256,128]{1,0:T(8,128)(2,1)S(1)}, bf16[256,128]{1,0:T(8,128)(2,1)S(1)}, u32[]{:S(2)}, u32[]{:S(2)}) collective-permute-start(bf16[256,128]{1,0:T(8,128)(2,1)S(1)} %constant_dynamic-update-slice_fusion), channel_id=1, source_target_pairs={{0,3},{1,2},{2,1},{3,0},{4,7},{5,6},{6,5},{7,4},{8,11},{9,10},{10,... | collective-permute-start | bytes 196616 | tf_op jit(solution)/shard_map/ppermute | solution.py:17
  40.3 15.4 %collective-permute-start.9 = (bf16[64,1024]{1,0:T(8,128)(2,1)}, bf16[64,1024]{1,0:T(8,128)(2,1)}, u32[]{:S(2)}, u32[]{:S(2)}) collective-permute-start(bf16[64,1024]{1,0:T(8,128)(2,1)} %param.7), channel_id=1, source_target_pairs={{0,1},{1,0},{2,3},{3,2},{4,5},{5,4},{6,7},{7,6},{8,9},{9,8},{10,11... | collective-permute-start | bytes 393224 | tf_op jit(solution)/shard_map/ppermute | solution.py:17
  40.6 15.0 %collective-permute-start.10 = (bf16[64,1024]{1,0:T(8,128)(2,1)}, bf16[64,1024]{1,0:T(8,128)(2,1)}, u32[]{:S(2)}, u32[]{:S(2)}) collective-permute-start(bf16[64,1024]{1,0:T(8,128)(2,1)} %param.7), channel_id=1, source_target_pairs={{0,2},{1,3},{2,0},{3,1},{4,6},{5,7},{6,4},{7,5},{8,10},{9,11},{10,... | collective-permute-start | bytes 393224 | tf_op jit(solution)/shard_map/ppermute | solution.py:17
  45.1 10.6 %collective-permute-start.11 = (bf16[64,1024]{1,0:T(8,128)(2,1)}, bf16[64,1024]{1,0:T(8,128)(2,1)}, u32[]{:S(2)}, u32[]{:S(2)}) collective-permute-start(bf16[64,1024]{1,0:T(8,128)(2,1)} %param.7), channel_id=1, source_target_pairs={{0,3},{1,2},{2,1},{3,0},{4,7},{5,6},{6,5},{7,4},{8,11},{9,10},{10,... | collective-permute-start | bytes 393224 | tf_op jit(solution)/shard_map/ppermute | solution.py:17
  57.6 6.8 %copy-start = (bf16[4,64,1024]{2,1,0:T(8,128)(2,1)S(1)}, bf16[4,64,1024]{2,1,0:T(8,128)(2,1)}, u32[]{:S(2)}) copy-start(bf16[4,64,1024]{2,1,0:T(8,128)(2,1)} %pad_maximum_fusion) | copy-start | bytes 1572868
  60.0 4.5 %collective-permute-start.6 = (bf16[16,1024]{1,0:T(8,128)(2,1)S(1)}, bf16[16,1024]{1,0:T(8,128)(2,1)S(1)}, u32[]{:S(2)}, u32[]{:S(2)}) collective-permute-start(bf16[16,1024]{1,0:T(8,128)(2,1)S(1)} %shard_map.46), channel_id=1, source_target_pairs={{0,4},{1,5},{2,6},{3,7},{4,0},{5,1},{6,2},{7,3},{8,12},{9,13},{10,... | collective-permute-start | bytes 98312 | tf_op jit(solution)/shard_map/ppermute | solution.py:17
  60.8 5.2 %collective-permute-start.7 = (bf16[16,1024]{1,0:T(8,128)(2,1)S(1)}, bf16[16,1024]{1,0:T(8,128)(2,1)S(1)}, u32[]{:S(2)}, u32[]{:S(2)}) collective-permute-start(bf16[16,1024]{1,0:T(8,128)(2,1)S(1)} %shard_map.46), channel_id=1, source_target_pairs={{0,8},{1,9},{2,10},{3,11},{4,12},{5,13},{6,14},{7,15},{8,0},{9,1},... | collective-permute-start | bytes 98312 | tf_op jit(solution)/shard_map/ppermute | solution.py:17
  62.1 5.7 %collective-permute-start.8 = (bf16[16,1024]{1,0:T(8,128)(2,1)S(1)}, bf16[16,1024]{1,0:T(8,128)(2,1)S(1)}, u32[]{:S(2)}, u32[]{:S(2)}) collective-permute-start(bf16[16,1024]{1,0:T(8,128)(2,1)S(1)} %shard_map.46), channel_id=1, source_target_pairs={{0,12},{1,13},{2,14},{3,15},{4,8},{5,9},{6,10},{7,11},{8,4},{9,5},... | collective-permute-start | bytes 98312 | tf_op jit(solution)/shard_map/ppermute | solution.py:17
  68.1 1.9 %collective-permute-start.12 = (bf16[16,256]{1,0:T(8,128)(2,1)S(1)}, bf16[16,256]{1,0:T(8,128)(2,1)S(1)}, u32[]{:S(2)}, u32[]{:S(2)}) collective-permute-start(bf16[16,256]{1,0:T(8,128)(2,1)S(1)} %get-tuple-element.31), channel_id=1, source_target_pairs={{0,1},{1,0},{2,3},{3,2},{4,5},{5,4},{6,7},{7,6},{8,9},{9,8},{10,11... | collective-permute-start | bytes 24584 | tf_op jit(solution)/shard_map/ppermute | solution.py:17
  68.1 3.7 %collective-permute-start.13 = (bf16[16,256]{1,0:T(8,128)(2,1)S(1)}, bf16[16,256]{1,0:T(8,128)(2,1)S(1)}, u32[]{:S(2)}, u32[]{:S(2)}) collective-permute-start(bf16[16,256]{1,0:T(8,128)(2,1)S(1)} %get-tuple-element.31), channel_id=1, source_target_pairs={{0,2},{1,3},{2,0},{3,1},{4,6},{5,7},{6,4},{7,5},{8,10},{9,11},{10,... | collective-permute-start | bytes 24584 | tf_op jit(solution)/shard_map/ppermute | solution.py:17
  69.6 3.1 %collective-permute-start.14 = (bf16[16,256]{1,0:T(8,128)(2,1)S(1)}, bf16[16,256]{1,0:T(8,128)(2,1)S(1)}, u32[]{:S(2)}, u32[]{:S(2)}) collective-permute-start(bf16[16,256]{1,0:T(8,128)(2,1)S(1)} %get-tuple-element.31), channel_id=1, source_target_pairs={{0,3},{1,2},{2,1},{3,0},{4,7},{5,6},{6,5},{7,4},{8,11},{9,10},{10,... | collective-permute-start | bytes 24584 | tf_op jit(solution)/shard_map/ppermute | solution.py:17
  72.7 4.9 %collective-permute-start.15 = (bf16[16,256]{1,0:T(8,128)(2,1)S(1)}, bf16[16,256]{1,0:T(8,128)(2,1)S(1)}, u32[]{:S(2)}, u32[]{:S(2)}) collective-permute-start(bf16[16,256]{1,0:T(8,128)(2,1)S(1)} %add_convert_fusion.2.refs_0_), channel_id=1, source_target_pairs={{0,4},{1,5},{2,6},{3,7},{4,0},{5,1},{6,2},{7,3},{8,12},{9,13},{10,... | collective-permute-start | bytes 24584 | tf_op jit(solution)/shard_map/ppermute | solution.py:17
  72.7 4.9 %collective-permute-start.16 = (bf16[16,256]{1,0:T(8,128)(2,1)S(1)}, bf16[16,256]{1,0:T(8,128)(2,1)S(1)}, u32[]{:S(2)}, u32[]{:S(2)}) collective-permute-start(bf16[16,256]{1,0:T(8,128)(2,1)S(1)} %add_convert_fusion.2.refs_0_), channel_id=1, source_target_pairs={{0,8},{1,9},{2,10},{3,11},{4,12},{5,13},{6,14},{7,15},{8,0},{9,1},... | collective-permute-start | bytes 24584 | tf_op jit(solution)/shard_map/ppermute | solution.py:17
  75.6 5.4 %collective-permute-start.17 = (bf16[16,256]{1,0:T(8,128)(2,1)S(1)}, bf16[16,256]{1,0:T(8,128)(2,1)S(1)}, u32[]{:S(2)}, u32[]{:S(2)}) collective-permute-start(bf16[16,256]{1,0:T(8,128)(2,1)S(1)} %add_convert_fusion.2.refs_0_), channel_id=1, source_target_pairs={{0,12},{1,13},{2,14},{3,15},{4,8},{5,9},{6,10},{7,11},{8,4},{9,5},... | collective-permute-start | bytes 24584 | tf_op jit(solution)/shard_map/ppermute | solution.py:17

commit v2 on v1

--- a/solution.py
+++ b/solution.py
@@ -48,7 +48,7 @@
         ],
         out_specs=pl.BlockSpec((batch, width), lambda i: (0, i)),
         out_shape=jax.ShapeDtypeStruct((batch, points), jnp.bfloat16),
-        compiler_params=pltpu.CompilerParams(vmem_limit_bytes=24 << 20),
+        compiler_params=pltpu.CompilerParams(vmem_limit_bytes=16 << 20),
         cost_estimate=pl.CostEstimate(
             flops=2 * exc_t.size * points,
             bytes_accessed=2 * (exc_t.size + cond_all.size + val_t.size),
@@ -100,7 +100,7 @@
             pltpu.VMEM(shape, jnp.bfloat16),
             pltpu.SemaphoreType.DMA((batch // span,)),
         ],
-        compiler_params=pltpu.CompilerParams(vmem_limit_bytes=32 << 20),
+        compiler_params=pltpu.CompilerParams(vmem_limit_bytes=16 << 20),
         cost_estimate=pl.CostEstimate(
             flops=2 * batch * valence * cond_local * points,
             bytes_accessed=2 * (cond_t.size + val_t.size + batch * cond_local * valence),
@@ -109,7 +109,7 @@
     )(z, cond_t, val_t, *fields)
 
 
-def body(size, excitations, valence_orb, conduction_orb, screened):
+def body_whole(size, excitations, valence_orb, conduction_orb, screened):
     batch, cond_local, valence = excitations.shape
     rows = valence_orb.shape[0]
     points = rows * size
@@ -142,6 +142,225 @@
     field = partial + sum(f.astype(jnp.float32) for f in exchange(sent, 1, q_size, size)[1:])
     fields = exchange(field.astype(jnp.bfloat16), q_size, z_size, size)
     return action_of(z.reshape(1), cond_all.T, val_t, fields)
+
+
+def slabs_of(index, cond, val, screened, chips, near):
+    width = cond.shape[1] // (2 * chips)
+    slabs = []
+    for k in range(chips):
+        parts = [lax.dynamic_slice_in_dim(cond, (index ^ j) * width, width, 1) for j in (2 * k, 2 * k + 1)]
+        slabs.append(jnp.concatenate(parts + [val] + [screened] * (k < near), axis=1))
+    return slabs
+
+
+def pack_kernel(*refs, first, middle):
+    *slabs, out_ref = refs
+    at = 0
+    for start, stop in [(first, middle), (middle, None)]:
+        for slab in slabs:
+            columns = (stop or slab.shape[1]) - start
+            if columns:
+                out_ref[:, at : at + columns] = slab[:, start : start + columns]
+                at += columns
+
+
+def pack(slabs, first, middle):
+    columns = sum(slab.shape[1] for slab in slabs) - first * len(slabs)
+    whole = pl.BlockSpec(memory_space=VMEM)
+    return pl.pallas_call(
+        functools.partial(pack_kernel, first=first, middle=middle),
+        in_specs=[whole] * len(slabs),
+        out_specs=whole,
+        out_shape=jax.ShapeDtypeStruct((slabs[0].shape[0], columns), slabs[0].dtype),
+        compiler_params=pltpu.CompilerParams(vmem_limit_bytes=8 << 20),
+        cost_estimate=pl.CostEstimate(flops=0, bytes_accessed=1 << 20, transcendentals=0),
+    )(*slabs)
+
+
+def density_part_kernel(*refs, blocks, val_at, step):
+    exc_ref, sources, (out_ref, cond_ref, val_ref) = refs[0], refs[1:-3], refs[-3:]
+    batch, valence, width = exc_ref.shape
+    rows = sources[0].shape[0]
+    val = []
+    for k in range(blocks):
+        source, start = (sources[k], 0) if len(sources) > 1 else (sources[0], k * step)
+        cond_ref[k * rows : (k + 1) * rows, :] = source[:, start : start + width]
+        val.append(source[:, start + val_at : start + val_at + valence])
+    val = jnp.concatenate(val, axis=0).T
+    val_ref[...] = val
+    val = val.astype(jnp.float32)
+    part = math.gcd(batch, 4)
+    sums = []
+    for first in range(0, batch, part):
+        exc = exc_ref[first : first + part].reshape(part * valence, width)
+        mixed = lax.dot_general(exc, cond_ref[...], NT, preferred_element_type=jnp.float32)
+        mixed = mixed.reshape(part, valence, -1) * val[None]
+        sums.append(jnp.sum(mixed, axis=1))
+    out_ref[...] = jnp.concatenate(sums, axis=0).astype(out_ref.dtype)
+
+
+def density_part(exc_t, sources, blocks, val_at, step):
+    batch, valence, width = exc_t.shape
+    points = blocks * sources[0].shape[0]
+    whole = pl.BlockSpec(memory_space=VMEM)
+    shapes = [(batch, points), (points, width), (valence, points)]
+    return pl.pallas_call(
+        functools.partial(density_part_kernel, blocks=blocks, val_at=val_at, step=step),
+        in_specs=[whole] * (1 + len(sources)),
+        out_specs=[whole] * len(shapes),
+        out_shape=[jax.ShapeDtypeStruct(shape, jnp.bfloat16) for shape in shapes],
+        compiler_params=pltpu.CompilerParams(vmem_limit_bytes=16 << 20),
+        cost_estimate=pl.CostEstimate(
+            flops=2 * exc_t.size * points, bytes_accessed=2 * exc_t.size, transcendentals=0
+        ),
+    )(exc_t, *sources)
+
+
+def turned(x, flag):
+    return jnp.where(flag, jnp.concatenate([x[:, x.shape[1] // 2 :], x[:, : x.shape[1] // 2]], axis=1), x)
+
+
+def field_kernel(index_ref, *refs, z_size, near, start, rows):
+    densities, screened, (forwarded, out_ref, held_ref) = refs[:z_size], refs[z_size:-3], refs[-3:]
+    points = held_ref.shape[1]
+    pair, chips = 2 * rows, points // (2 * rows)
+    chip, core = index_ref[0] // 2, index_ref[0] % 2
+    for k in range(chips):
+        total = None
+        for layer in range(z_size):
+            at = (k ^ (layer * near)) * rows
+            ref = densities[layer]
+            halves = [ref[:, at + c * points // 2 : at + c * points // 2 + rows] for c in range(2)]
+            term = jnp.concatenate(halves, axis=1).astype(jnp.float32)
+            total = term if total is None else total + term
+        place = pl.ds(pl.multiple_of((chip ^ k) * pair, pair), pair)
+        held_ref[:, place] = turned(total, core == 1)
+    density = held_ref[...].astype(jnp.bfloat16)
+    for k in range(near):
+        slab = screened[k]
+        at = start + k * points
+        both = [slab[:, slab.shape[1] - points :], forwarded[:, at : at + points]]
+        both = jnp.concatenate(both, axis=0)
+        partial = lax.dot_general(density, both, NT, preferred_element_type=jnp.float32)
+        place = pl.ds(pl.multiple_of(((chip % near) ^ k) * pair, pair), pair)
+        partial = turned(partial, core == 1).astype(out_ref.dtype)
+        for target in range(out_ref.shape[0]):
+            out_ref[target, :, place] = partial
+
+
+def field_of(index, densities, screened, forwarded, copies, start):
+    batch, points = densities[0].shape
+    near, rows = len(screened), screened[0].shape[0]
+    whole = pl.BlockSpec(memory_space=VMEM)
+    columns = 2 * near * rows
+    return pl.pallas_call(
+        functools.partial(field_kernel, z_size=len(densities), near=near, start=start, rows=rows),
+        in_specs=[pl.BlockSpec(memory_space=pltpu.SMEM)] + [whole] * (len(densities) + near + 1),
+        out_specs=whole,
+        out_shape=jax.ShapeDtypeStruct((copies, batch, columns), jnp.bfloat16),
+        scratch_shapes=[pltpu.VMEM((batch, points), jnp.float32)],
+        compiler_params=pltpu.CompilerParams(vmem_limit_bytes=16 << 20),
+        cost_estimate=pl.CostEstimate(
+            flops=2 * batch * points * columns, bytes_accessed=2 * points * columns, transcendentals=0
+        ),
+    )(index, *densities, *screened, forwarded)
+
+
+def project_kernel(index_ref, field_ref, *refs, parts, span):
+    conds, vals = refs[:parts], refs[parts : 2 * parts]
+    out_ref, pairs_ref, total_ref, sems = refs[2 * parts :]
+    size, batch, chunk = field_ref.shape
+    chips, _, pair = pairs_ref.shape
+    near = chunk // pair
+    q_size = 2 * near
+    valence = vals[0].shape[0]
+    chip, core = index_ref[0] // 2, index_ref[0] % 2
+    for layer in range(size // q_size):
+        field = sum(field_ref[layer * q_size + k].astype(jnp.float32) for k in range(q_size))
+        for k in range(near):
+            pairs_ref[layer * near + k] = field[:, k * pair : (k + 1) * pair]
+    both = [turned(pairs_ref[chip ^ k], core == 1) for k in range(chips)]
+    halves = [x[:, : pair // 2] for x in both] + [x[:, pair // 2 :] for x in both]
+    field = jnp.concatenate(halves, axis=1)
+    field = field.astype(jnp.bfloat16).astype(jnp.float32)
+    copies = []
+    for first in range(0, batch, span):
+        total, at = None, 0
+        for cond, val in zip(conds, vals):
+            stop = at + val.shape[1]
+            sides = [
+                (val[...].astype(jnp.float32) * field[b : b + 1, at:stop]).astype(jnp.bfloat16)
+                for b in range(first, first + span)
+            ]
+            weights = jnp.concatenate(sides, axis=0)
+            term = jnp.dot(weights, cond[...], preferred_element_type=jnp.float32)
+            total, at = term if total is None else total + term, stop
+        total = total.astype(total_ref.dtype)
+        for part in range(span):
+            total_ref[first + part] = total[part * valence : (part + 1) * valence].T
+        piece = pl.ds(first, span)
+        copies.append(pltpu.make_async_copy(total_ref.at[piece], out_ref.at[piece], sems.at[first // span]))
+        copies[-1].start()
+    for copy in copies:
+        copy.wait()
+
+
+def project(index, field, conds, vals):
+    size, batch, _ = field.shape
+    points, width = sum(cond.shape[0] for cond in conds), conds[0].shape[1]
+    valence, span = vals[0].shape[0], math.gcd(batch, 4)
+    whole = pl.BlockSpec(memory_space=VMEM)
+    shape = (batch, width, valence)
+    return pl.pallas_call(
+        functools.partial(project_kernel, parts=len(conds), span=span),
+        in_specs=[pl.BlockSpec(memory_space=pltpu.SMEM)] + [whole] * (1 + 2 * len(conds)),
+        out_specs=pl.BlockSpec(memory_space=pl.ANY),
+        out_shape=jax.ShapeDtypeStruct(shape, jnp.bfloat16),
+        scratch_shapes=[
+            pltpu.VMEM((size // 2, batch, 2 * points // size), jnp.float32),
+            pltpu.VMEM(shape, jnp.bfloat16),
+            pltpu.SemaphoreType.DMA((batch // span,)),
+        ],
+        compiler_params=pltpu.CompilerParams(vmem_limit_bytes=16 << 20),
+        cost_estimate=pl.CostEstimate(
+            flops=2 * batch * valence * width * points,
+            bytes_accessed=2 * batch * width * valence,
+            transcendentals=0,
+        ),
+    )(index, field, *conds, *vals)
+
+
+def body_slabs(size, excitations, valence_orb, conduction_orb, screened):
+    batch, width, valence = excitations.shape
+    q_size = 1 << ((size.bit_length() - 1) // 2)
+    z_size = size // q_size
+    chips = size // 2
+    index = lax.axis_index(AXIS)
+    place = index.reshape(1)
+
+    half, near = chips // 2, q_size // 2
+    slabs = slabs_of(index, conduction_orb, valence_orb, screened, chips, near)
+    slabs = [slabs[0]] + [swap(slabs[k], 2 * k, size) for k in range(1, chips)]
+    exc_t = excitations.transpose(0, 2, 1)
+
+    exc_t, *slabs = lax.optimization_barrier((exc_t, *slabs))
+    lead = width + valence
+    other = swap(pack(slabs, width, 2 * width + valence), 1, size)
+    straight, cond, val = density_part(exc_t, slabs, chips, 2 * width, 0)
+    turned_in, cond_other, val_other = density_part(exc_t, [other], chips, width, lead)
+    density = jnp.concatenate([straight, turned_in], axis=1)
+
+    densities = exchange(density, q_size, z_size, size)
+    field = field_of(place, densities, slabs[:near], other, size, chips * lead)
+    field = lax.all_to_all(field, AXIS, split_axis=0, concat_axis=0, tiled=True)
+    return project(place, field, [cond, cond_other], [val, val_other])
+
+
+def body(size, excitations, valence_orb, conduction_orb, screened):
+    powers = size >= 8 and size & (size - 1) == 0
+    aligned = excitations.shape[1] % 128 == 0 and (2 * valence_orb.shape[0]) % 128 == 0
+    run = body_slabs if powers and aligned else body_whole
+    return run(size, excitations, valence_orb, conduction_orb, screened)
 
 
 def solution(mesh):

time: 84.7 us -> 59.3 us (0.70)
  waiting for transfers between devices: 32.8 us -> 14.7 us
  local copies, waits for them, and re-layouts: 16.9 us -> 4.24 us
  blocking collectives: 0 us -> 11.7 us
  starting transfers between devices: 26.4 us -> 20.1 us
  Pallas kernels: 5.6 us -> 6.65 us
    ppermute x18 -> x11, waiting for transfers between devices: 32.8 us -> 14.7 us  [swap(): return lax.ppermute(x, AXIS, [(i, i ^ bits) for i in range(size)])]
    all_to_all x0 -> x1, blocking collectives: none -> 11.7 us  [body_slabs(): field = lax.all_to_all(field, AXIS, split_axis=0, concat_axis=0, tiled=True)]
    unnamed x25 -> x6, local copies, waits for them, and re-layouts: 13.6 us -> 2.86 us
    all_to_all x1 -> x0, starting transfers between devices: 7.39 us -> none  [body(): lax.all_to_all(blocks, AXIS, split_axis=0, concat_axis=0, tiled=True)]
    another operation x2 -> x0, other arithmetic: 2.01 us -> none  [the longest x1 1.97 us: body(): scr = jnp.stack(exchange(screened, 1, q_size, size))]
    concatenate x0 -> x2, other arithmetic: none -> 1.62 us  [slabs_of(): jnp.concatenate(parts + [val] + [screened] * (k < near), axis=1)]
    optimization_barrier x1 -> x0, local copies, waits for them, and re-layouts: 1.55 us -> none  [body(): lax.optimization_barrier((blocks, valence_orb, screened))]
    dynamic_slice x1, local copies, waits for them, and re-layouts: 0.12 us -> 1.37 us  [slabs_of(): lax.dynamic_slice_in_dim(cond, (index ^ j) * width, width, 1)]
  transfers between devices with their start and end apart: 19 -> 11, of which waited for: 7 -> 6; matrix products, arithmetic and copies ran while one was open for 19% -> 6% of each run, Pallas kernels for 0% -> 2%
where the time goes in v2:
time: 59.3 us; the launch traced here: 59 us
  starting transfers between devices  20.1 us (34%)
  waiting for transfers between devices  14.7 us (25%)
  blocking collectives  11.7 us (20%)
  Pallas kernels  6.65 us (11%)
  local copies, waits for them, and re-layouts  4.24 us (7%)
  other arithmetic  1.62 us (3%)
    ppermute x11, starting transfers between devices, swap(): return lax.ppermute(x, AXIS, [(i, i ^ bits) for i in range(size)])  20.1 us
    ppermute x11, waiting for transfers between devices, swap(): return lax.ppermute(x, AXIS, [(i, i ^ bits) for i in range(size)])  14.7 us
    all_to_all x1, blocking collectives, body_slabs(): field = lax.all_to_all(field, AXIS, split_axis=0, concat_axis=0, tiled=True)  11.7 us
    pallas_call x1, Pallas kernels, project(): pl.pallas_call(functools.partial(project_kernel, parts=len(conds), span=s...  3.47 us
    unnamed x6, local copies, waits for them, and re-layouts  2.86 us
    pallas_call x2, Pallas kernels, density_part(): pl.pallas_call(functools.partial(density_part_kernel, blocks=blocks, val_...  2.63 us
    concatenate x2, other arithmetic, slabs_of(): jnp.concatenate(parts + [val] + [screened] * (k < near), axis=1)  1.62 us
    dynamic_slice x1, local copies, waits for them, and re-layouts, slabs_of(): lax.dynamic_slice_in_dim(cond, (index ^ j) * width, width, 1)  1.37 us
  transfers between devices with their start and end apart: 11, of which 6 were waited for; matrix products, arithmetic and copies ran while one was open for 6% of the time, Pallas kernels for 2%

profile of v2, /device:TPU:0, one launch (start us, length us, event | category | flops | bytes accessed | tf_op | source)
XLA Modules:
  0.0 59.0 jit_solution(12459564697026872867)
XLA Ops:
  0.0 1.4 %constant_dynamic-slice_fusion.1 = (bf16[64,512]{1,0:T(8,128)(2,1)S(1)}, bf16[64,512]{1,0:T(8,128)(2,1)S(1)}, bf16[64,512]{1,0:T(8,128)(2,1)S(1)}, bf16[64,512]{...) fusion(bf16[64,8192]{1,0:T(8,128)(2,1)} %param.6, ...), kind=kLoop, calls=%fused_computation.13 | loop fusion | bytes 2097216 | tf_op jit(solution)/shard_map/dynamic_slice | solution.py:151
  1.4 0.9 %pad_maximum_fusion = (bf16[64,1152]{1,0:T(8,128)(2,1)S(1)}, bf16[64,1152]{1,0:T(8,128)(2,1)S(1)}, bf16[64,1152]{1,0:T(8,128)(2,1)}, bf16[64,1152]{1,0:T(8,128)(...) fusion(bf16[64,128]{1,0:T(8,128)(2,1)S(1)} %copy-done.1, bf16[64,512]{1,0:T(8,128)(2,1)S(1)} %get-tuple-element.50, ...), kind=kLoop, calls=%fused_computation | loop fusion | flops 2285568 | bytes 1687552 | tf_op jit(solution)/shard_map/concatenate | solution.py:152
  2.3 6.0 %collective-permute-start.6 = (bf16[64,1152]{1,0:T(8,128)(2,1)S(1)}, bf16[64,1152]{1,0:T(8,128)(2,1)S(1)}, u32[]{:S(2)}, u32[]{:S(2)}) collective-permute-start(bf16[64,1152]{1,0:T(8,128)(2,1)S(1)} %get-tuple-element.53), channel_id=1, source_target_pairs={{0,14},{1,15},{2,12},{3,13},{4,10},{5,11},{6,8},{7,9},{8,6},{9,7},... | collective-permute-start | bytes 442376 | tf_op jit(solution)/shard_map/ppermute | solution.py:17
  8.3 0.0 collective-permute-start.2
  8.3 0.8 %pad_maximum_fusion.8 = (bf16[64,2176]{1,0:T(8,128)(2,1)}, bf16[64,2176]{1,0:T(8,128)(2,1)S(1)}) fusion(bf16[64,1024]{1,0:T(8,128)(2,1)S(1)} %copy-done, bf16[64,128]{1,0:T(8,128)(2,1)S(1)} %copy-done.1, bf16[64,512]{1,0:T(8,128)(2,1)S(1)} %get-tuple-element.46, bf16[64,512]{1,0:T(8,128)(2,1)S(1)} %get-tuple-element.47, ...), kind=kLoop, calls=%fused_computation.8 | loop fusion | flops 1949696 | bytes 966656 | tf_op jit(solution)/shard_map/concatenate | solution.py:152
  9.0 1.0 %collective-permute-start = (bf16[64,2176]{1,0:T(8,128)(2,1)}, bf16[64,2176]{1,0:T(8,128)(2,1)S(1)}, u32[]{:S(2)}, u32[]{:S(2)}) collective-permute-start(bf16[64,2176]{1,0:T(8,128)(2,1)} %get-tuple-element.51), channel_id=1, source_target_pairs={{0,2},{1,3},{2,0},{3,1},{4,6},{5,7},{6,4},{7,5},{8,10},{9,11},{10,... | collective-permute-start | bytes 835592 | tf_op jit(solution)/shard_map/ppermute | solution.py:17
  10.0 1.2 %collective-permute-start.3 = (bf16[64,1152]{1,0:T(8,128)(2,1)}, bf16[64,1152]{1,0:T(8,128)(2,1)S(1)}, u32[]{:S(2)}, u32[]{:S(2)}) collective-permute-start(bf16[64,1152]{1,0:T(8,128)(2,1)} %get-tuple-element.55), channel_id=1, source_target_pairs={{0,8},{1,9},{2,10},{3,11},{4,12},{5,13},{6,14},{7,15},{8,0},{9,1},... | collective-permute-start | bytes 442376 | tf_op jit(solution)/shard_map/ppermute | solution.py:17
  11.3 2.1 %collective-permute-start.4 = (bf16[64,1152]{1,0:T(8,128)(2,1)}, bf16[64,1152]{1,0:T(8,128)(2,1)S(1)}, u32[]{:S(2)}, u32[]{:S(2)}) collective-permute-start(bf16[64,1152]{1,0:T(8,128)(2,1)} %get-tuple-element.56), channel_id=1, source_target_pairs={{0,10},{1,11},{2,8},{3,9},{4,14},{5,15},{6,12},{7,13},{8,2},{9,3},... | collective-permute-start | bytes 442376 | tf_op jit(solution)/shard_map/ppermute | solution.py:17
  13.4 0.0 collective-permute-done.6.refs_8_.refs_7_
  13.4 3.3 %collective-permute-start.5 = (bf16[64,1152]{1,0:T(8,128)(2,1)}, bf16[64,1152]{1,0:T(8,128)(2,1)S(1)}, u32[]{:S(2)}, u32[]{:S(2)}) collective-permute-start(bf16[64,1152]{1,0:T(8,128)(2,1)} %get-tuple-element.57), channel_id=1, source_target_pairs={{0,12},{1,13},{2,14},{3,15},{4,8},{5,9},{6,10},{7,11},{8,4},{9,5},... | collective-permute-start | bytes 442376 | tf_op jit(solution)/shard_map/ppermute | solution.py:17
  16.7 0.0 collective-permute-done.2.refs_4_.refs_3_
  16.7 1.7 %collective-permute-start.1 = (bf16[64,1152]{1,0:T(8,128)(2,1)}, bf16[64,1152]{1,0:T(8,128)(2,1)S(1)}, u32[]{:S(2)}, u32[]{:S(2)}) collective-permute-start(bf16[64,1152]{1,0:T(8,128)(2,1)} %get-tuple-element.58), channel_id=1, source_target_pairs={{0,4},{1,5},{2,6},{3,7},{4,0},{5,1},{6,2},{7,3},{8,12},{9,13},{10,... | collective-permute-start | bytes 442376 | tf_op jit(solution)/shard_map/ppermute | solution.py:17
  18.4 2.9 %copy.5 = bf16[16,512,128]{1,2,0:T(8,128)(2,1)S(1)} copy(bf16[16,512,128]{2,1,0:T(8,128)(2,1)} %param.4) | data formatting | bytes 4194304 | tf_op args[0]
  21.3 6.8 %collective-permute-done.3.refs_5_.refs_4_ = bf16[64,1152]{1,0:T(8,128)(2,1)S(1)} collective-permute-done((bf16[64,1152]{1,0:T(8,128)(2,1)}, bf16[64,1152]{1,0:T(8,128)(2,1)S(1)}, u32[]{:S(2)}, u32[]{:S(2)}) %collective-permute-start.3) | collective-permute-done | bytes 147488 | tf_op jit(solution)/shard_map/ppermute | solution.py:17
  28.1 3.0 %collective-permute-done.4.refs_6_.refs_5_ = bf16[64,1152]{1,0:T(8,128)(2,1)S(1)} collective-permute-done((bf16[64,1152]{1,0:T(8,128)(2,1)}, bf16[64,1152]{1,0:T(8,128)(2,1)S(1)}, u32[]{:S(2)}, u32[]{:S(2)}) %collective-permute-start.4) | collective-permute-done | bytes 147488 | tf_op jit(solution)/shard_map/ppermute | solution.py:17
  31.0 0.0 collective-permute-done.5.refs_7_.refs_6_
  31.0 0.0 collective-permute-done.1.refs_3_.refs_2_
  31.1 0.0 collective-permute-done.refs_2_.refs_1_.refs_5_
  31.1 0.1 shard_map.47
  31.1 0.1 collective-permute-start.7
  31.2 1.3 %shard_map.46 = (bf16[16,512]{1,0:T(8,128)(2,1)S(1)}, bf16[512,512]{1,0:T(8,128)(2,1)S(1)}, bf16[128,512]{1,0:T(8,128)(2,1)S(1)}) custom-call(bf16[16,128,512]{2,1,0:T(8,128)(2,1)S(1)} %bitcast.2, bf16[64,2176]{1,0:T(8,128)(2,1)S(1)} %get-tuple-element.21.refs_1_.refs_0_.refs_4_, bf16[64,2176]{1,0:T(8,128)(2,1)S(1)} %collective-permute-done.refs_2_.refs_1_.refs_5_, ...), custom_call_target="tpu_custom_call" | custom-call | flops 1073741824 | bytes 2097152 | tf_op jit(solution)/shard_map/pallas_call | solution.py:207
  32.5 1.1 %collective-permute-done.7.refs_1_.refs_6_ = bf16[64,7168]{1,0:T(8,128)(2,1)S(1)} collective-permute-done((bf16[64,7168]{1,0:T(8,128)(2,1)S(1)}, bf16[64,7168]{1,0:T(8,128)(2,1)S(1)}, u32[]{:S(2)}, u32[]{:S(2)}) %collective-permute-start.7) | collective-permute-done | bytes 917536 | tf_op jit(solution)/shard_map/ppermute | solution.py:17
  33.7 1.3 %shard_map.48 = (bf16[16,512]{1,0:T(8,128)(2,1)S(1)}, bf16[512,512]{1,0:T(8,128)(2,1)S(1)}, bf16[128,512]{1,0:T(8,128)(2,1)S(1)}) custom-call(bf16[16,128,512]{2,1,0:T(8,128)(2,1)S(1)} %bitcast.3, bf16[64,7168]{1,0:T(8,128)(2,1)S(1)} %collective-permute-done.7.refs_1_.refs_6_), custom_call_target="tpu_custom_call" | custom-call | flops 1073741824 | bytes 2097152 | tf_op jit(solution)/shard_map/pallas_call | solution.py:207
  35.0 2.6 %collective-permute-start.10 = (bf16[16,1024]{1,0:T(8,128)(2,1)S(1)}, bf16[16,1024]{1,0:T(8,128)(2,1)S(1)}, u32[]{:S(2)}, u32[]{:S(2)}) collective-permute-start(bf16[16,1024]{1,0:T(8,128)(2,1)S(1)} %constant_dynamic-update-slice_fusion.refs_0_), channel_id=1, source_target_pairs={{0,12},{1,13},{2,14},{3,15},{4,8},{5,9},{6,10},{7,11},{8,4},{9,5},... | collective-permute-start | bytes 98312 | tf_op jit(solution)/shard_map/ppermute | solution.py:17
  37.6 1.8 %collective-permute-start.9 = (bf16[16,1024]{1,0:T(8,128)(2,1)S(1)}, bf16[16,1024]{1,0:T(8,128)(2,1)S(1)}, u32[]{:S(2)}, u32[]{:S(2)}) collective-permute-start(bf16[16,1024]{1,0:T(8,128)(2,1)S(1)} %constant_dynamic-update-slice_fusion.refs_0_), channel_id=1, source_target_pairs={{0,8},{1,9},{2,10},{3,11},{4,12},{5,13},{6,14},{7,15},{8,0},{9,1},... | collective-permute-start | bytes 98312 | tf_op jit(solution)/shard_map/ppermute | solution.py:17
  39.5 0.1 collective-permute-start.8
  39.6 1.3 %collective-permute-done.10.refs_3_ = bf16[16,1024]{1,0:T(8,128)(2,1)S(1)} collective-permute-done((bf16[16,1024]{1,0:T(8,128)(2,1)S(1)}, bf16[16,1024]{1,0:T(8,128)(2,1)S(1)}, u32[]{:S(2)}, u32[]{:S(2)}) %collective-permute-start.10) | collective-permute-done | bytes 32800 | tf_op jit(solution)/shard_map/ppermute | solution.py:17
  40.9 1.6 %collective-permute-done.9.refs_2_ = bf16[16,1024]{1,0:T(8,128)(2,1)S(1)} collective-permute-done((bf16[16,1024]{1,0:T(8,128)(2,1)S(1)}, bf16[16,1024]{1,0:T(8,128)(2,1)S(1)}, u32[]{:S(2)}, u32[]{:S(2)}) %collective-permute-start.9) | collective-permute-done | bytes 32800 | tf_op jit(solution)/shard_map/ppermute | solution.py:17
  42.5 0.9 %collective-permute-done.8.refs_1_ = bf16[16,1024]{1,0:T(8,128)(2,1)S(1)} collective-permute-done((bf16[16,1024]{1,0:T(8,128)(2,1)S(1)}, bf16[16,1024]{1,0:T(8,128)(2,1)S(1)}, u32[]{:S(2)}, u32[]{:S(2)}) %collective-permute-start.8) | collective-permute-done | bytes 32800 | tf_op jit(solution)/shard_map/ppermute | solution.py:17
  43.4 0.5 shard_map.49
  43.9 11.7 %all_to_all.5.field_ref = bf16[16,16,256]{2,1,0:T(8,128)(2,1)S(1)} all-to-all(bf16[16,16,256]{2,1,0:T(8,128)(2,1)S(1)} %shard_map.49), channel_id=1, replica_groups=mesh['grp'=2,'row'=16] {'row'}, dimensions={0} | all-to-all | bytes 262144 | tf_op jit(solution)/shard_map/all_to_all | solution.py:355
  55.6 3.5 %shard_map.50 = bf16[16,512,128]{2,1,0:T(8,128)(2,1)} custom-call(s32[1]{0:T(128)} %bitcast.index_ref, bf16[16,16,256]{2,1,0:T(8,128)(2,1)S(1)} %all_to_all.5.field_ref, bf16[512,512]{1,0:T(8,128)(2,1)S(1)} %get-tuple-element.31.refs_0_, bf16[512,512]{1,0:T(8,128)(2,1)S(1)} %get-tuple-element.32.refs_1_, bf16[128,512]{1,0:T(8,128)(2,1)S(1)} %get-tuple-element.33.refs_2_, ...), custom_call_target="tpu_custom_call" | custom-call | flops 2147483648 | bytes 2097152 | tf_op jit(solution)/shard_map/pallas_call | solution.py:314
  (6 shorter events, 0.0 us)
Async XLA Ops:
  0.0 1.4 %copy-start.1 = (bf16[64,128]{1,0:T(8,128)(2,1)S(1)}, bf16[64,128]{1,0:T(8,128)(2,1)}, u32[]{:S(2)}) copy-start(bf16[64,128]{1,0:T(8,128)(2,1)} %param.5) | copy-start | bytes 49156
  0.0 8.3 %copy-start = (bf16[64,1024]{1,0:T(8,128)(2,1)S(1)}, bf16[64,1024]{1,0:T(8,128)(2,1)}, u32[]{:S(2)}) copy-start(bf16[64,1024]{1,0:T(8,128)(2,1)} %param.7) | copy-start | bytes 393220
  2.3 11.2 %collective-permute-start.6 = (bf16[64,1152]{1,0:T(8,128)(2,1)S(1)}, bf16[64,1152]{1,0:T(8,128)(2,1)S(1)}, u32[]{:S(2)}, u32[]{:S(2)}) collective-permute-start(bf16[64,1152]{1,0:T(8,128)(2,1)S(1)} %get-tuple-element.53), channel_id=1, source_target_pairs={{0,14},{1,15},{2,12},{3,13},{4,10},{5,11},{6,8},{7,9},{8,6},{9,7},... | collective-permute-start | bytes 442376 | tf_op jit(solution)/shard_map/ppermute | solution.py:17
  8.3 8.5 %collective-permute-start.2 = (bf16[64,1152]{1,0:T(8,128)(2,1)S(1)}, bf16[64,1152]{1,0:T(8,128)(2,1)S(1)}, u32[]{:S(2)}, u32[]{:S(2)}) collective-permute-start(bf16[64,1152]{1,0:T(8,128)(2,1)S(1)} %get-tuple-element.54), channel_id=1, source_target_pairs={{0,6},{1,7},{2,4},{3,5},{4,2},{5,3},{6,0},{7,1},{8,14},{9,15},{10,... | collective-permute-start | bytes 442376 | tf_op jit(solution)/shard_map/ppermute | solution.py:17
  9.0 22.0 %collective-permute-start = (bf16[64,2176]{1,0:T(8,128)(2,1)}, bf16[64,2176]{1,0:T(8,128)(2,1)S(1)}, u32[]{:S(2)}, u32[]{:S(2)}) collective-permute-start(bf16[64,2176]{1,0:T(8,128)(2,1)} %get-tuple-element.51), channel_id=1, source_target_pairs={{0,2},{1,3},{2,0},{3,1},{4,6},{5,7},{6,4},{7,5},{8,10},{9,11},{10,... | collective-permute-start | bytes 835592 | tf_op jit(solution)/shard_map/ppermute | solution.py:17
  10.0 18.0 %collective-permute-start.3 = (bf16[64,1152]{1,0:T(8,128)(2,1)}, bf16[64,1152]{1,0:T(8,128)(2,1)S(1)}, u32[]{:S(2)}, u32[]{:S(2)}) collective-permute-start(bf16[64,1152]{1,0:T(8,128)(2,1)} %get-tuple-element.55), channel_id=1, source_target_pairs={{0,8},{1,9},{2,10},{3,11},{4,12},{5,13},{6,14},{7,15},{8,0},{9,1},... | collective-permute-start | bytes 442376 | tf_op jit(solution)/shard_map/ppermute | solution.py:17
  11.3 19.8 %collective-permute-start.4 = (bf16[64,1152]{1,0:T(8,128)(2,1)}, bf16[64,1152]{1,0:T(8,128)(2,1)S(1)}, u32[]{:S(2)}, u32[]{:S(2)}) collective-permute-start(bf16[64,1152]{1,0:T(8,128)(2,1)} %get-tuple-element.56), channel_id=1, source_target_pairs={{0,10},{1,11},{2,8},{3,9},{4,14},{5,15},{6,12},{7,13},{8,2},{9,3},... | collective-permute-start | bytes 442376 | tf_op jit(solution)/shard_map/ppermute | solution.py:17
  13.4 17.6 %collective-permute-start.5 = (bf16[64,1152]{1,0:T(8,128)(2,1)}, bf16[64,1152]{1,0:T(8,128)(2,1)S(1)}, u32[]{:S(2)}, u32[]{:S(2)}) collective-permute-start(bf16[64,1152]{1,0:T(8,128)(2,1)} %get-tuple-element.57), channel_id=1, source_target_pairs={{0,12},{1,13},{2,14},{3,15},{4,8},{5,9},{6,10},{7,11},{8,4},{9,5},... | collective-permute-start | bytes 442376 | tf_op jit(solution)/shard_map/ppermute | solution.py:17
  16.7 14.3 %collective-permute-start.1 = (bf16[64,1152]{1,0:T(8,128)(2,1)}, bf16[64,1152]{1,0:T(8,128)(2,1)S(1)}, u32[]{:S(2)}, u32[]{:S(2)}) collective-permute-start(bf16[64,1152]{1,0:T(8,128)(2,1)} %get-tuple-element.58), channel_id=1, source_target_pairs={{0,4},{1,5},{2,6},{3,7},{4,0},{5,1},{6,2},{7,3},{8,12},{9,13},{10,... | collective-permute-start | bytes 442376 | tf_op jit(solution)/shard_map/ppermute | solution.py:17
  31.1 2.5 %collective-permute-start.7 = (bf16[64,7168]{1,0:T(8,128)(2,1)S(1)}, bf16[64,7168]{1,0:T(8,128)(2,1)S(1)}, u32[]{:S(2)}, u32[]{:S(2)}) collective-permute-start(bf16[64,7168]{1,0:T(8,128)(2,1)S(1)} %shard_map.47), channel_id=1, source_target_pairs={{0,1},{1,0},{2,3},{3,2},{4,5},{5,4},{6,7},{7,6},{8,9},{9,8},{10,11... | collective-permute-start | bytes 2752520 | tf_op jit(solution)/shard_map/ppermute | solution.py:17
  35.0 5.9 %collective-permute-start.10 = (bf16[16,1024]{1,0:T(8,128)(2,1)S(1)}, bf16[16,1024]{1,0:T(8,128)(2,1)S(1)}, u32[]{:S(2)}, u32[]{:S(2)}) collective-permute-start(bf16[16,1024]{1,0:T(8,128)(2,1)S(1)} %constant_dynamic-update-slice_fusion.refs_0_), channel_id=1, source_target_pairs={{0,12},{1,13},{2,14},{3,15},{4,8},{5,9},{6,10},{7,11},{8,4},{9,5},... | collective-permute-start | bytes 98312 | tf_op jit(solution)/shard_map/ppermute | solution.py:17
  37.6 4.8 %collective-permute-start.9 = (bf16[16,1024]{1,0:T(8,128)(2,1)S(1)}, bf16[16,1024]{1,0:T(8,128)(2,1)S(1)}, u32[]{:S(2)}, u32[]{:S(2)}) collective-permute-start(bf16[16,1024]{1,0:T(8,128)(2,1)S(1)} %constant_dynamic-update-slice_fusion.refs_0_), channel_id=1, source_target_pairs={{0,8},{1,9},{2,10},{3,11},{4,12},{5,13},{6,14},{7,15},{8,0},{9,1},... | collective-permute-start | bytes 98312 | tf_op jit(solution)/shard_map/ppermute | solution.py:17
  39.5 3.9 %collective-permute-start.8 = (bf16[16,1024]{1,0:T(8,128)(2,1)S(1)}, bf16[16,1024]{1,0:T(8,128)(2,1)S(1)}, u32[]{:S(2)}, u32[]{:S(2)}) collective-permute-start(bf16[16,1024]{1,0:T(8,128)(2,1)S(1)} %constant_dynamic-update-slice_fusion.refs_0_), channel_id=1, source_target_pairs={{0,4},{1,5},{2,6},{3,7},{4,0},{5,1},{6,2},{7,3},{8,12},{9,13},{10,... | collective-permute-start | bytes 98312 | tf_op jit(solution)/shard_map/ppermute | solution.py:17

commit v3 on v2

--- a/solution.py
+++ b/solution.py
@@ -144,48 +144,52 @@
     return action_of(z.reshape(1), cond_all.T, val_t, fields)
 
 
-def slabs_of(index, cond, val, screened, chips, near):
-    width = cond.shape[1] // (2 * chips)
-    slabs = []
-    for k in range(chips):
-        parts = [lax.dynamic_slice_in_dim(cond, (index ^ j) * width, width, 1) for j in (2 * k, 2 * k + 1)]
-        slabs.append(jnp.concatenate(parts + [val] + [screened] * (k < near), axis=1))
-    return slabs
-
-
-def pack_kernel(*refs, first, middle):
+def pack_kernel(index_ref, *refs, width, half):
     *slabs, out_ref = refs
+    other = pl.ds(pl.multiple_of((1 - index_ref[0] % 2) * width, 128), width)
     at = 0
-    for start, stop in [(first, middle), (middle, None)]:
-        for slab in slabs:
-            columns = (stop or slab.shape[1]) - start
+    for slab in slabs:
+        out_ref[:, at : at + width] = slab[:, other]
+        at += width
+    valence = min(slab.shape[1] for slab in slabs[:half]) - 2 * width
+    for first, extra in ((2 * width, valence), (2 * width + valence, None)):
+        for slab in slabs[:half]:
+            columns = extra or slab.shape[1] - first
             if columns:
-                out_ref[:, at : at + columns] = slab[:, start : start + columns]
+                out_ref[:, at : at + columns] = slab[:, first : first + columns]
                 at += columns
 
 
-def pack(slabs, first, middle):
-    columns = sum(slab.shape[1] for slab in slabs) - first * len(slabs)
-    whole = pl.BlockSpec(memory_space=VMEM)
-    return pl.pallas_call(
-        functools.partial(pack_kernel, first=first, middle=middle),
-        in_specs=[whole] * len(slabs),
+def pack(index, slabs, width):
+    half = len(slabs) // 2
+    columns = sum(slab.shape[1] for slab in slabs) - width * len(slabs)
+    whole = pl.BlockSpec(memory_space=VMEM)
+    return pl.pallas_call(
+        functools.partial(pack_kernel, width=width, half=half),
+        in_specs=[pl.BlockSpec(memory_space=pltpu.SMEM)] + [whole] * len(slabs),
         out_specs=whole,
         out_shape=jax.ShapeDtypeStruct((slabs[0].shape[0], columns), slabs[0].dtype),
         compiler_params=pltpu.CompilerParams(vmem_limit_bytes=8 << 20),
         cost_estimate=pl.CostEstimate(flops=0, bytes_accessed=1 << 20, transcendentals=0),
-    )(*slabs)
-
-
-def density_part_kernel(*refs, blocks, val_at, step):
+    )(index, *slabs)
+
+
+def density_part_kernel(index_ref, *refs, blocks):
     exc_ref, sources, (out_ref, cond_ref, val_ref) = refs[0], refs[1:-3], refs[-3:]
     batch, valence, width = exc_ref.shape
     rows = sources[0].shape[0]
     val = []
+    mine = pl.ds(pl.multiple_of(index_ref[0] % 2 * width, 128), width)
+    half = blocks // 2
     for k in range(blocks):
-        source, start = (sources[k], 0) if len(sources) > 1 else (sources[0], k * step)
-        cond_ref[k * rows : (k + 1) * rows, :] = source[:, start : start + width]
-        val.append(source[:, start + val_at : start + val_at + valence])
+        far, near = k // half, k % half
+        if len(sources) > 1:
+            cond, val_source, start = sources[k][:, mine], sources[near], 2 * width + far * valence
+        else:
+            cond, val_source = sources[0][:, k * width : (k + 1) * width], sources[0]
+            start = blocks * width + (2 * near + far) * valence
+        cond_ref[k * rows : (k + 1) * rows, :] = cond
+        val.append(val_source[:, start : start + valence])
     val = jnp.concatenate(val, axis=0).T
     val_ref[...] = val
     val = val.astype(jnp.float32)
@@ -199,21 +203,21 @@
     out_ref[...] = jnp.concatenate(sums, axis=0).astype(out_ref.dtype)
 
 
-def density_part(exc_t, sources, blocks, val_at, step):
+def density_part(index, exc_t, sources, blocks):
     batch, valence, width = exc_t.shape
     points = blocks * sources[0].shape[0]
     whole = pl.BlockSpec(memory_space=VMEM)
     shapes = [(batch, points), (points, width), (valence, points)]
     return pl.pallas_call(
-        functools.partial(density_part_kernel, blocks=blocks, val_at=val_at, step=step),
-        in_specs=[whole] * (1 + len(sources)),
+        functools.partial(density_part_kernel, blocks=blocks),
+        in_specs=[pl.BlockSpec(memory_space=pltpu.SMEM)] + [whole] * (1 + len(sources)),
         out_specs=[whole] * len(shapes),
         out_shape=[jax.ShapeDtypeStruct(shape, jnp.bfloat16) for shape in shapes],
         compiler_params=pltpu.CompilerParams(vmem_limit_bytes=16 << 20),
         cost_estimate=pl.CostEstimate(
             flops=2 * exc_t.size * points, bytes_accessed=2 * exc_t.size, transcendentals=0
         ),
-    )(exc_t, *sources)
+    )(index, exc_t, *sources)
 
 
 def turned(x, flag):
@@ -339,19 +343,31 @@
     place = index.reshape(1)
 
     half, near = chips // 2, q_size // 2
-    slabs = slabs_of(index, conduction_orb, valence_orb, screened, chips, near)
-    slabs = [slabs[0]] + [swap(slabs[k], 2 * k, size) for k in range(1, chips)]
     exc_t = excitations.transpose(0, 2, 1)
 
+    def columns(x, k):
+        return lax.dynamic_slice_in_dim(x, (index // 2 ^ k) * 2 * width, 2 * width, 1)
+
+    lead = columns(conduction_orb, chips - 1)
+    lead, conduction_orb = lax.optimization_barrier((lead, conduction_orb))
+    far = [columns(conduction_orb, k) for k in range(half, chips - 1)] + [lead]
+    far = [swap(far[k - half], 2 * k, size) for k in range(half, chips)]
+    crossed = swap(valence_orb, 2 * half, size)
+    crossed, conduction_orb = lax.optimization_barrier((crossed, conduction_orb))
+    close = []
+    for k in range(half):
+        parts = [columns(conduction_orb, k), valence_orb, crossed] + [screened] * (k < near)
+        close.append(jnp.concatenate(parts, axis=1))
+    slabs = close[:1] + [swap(close[k], 2 * k, size) for k in range(1, half)] + far
+
     exc_t, *slabs = lax.optimization_barrier((exc_t, *slabs))
-    lead = width + valence
-    other = swap(pack(slabs, width, 2 * width + valence), 1, size)
-    straight, cond, val = density_part(exc_t, slabs, chips, 2 * width, 0)
-    turned_in, cond_other, val_other = density_part(exc_t, [other], chips, width, lead)
+    other = swap(pack(place, slabs, width), 1, size)
+    straight, cond, val = density_part(place, exc_t, slabs, chips)
+    turned_in, cond_other, val_other = density_part(place, exc_t, [other], chips)
     density = jnp.concatenate([straight, turned_in], axis=1)
 
     densities = exchange(density, q_size, z_size, size)
-    field = field_of(place, densities, slabs[:near], other, size, chips * lead)
+    field = field_of(place, densities, slabs[:near], other, size, chips * (width + valence))
     field = lax.all_to_all(field, AXIS, split_axis=0, concat_axis=0, tiled=True)
     return project(place, field, [cond, cond_other], [val, val_other])
 

time: 59.3 us -> 58 us (0.978)
  waiting for transfers between devices: 14.7 us -> 11.6 us
  local copies, waits for them, and re-layouts: 4.24 us -> 6.66 us
    ppermute x11 -> x12, waiting for transfers between devices: 14.7 us -> 11.6 us  [swap(): return lax.ppermute(x, AXIS, [(i, i ^ bits) for i in range(size)])]
    dynamic_slice x1 -> x3, local copies, waits for them, and re-layouts: 1.37 us -> 3.8 us  [columns(): lax.dynamic_slice_in_dim(x, (index // 2 ^ k) * 2 * width, 2 * width, 1)]
    ppermute x11 -> x12, starting transfers between devices: 20.1 us -> 19.9 us  [swap(): return lax.ppermute(x, AXIS, [(i, i ^ bits) for i in range(size)])]
  transfers between devices with their start and end apart: 11 -> 12, of which waited for: 6 -> 5; matrix products, arithmetic and copies ran while one was open for 6% -> 14% of each run, Pallas kernels for 2% -> 2%
where the time goes in v3:
time: 58 us; the launch traced here: 57.8 us
  starting transfers between devices  19.9 us (34%)
  waiting for transfers between devices  11.6 us (20%)
  blocking collectives  11.3 us (19%)
  local copies, waits for them, and re-layouts  6.66 us (11%)
  Pallas kernels  6.65 us (11%)
  other arithmetic  1.51 us (3%)
    ppermute x12, starting transfers between devices, swap(): return lax.ppermute(x, AXIS, [(i, i ^ bits) for i in range(size)])  19.9 us
    ppermute x12, waiting for transfers between devices, swap(): return lax.ppermute(x, AXIS, [(i, i ^ bits) for i in range(size)])  11.6 us
    all_to_all x1, blocking collectives, body_slabs(): field = lax.all_to_all(field, AXIS, split_axis=0, concat_axis=0, tiled=True)  11.3 us
    dynamic_slice x3, local copies, waits for them, and re-layouts, columns(): lax.dynamic_slice_in_dim(x, (index // 2 ^ k) * 2 * width, 2 * width, 1)  3.8 us
    pallas_call x1, Pallas kernels, project(): pl.pallas_call(functools.partial(project_kernel, parts=len(conds), span=s...  3.47 us
    unnamed x6, local copies, waits for them, and re-layouts  2.86 us
    pallas_call x2, Pallas kernels, density_part(): pl.pallas_call(functools.partial(density_part_kernel, blocks=blocks), in_...  2.64 us
    concatenate x2, other arithmetic, body_slabs(): close.append(jnp.concatenate(parts, axis=1))  1.51 us
  transfers between devices with their start and end apart: 12, of which 5 were waited for; matrix products, arithmetic and copies ran while one was open for 14% of the time, Pallas kernels for 2%

profile of v3, /device:TPU:0, one launch (start us, length us, event | category | flops | bytes accessed | tf_op | source)
XLA Modules:
  0.0 57.8 jit_solution(1418484480153381609)
XLA Ops:
  0.0 4.0 %collective-permute-start = (bf16[64,128]{1,0:T(8,128)(2,1)}, bf16[64,128]{1,0:T(8,128)(2,1)S(1)}, u32[]{:S(2)}, u32[]{:S(2)}) collective-permute-start(bf16[64,128]{1,0:T(8,128)(2,1)} %param.5), channel_id=1, source_target_pairs={{0,8},{1,9},{2,10},{3,11},{4,12},{5,13},{6,14},{7,15},{8,0},{9,1},... | collective-permute-start | bytes 49160 | tf_op jit(solution)/shard_map/ppermute | solution.py:17
  4.0 0.9 %constant_dynamic-slice_fusion.7 = bf16[64,1024]{1,0:T(8,128)(2,1)S(1)} fusion(bf16[64,8192]{1,0:T(8,128)(2,1)} %param.6, s32[]{:T(128)S(6)} %select_n.37), kind=kLoop, calls=%fused_computation.19 | loop fusion | bytes 262148 | tf_op jit(solution)/shard_map/dynamic_slice | solution.py:349
  5.0 2.4 %collective-permute-start.7 = (bf16[64,1024]{1,0:T(8,128)(2,1)S(1)}, bf16[64,1024]{1,0:T(8,128)(2,1)S(1)}, u32[]{:S(2)}, u32[]{:S(2)}) collective-permute-start(bf16[64,1024]{1,0:T(8,128)(2,1)S(1)} %constant_dynamic-slice_fusion.7), channel_id=1, source_target_pairs={{0,14},{1,15},{2,12},{3,13},{4,10},{5,11},{6,8},{7,9},{8,6},{9,7},... | collective-permute-start | bytes 393224 | tf_op jit(solution)/shard_map/ppermute | solution.py:17
  7.3 1.8 %constant_dynamic-slice_fusion = (bf16[64,1024]{1,0:T(8,128)(2,1)S(1)}, bf16[64,1024]{1,0:T(8,128)(2,1)}, bf16[64,1024]{1,0:T(8,128)(2,1)}) fusion(bf16[64,8192]{1,0:T(8,128)(2,1)} %param.6, s32[]{:T(128)S(6)} %select_n.44, s32[]{:T(128)S(6)} %select_n.43, s32[]{:T(128)S(6)} %select_n.42), kind=kLoop, calls=%fused_computation.12 | loop fusion | bytes 786444 | tf_op jit(solution)/shard_map/dynamic_slice | solution.py:349
  9.1 2.5 %collective-permute-start.6 = (bf16[64,1024]{1,0:T(8,128)(2,1)S(1)}, bf16[64,1024]{1,0:T(8,128)(2,1)S(1)}, u32[]{:S(2)}, u32[]{:S(2)}) collective-permute-start(bf16[64,1024]{1,0:T(8,128)(2,1)S(1)} %get-tuple-element.43), channel_id=1, source_target_pairs={{0,12},{1,13},{2,14},{3,15},{4,8},{5,9},{6,10},{7,11},{8,4},{9,5},... | collective-permute-start | bytes 393224 | tf_op jit(solution)/shard_map/ppermute | solution.py:17
  11.6 0.0 collective-permute-done
  11.6 1.1 %constant_dynamic-slice_fusion.3 = (bf16[64,1024]{1,0:T(8,128)(2,1)S(1)}, bf16[64,1024]{1,0:T(8,128)(2,1)S(1)}, bf16[64,1024]{1,0:T(8,128)(2,1)S(1)}, bf16[64,1024]{1,0:T(8,128)(2,1)S(1)}) fusion(bf16[64,8192]{1,0:T(8,128)(2,1)} %param.6, s32[]{:T(128)S(6)} %select_n.41, s32[]{:T(128)S(6)} %select_n.40, s32[]{:T(128)S(6)} %select_n.39, s32[]{:T(128)S(6)} %select_n.38), kind=kLoop, calls=%fused_computation.15 | loop fusion | bytes 1048592 | tf_op jit(solution)/shard_map/dynamic_slice | solution.py:349
  12.7 0.8 %pad_maximum_fusion.4 = (bf16[64,2304]{1,0:T(8,128)(2,1)}, bf16[64,2304]{1,0:T(8,128)(2,1)S(1)}) fusion(bf16[64,1024]{1,0:T(8,128)(2,1)S(1)} %copy-done, bf16[64,128]{1,0:T(8,128)(2,1)S(1)} %collective-permute-done, bf16[64,128]{1,0:T(8,128)(2,1)S(1)} %copy-done.1, bf16[64,1024]{1,0:T(8,128)(2,1)S(1)} %get-tuple-element.48, ...), kind=kLoop, calls=%fused_computation.4 | loop fusion | flops 1916928 | bytes 1015808 | tf_op jit(solution)/shard_map/concatenate | solution.py:360
  13.5 0.5 collective-permute-start.1
  14.0 0.8 %pad_maximum_fusion.6 = (bf16[64,1280]{1,0:T(8,128)(2,1)}, bf16[64,1280]{1,0:T(8,128)(2,1)}) fusion(bf16[64,128]{1,0:T(8,128)(2,1)S(1)} %collective-permute-done, bf16[64,128]{1,0:T(8,128)(2,1)S(1)} %copy-done.1, bf16[64,1024]{1,0:T(8,128)(2,1)S(1)} %get-tuple-element.46, bf16[64,1024]{1,0:T(8,128)(2,1)S(1)} %get-tuple-element.47), kind=kLoop, calls=%fused_computation.6 | loop fusion | flops 819200 | bytes 622592 | tf_op jit(solution)/shard_map/concatenate | solution.py:360
  14.7 0.7 %collective-permute-start.3 = (bf16[64,1280]{1,0:T(8,128)(2,1)}, bf16[64,1280]{1,0:T(8,128)(2,1)S(1)}, u32[]{:S(2)}, u32[]{:S(2)}) collective-permute-start(bf16[64,1280]{1,0:T(8,128)(2,1)} %get-tuple-element.52), channel_id=1, source_target_pairs={{0,6},{1,7},{2,4},{3,5},{4,2},{5,3},{6,0},{7,1},{8,14},{9,15},{10,... | collective-permute-start | bytes 491528 | tf_op jit(solution)/shard_map/ppermute | solution.py:17
  15.5 2.2 %collective-permute-start.2 = (bf16[64,1280]{1,0:T(8,128)(2,1)}, bf16[64,1280]{1,0:T(8,128)(2,1)S(1)}, u32[]{:S(2)}, u32[]{:S(2)}) collective-permute-start(bf16[64,1280]{1,0:T(8,128)(2,1)} %get-tuple-element.53), channel_id=1, source_target_pairs={{0,4},{1,5},{2,6},{3,7},{4,0},{5,1},{6,2},{7,3},{8,12},{9,13},{10,... | collective-permute-start | bytes 491528 | tf_op jit(solution)/shard_map/ppermute | solution.py:17
  17.7 0.0 collective-permute-done.7.refs_8_.refs_7_
  17.7 2.1 %collective-permute-start.5 = (bf16[64,1024]{1,0:T(8,128)(2,1)}, bf16[64,1024]{1,0:T(8,128)(2,1)S(1)}, u32[]{:S(2)}, u32[]{:S(2)}) collective-permute-start(bf16[64,1024]{1,0:T(8,128)(2,1)} %get-tuple-element.44), channel_id=1, source_target_pairs={{0,10},{1,11},{2,8},{3,9},{4,14},{5,15},{6,12},{7,13},{8,2},{9,3},... | collective-permute-start | bytes 393224 | tf_op jit(solution)/shard_map/ppermute | solution.py:17
  19.8 0.9 %collective-permute-start.4 = (bf16[64,1024]{1,0:T(8,128)(2,1)}, bf16[64,1024]{1,0:T(8,128)(2,1)S(1)}, u32[]{:S(2)}, u32[]{:S(2)}) collective-permute-start(bf16[64,1024]{1,0:T(8,128)(2,1)} %get-tuple-element.45), channel_id=1, source_target_pairs={{0,8},{1,9},{2,10},{3,11},{4,12},{5,13},{6,14},{7,15},{8,0},{9,1},... | collective-permute-start | bytes 393224 | tf_op jit(solution)/shard_map/ppermute | solution.py:17
  20.7 2.9 %copy.5 = bf16[16,512,128]{1,2,0:T(8,128)(2,1)S(1)} copy(bf16[16,512,128]{2,1,0:T(8,128)(2,1)} %param.4) | data formatting | bytes 4194304 | tf_op args[0]
  23.6 6.9 %collective-permute-done.5.refs_6_.refs_5_ = bf16[64,1024]{1,0:T(8,128)(2,1)S(1)} collective-permute-done((bf16[64,1024]{1,0:T(8,128)(2,1)}, bf16[64,1024]{1,0:T(8,128)(2,1)S(1)}, u32[]{:S(2)}, u32[]{:S(2)}) %collective-permute-start.5) | collective-permute-done | bytes 131104 | tf_op jit(solution)/shard_map/ppermute | solution.py:17
  30.5 1.1 %collective-permute-done.4.refs_5_.refs_4_ = bf16[64,1024]{1,0:T(8,128)(2,1)S(1)} collective-permute-done((bf16[64,1024]{1,0:T(8,128)(2,1)}, bf16[64,1024]{1,0:T(8,128)(2,1)S(1)}, u32[]{:S(2)}, u32[]{:S(2)}) %collective-permute-start.4) | collective-permute-done | bytes 131104 | tf_op jit(solution)/shard_map/ppermute | solution.py:17
  31.6 0.0 collective-permute-done.1.refs_2_.refs_1_.refs_5_
  31.6 0.1 shard_map.47
  31.7 0.1 collective-permute-start.8
  31.8 1.3 %shard_map.46 = (bf16[16,512]{1,0:T(8,128)(2,1)S(1)}, bf16[512,512]{1,0:T(8,128)(2,1)S(1)}, bf16[128,512]{1,0:T(8,128)(2,1)S(1)}) custom-call(s32[1]{0:T(128)} %bitcast.index_ref, bf16[16,128,512]{2,1,0:T(8,128)(2,1)S(1)} %bitcast.2, bf16[64,2304]{1,0:T(8,128)(2,1)S(1)} %get-tuple-element.29.refs_1_.refs_0_.refs_4_, ...), custom_call_target="tpu_custom_call" | custom-call | flops 1073741824 | bytes 2097152 | tf_op jit(solution)/shard_map/pallas_call | solution.py:211
  33.1 1.1 %collective-permute-done.8.refs_1_.refs_6_ = bf16[64,7168]{1,0:T(8,128)(2,1)S(1)} collective-permute-done((bf16[64,7168]{1,0:T(8,128)(2,1)S(1)}, bf16[64,7168]{1,0:T(8,128)(2,1)S(1)}, u32[]{:S(2)}, u32[]{:S(2)}) %collective-permute-start.8) | collective-permute-done | bytes 917536 | tf_op jit(solution)/shard_map/ppermute | solution.py:17
  34.2 1.3 %shard_map.48 = (bf16[16,512]{1,0:T(8,128)(2,1)S(1)}, bf16[512,512]{1,0:T(8,128)(2,1)S(1)}, bf16[128,512]{1,0:T(8,128)(2,1)S(1)}) custom-call(s32[1]{0:T(128)} %bitcast.index_ref, bf16[16,128,512]{2,1,0:T(8,128)(2,1)S(1)} %bitcast.3, bf16[64,7168]{1,0:T(8,128)(2,1)S(1)} %collective-permute-done.8.refs_1_.refs_6_), custom_call_target="tpu_custom_call" | custom-call | flops 1073741824 | bytes 2097152 | tf_op jit(solution)/shard_map/pallas_call | solution.py:211
  35.6 2.0 %collective-permute-start.11 = (bf16[16,1024]{1,0:T(8,128)(2,1)S(1)}, bf16[16,1024]{1,0:T(8,128)(2,1)S(1)}, u32[]{:S(2)}, u32[]{:S(2)}) collective-permute-start(bf16[16,1024]{1,0:T(8,128)(2,1)S(1)} %constant_dynamic-update-slice_fusion.refs_0_), channel_id=1, source_target_pairs={{0,12},{1,13},{2,14},{3,15},{4,8},{5,9},{6,10},{7,11},{8,4},{9,5},... | collective-permute-start | bytes 98312 | tf_op jit(solution)/shard_map/ppermute | solution.py:17
  37.6 2.4 %collective-permute-start.9 = (bf16[16,1024]{1,0:T(8,128)(2,1)S(1)}, bf16[16,1024]{1,0:T(8,128)(2,1)S(1)}, u32[]{:S(2)}, u32[]{:S(2)}) collective-permute-start(bf16[16,1024]{1,0:T(8,128)(2,1)S(1)} %constant_dynamic-update-slice_fusion.refs_0_), channel_id=1, source_target_pairs={{0,4},{1,5},{2,6},{3,7},{4,0},{5,1},{6,2},{7,3},{8,12},{9,13},{10,... | collective-permute-start | bytes 98312 | tf_op jit(solution)/shard_map/ppermute | solution.py:17
  40.0 1.4 %collective-permute-done.11.refs_3_ = bf16[16,1024]{1,0:T(8,128)(2,1)S(1)} collective-permute-done((bf16[16,1024]{1,0:T(8,128)(2,1)S(1)}, bf16[16,1024]{1,0:T(8,128)(2,1)S(1)}, u32[]{:S(2)}, u32[]{:S(2)}) %collective-permute-start.11) | collective-permute-done | bytes 32800 | tf_op jit(solution)/shard_map/ppermute | solution.py:17
  41.4 1.0 %collective-permute-done.10.refs_2_ = bf16[16,1024]{1,0:T(8,128)(2,1)S(1)} collective-permute-done((bf16[16,1024]{1,0:T(8,128)(2,1)S(1)}, bf16[16,1024]{1,0:T(8,128)(2,1)S(1)}, u32[]{:S(2)}, u32[]{:S(2)}) %collective-permute-start.10) | collective-permute-done | bytes 32800 | tf_op jit(solution)/shard_map/ppermute | solution.py:17
  42.4 0.0 collective-permute-done.9.refs_1_
  42.5 0.5 shard_map.49
  42.9 11.3 %all_to_all.5.field_ref = bf16[16,16,256]{2,1,0:T(8,128)(2,1)S(1)} all-to-all(bf16[16,16,256]{2,1,0:T(8,128)(2,1)S(1)} %shard_map.49), channel_id=1, replica_groups=mesh['grp'=2,'row'=16] {'row'}, dimensions={0} | all-to-all | bytes 262144 | tf_op jit(solution)/shard_map/all_to_all | solution.py:371
  54.3 3.5 %shard_map.50 = bf16[16,512,128]{2,1,0:T(8,128)(2,1)} custom-call(s32[1]{0:T(128)} %bitcast.index_ref, bf16[16,16,256]{2,1,0:T(8,128)(2,1)S(1)} %all_to_all.5.field_ref, bf16[512,512]{1,0:T(8,128)(2,1)S(1)} %get-tuple-element.39.refs_0_, bf16[512,512]{1,0:T(8,128)(2,1)S(1)} %get-tuple-element.40.refs_1_, bf16[128,512]{1,0:T(8,128)(2,1)S(1)} %get-tuple-element.41.refs_2_, ...), custom_call_target="tpu_custom_call" | custom-call | flops 2147483648 | bytes 2097152 | tf_op jit(solution)/shard_map/pallas_call | solution.py:318
  (10 shorter events, 0.0 us)
Async XLA Ops:
  0.0 12.7 %copy-start.1 = (bf16[64,128]{1,0:T(8,128)(2,1)S(1)}, bf16[64,128]{1,0:T(8,128)(2,1)}, u32[]{:S(2)}) copy-start(bf16[64,128]{1,0:T(8,128)(2,1)} %param.5) | copy-start | bytes 49156
  0.0 12.7 %copy-start = (bf16[64,1024]{1,0:T(8,128)(2,1)S(1)}, bf16[64,1024]{1,0:T(8,128)(2,1)}, u32[]{:S(2)}) copy-start(bf16[64,1024]{1,0:T(8,128)(2,1)} %param.7) | copy-start | bytes 393220
  0.0 11.6 %collective-permute-start = (bf16[64,128]{1,0:T(8,128)(2,1)}, bf16[64,128]{1,0:T(8,128)(2,1)S(1)}, u32[]{:S(2)}, u32[]{:S(2)}) collective-permute-start(bf16[64,128]{1,0:T(8,128)(2,1)} %param.5), channel_id=1, source_target_pairs={{0,8},{1,9},{2,10},{3,11},{4,12},{5,13},{6,14},{7,15},{8,0},{9,1},... | collective-permute-start | bytes 49160 | tf_op jit(solution)/shard_map/ppermute | solution.py:17
  5.0 12.8 %collective-permute-start.7 = (bf16[64,1024]{1,0:T(8,128)(2,1)S(1)}, bf16[64,1024]{1,0:T(8,128)(2,1)S(1)}, u32[]{:S(2)}, u32[]{:S(2)}) collective-permute-start(bf16[64,1024]{1,0:T(8,128)(2,1)S(1)} %constant_dynamic-slice_fusion.7), channel_id=1, source_target_pairs={{0,14},{1,15},{2,12},{3,13},{4,10},{5,11},{6,8},{7,9},{8,6},{9,7},... | collective-permute-start | bytes 393224 | tf_op jit(solution)/shard_map/ppermute | solution.py:17
  9.1 10.7 %collective-permute-start.6 = (bf16[64,1024]{1,0:T(8,128)(2,1)S(1)}, bf16[64,1024]{1,0:T(8,128)(2,1)S(1)}, u32[]{:S(2)}, u32[]{:S(2)}) collective-permute-start(bf16[64,1024]{1,0:T(8,128)(2,1)S(1)} %get-tuple-element.43), channel_id=1, source_target_pairs={{0,12},{1,13},{2,14},{3,15},{4,8},{5,9},{6,10},{7,11},{8,4},{9,5},... | collective-permute-start | bytes 393224 | tf_op jit(solution)/shard_map/ppermute | solution.py:17
  13.5 18.1 %collective-permute-start.1 = (bf16[64,2304]{1,0:T(8,128)(2,1)}, bf16[64,2304]{1,0:T(8,128)(2,1)S(1)}, u32[]{:S(2)}, u32[]{:S(2)}) collective-permute-start(bf16[64,2304]{1,0:T(8,128)(2,1)} %get-tuple-element.50), channel_id=1, source_target_pairs={{0,2},{1,3},{2,0},{3,1},{4,6},{5,7},{6,4},{7,5},{8,10},{9,11},{10,... | collective-permute-start | bytes 884744 | tf_op jit(solution)/shard_map/ppermute | solution.py:17
  14.7 16.9 %collective-permute-start.3 = (bf16[64,1280]{1,0:T(8,128)(2,1)}, bf16[64,1280]{1,0:T(8,128)(2,1)S(1)}, u32[]{:S(2)}, u32[]{:S(2)}) collective-permute-start(bf16[64,1280]{1,0:T(8,128)(2,1)} %get-tuple-element.52), channel_id=1, source_target_pairs={{0,6},{1,7},{2,4},{3,5},{4,2},{5,3},{6,0},{7,1},{8,14},{9,15},{10,... | collective-permute-start | bytes 491528 | tf_op jit(solution)/shard_map/ppermute | solution.py:17
  15.5 16.2 %collective-permute-start.2 = (bf16[64,1280]{1,0:T(8,128)(2,1)}, bf16[64,1280]{1,0:T(8,128)(2,1)S(1)}, u32[]{:S(2)}, u32[]{:S(2)}) collective-permute-start(bf16[64,1280]{1,0:T(8,128)(2,1)} %get-tuple-element.53), channel_id=1, source_target_pairs={{0,4},{1,5},{2,6},{3,7},{4,0},{5,1},{6,2},{7,3},{8,12},{9,13},{10,... | collective-permute-start | bytes 491528 | tf_op jit(solution)/shard_map/ppermute | solution.py:17
  17.7 12.8 %collective-permute-start.5 = (bf16[64,1024]{1,0:T(8,128)(2,1)}, bf16[64,1024]{1,0:T(8,128)(2,1)S(1)}, u32[]{:S(2)}, u32[]{:S(2)}) collective-permute-start(bf16[64,1024]{1,0:T(8,128)(2,1)} %get-tuple-element.44), channel_id=1, source_target_pairs={{0,10},{1,11},{2,8},{3,9},{4,14},{5,15},{6,12},{7,13},{8,2},{9,3},... | collective-permute-start | bytes 393224 | tf_op jit(solution)/shard_map/ppermute | solution.py:17
  19.8 11.8 %collective-permute-start.4 = (bf16[64,1024]{1,0:T(8,128)(2,1)}, bf16[64,1024]{1,0:T(8,128)(2,1)S(1)}, u32[]{:S(2)}, u32[]{:S(2)}) collective-permute-start(bf16[64,1024]{1,0:T(8,128)(2,1)} %get-tuple-element.45), channel_id=1, source_target_pairs={{0,8},{1,9},{2,10},{3,11},{4,12},{5,13},{6,14},{7,15},{8,0},{9,1},... | collective-permute-start | bytes 393224 | tf_op jit(solution)/shard_map/ppermute | solution.py:17
  31.7 2.5 %collective-permute-start.8 = (bf16[64,7168]{1,0:T(8,128)(2,1)S(1)}, bf16[64,7168]{1,0:T(8,128)(2,1)S(1)}, u32[]{:S(2)}, u32[]{:S(2)}) collective-permute-start(bf16[64,7168]{1,0:T(8,128)(2,1)S(1)} %shard_map.47), channel_id=1, source_target_pairs={{0,1},{1,0},{2,3},{3,2},{4,5},{5,4},{6,7},{7,6},{8,9},{9,8},{10,11... | collective-permute-start | bytes 2752520 | tf_op jit(solution)/shard_map/ppermute | solution.py:17
  35.6 5.9 %collective-permute-start.11 = (bf16[16,1024]{1,0:T(8,128)(2,1)S(1)}, bf16[16,1024]{1,0:T(8,128)(2,1)S(1)}, u32[]{:S(2)}, u32[]{:S(2)}) collective-permute-start(bf16[16,1024]{1,0:T(8,128)(2,1)S(1)} %constant_dynamic-update-slice_fusion.refs_0_), channel_id=1, source_target_pairs={{0,12},{1,13},{2,14},{3,15},{4,8},{5,9},{6,10},{7,11},{8,4},{9,5},... | collective-permute-start | bytes 98312 | tf_op jit(solution)/shard_map/ppermute | solution.py:17
  37.6 4.9 %collective-permute-start.10 = (bf16[16,1024]{1,0:T(8,128)(2,1)S(1)}, bf16[16,1024]{1,0:T(8,128)(2,1)S(1)}, u32[]{:S(2)}, u32[]{:S(2)}) collective-permute-start(bf16[16,1024]{1,0:T(8,128)(2,1)S(1)} %constant_dynamic-update-slice_fusion.refs_0_), channel_id=1, source_target_pairs={{0,8},{1,9},{2,10},{3,11},{4,12},{5,13},{6,14},{7,15},{8,0},{9,1},... | collective-permute-start | bytes 98312 | tf_op jit(solution)/shard_map/ppermute | solution.py:17
  37.6 4.9 %collective-permute-start.9 = (bf16[16,1024]{1,0:T(8,128)(2,1)S(1)}, bf16[16,1024]{1,0:T(8,128)(2,1)S(1)}, u32[]{:S(2)}, u32[]{:S(2)}) collective-permute-start(bf16[16,1024]{1,0:T(8,128)(2,1)S(1)} %constant_dynamic-update-slice_fusion.refs_0_), channel_id=1, source_target_pairs={{0,4},{1,5},{2,6},{3,7},{4,0},{5,1},{6,2},{7,3},{8,12},{9,13},{10,... | collective-permute-start | bytes 98312 | tf_op jit(solution)/shard_map/ppermute | solution.py:17

commit v4 on v3

--- a/solution.py
+++ b/solution.py
@@ -144,50 +144,54 @@
     return action_of(z.reshape(1), cond_all.T, val_t, fields)
 
 
-def pack_kernel(index_ref, *refs, width, half):
-    *slabs, out_ref = refs
+def pack_kernel(index_ref, *refs, width):
+    *slabs, near_ref, far_ref = refs
+    half = len(slabs) // 2
     other = pl.ds(pl.multiple_of((1 - index_ref[0] % 2) * width, 128), width)
-    at = 0
-    for slab in slabs:
-        out_ref[:, at : at + width] = slab[:, other]
-        at += width
-    valence = min(slab.shape[1] for slab in slabs[:half]) - 2 * width
-    for first, extra in ((2 * width, valence), (2 * width + valence, None)):
-        for slab in slabs[:half]:
-            columns = extra or slab.shape[1] - first
-            if columns:
-                out_ref[:, at : at + columns] = slab[:, first : first + columns]
-                at += columns
-
-
-def pack(index, slabs, width):
-    half = len(slabs) // 2
-    columns = sum(slab.shape[1] for slab in slabs) - width * len(slabs)
+    valence = near_ref.shape[1] // half - width
+    for k in range(half):
+        near_ref[:, k * width : (k + 1) * width] = slabs[k][:, other]
+        far_ref[:, k * width : (k + 1) * width] = slabs[half + k][:, other]
+        at = half * width + k * valence
+        near_ref[:, at : at + valence] = slabs[k][:, 2 * width : 2 * width + valence]
+    at = half * width
+    for slab in slabs[:half]:
+        columns = slab.shape[1] - 2 * width - valence
+        if columns:
+            far_ref[:, at : at + columns] = slab[:, 2 * width + valence :]
+            at += columns
+
+
+def pack(index, slabs, width, valence):
+    half, rows = len(slabs) // 2, slabs[0].shape[0]
     whole = pl.BlockSpec(memory_space=VMEM)
-    return pl.pallas_call(
-        functools.partial(pack_kernel, width=width, half=half),
+    extra = sum(slab.shape[1] - 2 * (width + valence) for slab in slabs[:half])
+    columns = (half * (width + 2 * valence), half * width + extra)
+    return pl.pallas_call(
+        functools.partial(pack_kernel, width=width),
         in_specs=[pl.BlockSpec(memory_space=pltpu.SMEM)] + [whole] * len(slabs),
-        out_specs=whole,
-        out_shape=jax.ShapeDtypeStruct((slabs[0].shape[0], columns), slabs[0].dtype),
+        out_specs=[whole] * 2,
+        out_shape=[jax.ShapeDtypeStruct((rows, n), slabs[0].dtype) for n in columns],
         compiler_params=pltpu.CompilerParams(vmem_limit_bytes=8 << 20),
         cost_estimate=pl.CostEstimate(flops=0, bytes_accessed=1 << 20, transcendentals=0),
     )(index, *slabs)
 
 
-def density_part_kernel(index_ref, *refs, blocks):
+def density_part_kernel(index_ref, *refs, straight):
     exc_ref, sources, (out_ref, cond_ref, val_ref) = refs[0], refs[1:-3], refs[-3:]
     batch, valence, width = exc_ref.shape
     rows = sources[0].shape[0]
+    blocks = cond_ref.shape[0] // rows
+    mine = pl.ds(pl.multiple_of(index_ref[0] % 2 * width, 128), width)
     val = []
-    mine = pl.ds(pl.multiple_of(index_ref[0] % 2 * width, 128), width)
-    half = blocks // 2
     for k in range(blocks):
-        far, near = k // half, k % half
-        if len(sources) > 1:
-            cond, val_source, start = sources[k][:, mine], sources[near], 2 * width + far * valence
+        if straight:
+            half = blocks // 2
+            cond = sources[k][:, mine]
+            val_source, start = sources[k % half], 2 * width + k // half * valence
         else:
-            cond, val_source = sources[0][:, k * width : (k + 1) * width], sources[0]
-            start = blocks * width + (2 * near + far) * valence
+            cond = sources[-1][:, k * width : (k + 1) * width]
+            val_source, start = sources[0], blocks * width + (2 * k + len(sources) - 1) * valence
         cond_ref[k * rows : (k + 1) * rows, :] = cond
         val.append(val_source[:, start : start + valence])
     val = jnp.concatenate(val, axis=0).T
@@ -203,13 +207,13 @@
     out_ref[...] = jnp.concatenate(sums, axis=0).astype(out_ref.dtype)
 
 
-def density_part(index, exc_t, sources, blocks):
+def density_part(index, exc_t, sources, blocks, straight):
     batch, valence, width = exc_t.shape
     points = blocks * sources[0].shape[0]
     whole = pl.BlockSpec(memory_space=VMEM)
     shapes = [(batch, points), (points, width), (valence, points)]
     return pl.pallas_call(
-        functools.partial(density_part_kernel, blocks=blocks),
+        functools.partial(density_part_kernel, straight=straight),
         in_specs=[pl.BlockSpec(memory_space=pltpu.SMEM)] + [whole] * (1 + len(sources)),
         out_specs=[whole] * len(shapes),
         out_shape=[jax.ShapeDtypeStruct(shape, jnp.bfloat16) for shape in shapes],
@@ -301,10 +305,10 @@
             total, at = term if total is None else total + term, stop
         total = total.astype(total_ref.dtype)
         for part in range(span):
-            total_ref[first + part] = total[part * valence : (part + 1) * valence].T
-        piece = pl.ds(first, span)
-        copies.append(pltpu.make_async_copy(total_ref.at[piece], out_ref.at[piece], sems.at[first // span]))
-        copies[-1].start()
+            b = first + part
+            total_ref[b] = total[part * valence : (part + 1) * valence].T
+            copies.append(pltpu.make_async_copy(total_ref.at[b], out_ref.at[b], sems.at[b]))
+            copies[-1].start()
     for copy in copies:
         copy.wait()
 
@@ -323,7 +327,7 @@
         scratch_shapes=[
             pltpu.VMEM((size // 2, batch, 2 * points // size), jnp.float32),
             pltpu.VMEM(shape, jnp.bfloat16),
-            pltpu.SemaphoreType.DMA((batch // span,)),
+            pltpu.SemaphoreType.DMA((batch,)),
         ],
         compiler_params=pltpu.CompilerParams(vmem_limit_bytes=16 << 20),
         cost_estimate=pl.CostEstimate(
@@ -361,15 +365,20 @@
     slabs = close[:1] + [swap(close[k], 2 * k, size) for k in range(1, half)] + far
 
     exc_t, *slabs = lax.optimization_barrier((exc_t, *slabs))
-    other = swap(pack(place, slabs, width), 1, size)
-    straight, cond, val = density_part(place, exc_t, slabs, chips)
-    turned_in, cond_other, val_other = density_part(place, exc_t, [other], chips)
-    density = jnp.concatenate([straight, turned_in], axis=1)
+    near_part, far_part = pack(place, slabs, width, valence)
+    near_part, far_part = swap(near_part, 1, size), swap(far_part, 1, size)
+    parts = [
+        density_part(place, exc_t, slabs, chips, True),
+        density_part(place, exc_t, [near_part], half, False),
+        density_part(place, exc_t, [near_part, far_part], half, False),
+    ]
+    density, conds, vals = [list(x) for x in zip(*parts)]
+    density = jnp.concatenate(density, axis=1)
 
     densities = exchange(density, q_size, z_size, size)
-    field = field_of(place, densities, slabs[:near], other, size, chips * (width + valence))
+    field = field_of(place, densities, slabs[:near], far_part, size, half * width)
     field = lax.all_to_all(field, AXIS, split_axis=0, concat_axis=0, tiled=True)
-    return project(place, field, [cond, cond_other], [val, val_other])
+    return project(place, field, conds, vals)
 
 
 def body(size, excitations, valence_orb, conduction_orb, screened):

time: 58 us -> 57.6 us (level)
  waiting for transfers between devices: 11.6 us -> 10.4 us
    ppermute x12 -> x13, waiting for transfers between devices: 11.6 us -> 10.4 us  [swap(): return lax.ppermute(x, AXIS, [(i, i ^ bits) for i in range(size)])]
    ppermute x12 -> x13, starting transfers between devices: 19.9 us -> 20.4 us  [swap(): return lax.ppermute(x, AXIS, [(i, i ^ bits) for i in range(size)])]
    pallas_call x3 -> x4, Pallas kernels: 2.7 us -> 2.89 us  [the longest x3 2.83 us: density_part(): pl.pallas_call(functools.partial(density_part_kernel, straight=straight),...]
    unnamed x6 -> x7, local copies, waits for them, and re-layouts: 2.86 us -> 2.87 us
  transfers between devices with their start and end apart: 12 -> 13, of which waited for: 5 -> 4; matrix products, arithmetic and copies ran while one was open for 14% -> 14% of each run, Pallas kernels for 2% -> 4%
where the time goes in v4:
time: 57.6 us; the launch traced here: 57.3 us
  starting transfers between devices  20.4 us (35%)
  blocking collectives  11.4 us (20%)
  waiting for transfers between devices  10.4 us (18%)
  Pallas kernels  6.79 us (12%)
  local copies, waits for them, and re-layouts  6.66 us (12%)
  other arithmetic  1.5 us (3%)
    ppermute x13, starting transfers between devices, swap(): return lax.ppermute(x, AXIS, [(i, i ^ bits) for i in range(size)])  20.4 us
    all_to_all x1, blocking collectives, body_slabs(): field = lax.all_to_all(field, AXIS, split_axis=0, concat_axis=0, tiled=True)  11.4 us
    ppermute x13, waiting for transfers between devices, swap(): return lax.ppermute(x, AXIS, [(i, i ^ bits) for i in range(size)])  10.4 us
    dynamic_slice x3, local copies, waits for them, and re-layouts, columns(): lax.dynamic_slice_in_dim(x, (index // 2 ^ k) * 2 * width, 2 * width, 1)  3.79 us
    pallas_call x1, Pallas kernels, project(): pl.pallas_call(functools.partial(project_kernel, parts=len(conds), span=s...  3.42 us
    unnamed x7, local copies, waits for them, and re-layouts  2.87 us
    pallas_call x3, Pallas kernels, density_part(): pl.pallas_call(functools.partial(density_part_kernel, straight=straight),...  2.83 us
    concatenate x2, other arithmetic, body_slabs(): close.append(jnp.concatenate(parts, axis=1))  1.5 us
  transfers between devices with their start and end apart: 13, of which 4 were waited for; matrix products, arithmetic and copies ran while one was open for 14% of the time, Pallas kernels for 4%

profile of v4, /device:TPU:0, one launch (start us, length us, event | category | flops | bytes accessed | tf_op | source)
XLA Modules:
  0.0 57.3 jit_solution(16383528177366888216)
XLA Ops:
  0.0 4.0 %collective-permute-start = (bf16[64,128]{1,0:T(8,128)(2,1)}, bf16[64,128]{1,0:T(8,128)(2,1)S(1)}, u32[]{:S(2)}, u32[]{:S(2)}) collective-permute-start(bf16[64,128]{1,0:T(8,128)(2,1)} %param.5), channel_id=1, source_target_pairs={{0,8},{1,9},{2,10},{3,11},{4,12},{5,13},{6,14},{7,15},{8,0},{9,1},... | collective-permute-start | bytes 49160 | tf_op jit(solution)/shard_map/ppermute | solution.py:17
  4.0 0.9 %constant_dynamic-slice_fusion.7 = bf16[64,1024]{1,0:T(8,128)(2,1)S(1)} fusion(bf16[64,8192]{1,0:T(8,128)(2,1)} %param.6, s32[]{:T(128)S(6)} %select_n.37), kind=kLoop, calls=%fused_computation.20 | loop fusion | bytes 262148 | tf_op jit(solution)/shard_map/dynamic_slice | solution.py:353
  5.0 2.4 %collective-permute-start.7 = (bf16[64,1024]{1,0:T(8,128)(2,1)S(1)}, bf16[64,1024]{1,0:T(8,128)(2,1)S(1)}, u32[]{:S(2)}, u32[]{:S(2)}) collective-permute-start(bf16[64,1024]{1,0:T(8,128)(2,1)S(1)} %constant_dynamic-slice_fusion.7), channel_id=1, source_target_pairs={{0,14},{1,15},{2,12},{3,13},{4,10},{5,11},{6,8},{7,9},{8,6},{9,7},... | collective-permute-start | bytes 393224 | tf_op jit(solution)/shard_map/ppermute | solution.py:17
  7.3 1.7 %constant_dynamic-slice_fusion = (bf16[64,1024]{1,0:T(8,128)(2,1)S(1)}, bf16[64,1024]{1,0:T(8,128)(2,1)}, bf16[64,1024]{1,0:T(8,128)(2,1)}) fusion(bf16[64,8192]{1,0:T(8,128)(2,1)} %param.6, s32[]{:T(128)S(6)} %select_n.44, s32[]{:T(128)S(6)} %select_n.43, s32[]{:T(128)S(6)} %select_n.42), kind=kLoop, calls=%fused_computation.13 | loop fusion | bytes 786444 | tf_op jit(solution)/shard_map/dynamic_slice | solution.py:353
  9.1 2.5 %collective-permute-start.6 = (bf16[64,1024]{1,0:T(8,128)(2,1)S(1)}, bf16[64,1024]{1,0:T(8,128)(2,1)S(1)}, u32[]{:S(2)}, u32[]{:S(2)}) collective-permute-start(bf16[64,1024]{1,0:T(8,128)(2,1)S(1)} %get-tuple-element.53), channel_id=1, source_target_pairs={{0,12},{1,13},{2,14},{3,15},{4,8},{5,9},{6,10},{7,11},{8,4},{9,5},... | collective-permute-start | bytes 393224 | tf_op jit(solution)/shard_map/ppermute | solution.py:17
  11.6 0.0 collective-permute-done
  11.6 1.1 %constant_dynamic-slice_fusion.3 = (bf16[64,1024]{1,0:T(8,128)(2,1)S(1)}, bf16[64,1024]{1,0:T(8,128)(2,1)S(1)}, bf16[64,1024]{1,0:T(8,128)(2,1)S(1)}, bf16[64,1024]{1,0:T(8,128)(2,1)S(1)}) fusion(bf16[64,8192]{1,0:T(8,128)(2,1)} %param.6, s32[]{:T(128)S(6)} %select_n.41, s32[]{:T(128)S(6)} %select_n.40, s32[]{:T(128)S(6)} %select_n.39, s32[]{:T(128)S(6)} %select_n.38), kind=kLoop, calls=%fused_computation.16 | loop fusion | bytes 1048592 | tf_op jit(solution)/shard_map/dynamic_slice | solution.py:353
  12.7 0.8 %pad_maximum_fusion.4 = (bf16[64,2304]{1,0:T(8,128)(2,1)}, bf16[64,2304]{1,0:T(8,128)(2,1)S(1)}) fusion(bf16[64,1024]{1,0:T(8,128)(2,1)S(1)} %copy-done, bf16[64,128]{1,0:T(8,128)(2,1)S(1)} %collective-permute-done, bf16[64,128]{1,0:T(8,128)(2,1)S(1)} %copy-done.1, bf16[64,1024]{1,0:T(8,128)(2,1)S(1)} %get-tuple-element.58, ...), kind=kLoop, calls=%fused_computation.4 | loop fusion | flops 1916928 | bytes 1015808 | tf_op jit(solution)/shard_map/concatenate | solution.py:364
  13.5 0.5 collective-permute-start.1
  14.0 0.7 %pad_maximum_fusion.6 = (bf16[64,1280]{1,0:T(8,128)(2,1)}, bf16[64,1280]{1,0:T(8,128)(2,1)}) fusion(bf16[64,128]{1,0:T(8,128)(2,1)S(1)} %collective-permute-done, bf16[64,128]{1,0:T(8,128)(2,1)S(1)} %copy-done.1, bf16[64,1024]{1,0:T(8,128)(2,1)S(1)} %get-tuple-element.56, bf16[64,1024]{1,0:T(8,128)(2,1)S(1)} %get-tuple-element.57), kind=kLoop, calls=%fused_computation.6 | loop fusion | flops 819200 | bytes 622592 | tf_op jit(solution)/shard_map/concatenate | solution.py:364
  14.7 0.7 %collective-permute-start.3 = (bf16[64,1280]{1,0:T(8,128)(2,1)}, bf16[64,1280]{1,0:T(8,128)(2,1)S(1)}, u32[]{:S(2)}, u32[]{:S(2)}) collective-permute-start(bf16[64,1280]{1,0:T(8,128)(2,1)} %get-tuple-element.62), channel_id=1, source_target_pairs={{0,6},{1,7},{2,4},{3,5},{4,2},{5,3},{6,0},{7,1},{8,14},{9,15},{10,... | collective-permute-start | bytes 491528 | tf_op jit(solution)/shard_map/ppermute | solution.py:17
  15.5 2.2 %collective-permute-start.2 = (bf16[64,1280]{1,0:T(8,128)(2,1)}, bf16[64,1280]{1,0:T(8,128)(2,1)S(1)}, u32[]{:S(2)}, u32[]{:S(2)}) collective-permute-start(bf16[64,1280]{1,0:T(8,128)(2,1)} %get-tuple-element.63), channel_id=1, source_target_pairs={{0,4},{1,5},{2,6},{3,7},{4,0},{5,1},{6,2},{7,3},{8,12},{9,13},{10,... | collective-permute-start | bytes 491528 | tf_op jit(solution)/shard_map/ppermute | solution.py:17
  17.7 2.1 %collective-permute-start.5 = (bf16[64,1024]{1,0:T(8,128)(2,1)}, bf16[64,1024]{1,0:T(8,128)(2,1)S(1)}, u32[]{:S(2)}, u32[]{:S(2)}) collective-permute-start(bf16[64,1024]{1,0:T(8,128)(2,1)} %get-tuple-element.54), channel_id=1, source_target_pairs={{0,10},{1,11},{2,8},{3,9},{4,14},{5,15},{6,12},{7,13},{8,2},{9,3},... | collective-permute-start | bytes 393224 | tf_op jit(solution)/shard_map/ppermute | solution.py:17
  19.8 0.9 %collective-permute-start.4 = (bf16[64,1024]{1,0:T(8,128)(2,1)}, bf16[64,1024]{1,0:T(8,128)(2,1)S(1)}, u32[]{:S(2)}, u32[]{:S(2)}) collective-permute-start(bf16[64,1024]{1,0:T(8,128)(2,1)} %get-tuple-element.55), channel_id=1, source_target_pairs={{0,8},{1,9},{2,10},{3,11},{4,12},{5,13},{6,14},{7,15},{8,0},{9,1},... | collective-permute-start | bytes 393224 | tf_op jit(solution)/shard_map/ppermute | solution.py:17
  20.7 2.9 %copy.5 = bf16[16,512,128]{1,2,0:T(8,128)(2,1)S(1)} copy(bf16[16,512,128]{2,1,0:T(8,128)(2,1)} %param.4) | data formatting | bytes 4194304 | tf_op args[0]
  23.6 6.9 %collective-permute-done.5.refs_6_.refs_5_ = bf16[64,1024]{1,0:T(8,128)(2,1)S(1)} collective-permute-done((bf16[64,1024]{1,0:T(8,128)(2,1)}, bf16[64,1024]{1,0:T(8,128)(2,1)S(1)}, u32[]{:S(2)}, u32[]{:S(2)}) %collective-permute-start.5) | collective-permute-done | bytes 131104 | tf_op jit(solution)/shard_map/ppermute | solution.py:17
  30.5 1.1 %collective-permute-done.4.refs_5_.refs_4_ = bf16[64,1024]{1,0:T(8,128)(2,1)S(1)} collective-permute-done((bf16[64,1024]{1,0:T(8,128)(2,1)}, bf16[64,1024]{1,0:T(8,128)(2,1)S(1)}, u32[]{:S(2)}, u32[]{:S(2)}) %collective-permute-start.4) | collective-permute-done | bytes 131104 | tf_op jit(solution)/shard_map/ppermute | solution.py:17
  31.6 0.0 collective-permute-done.3.refs_4_.refs_3_
  31.6 0.0 collective-permute-done.2.refs_3_.refs_2_
  31.6 0.1 shard_map.47
  31.7 0.1 collective-permute-start.8
  31.8 0.5 collective-permute-start.9
  32.3 1.3 %shard_map.46 = (bf16[16,512]{1,0:T(8,128)(2,1)S(1)}, bf16[512,512]{1,0:T(8,128)(2,1)S(1)}, bf16[128,512]{1,0:T(8,128)(2,1)S(1)}) custom-call(s32[1]{0:T(128)} %bitcast.index_ref, bf16[16,128,512]{2,1,0:T(8,128)(2,1)S(1)} %bitcast.2, bf16[64,2304]{1,0:T(8,128)(2,1)S(1)} %get-tuple-element.34.refs_1_.refs_0_.refs_4_, ...), custom_call_target="tpu_custom_call" | custom-call | flops 1073741824 | bytes 2097152 | tf_op jit(solution)/shard_map/pallas_call | solution.py:215
  33.6 0.8 %shard_map.48 = (bf16[16,256]{1,0:T(8,128)(2,1)S(1)}, bf16[256,512]{1,0:T(8,128)(2,1)S(1)}, bf16[128,256]{1,0:T(8,128)(2,1)S(1)}) custom-call(s32[1]{0:T(128)} %bitcast.index_ref, bf16[16,128,512]{2,1,0:T(8,128)(2,1)S(1)} %bitcast.3, bf16[64,3072]{1,0:T(8,128)(2,1)S(1)} %collective-permute-done.8.refs_1_), custom_call_target="tpu_custom_call" | custom-call | flops 536870912 | bytes 2097152 | tf_op jit(solution)/shard_map/pallas_call | solution.py:215
  34.4 0.8 %shard_map.49 = (bf16[16,256]{1,0:T(8,128)(2,1)S(1)}, bf16[256,512]{1,0:T(8,128)(2,1)S(1)}, bf16[128,256]{1,0:T(8,128)(2,1)S(1)}) custom-call(s32[1]{0:T(128)} %bitcast.index_ref, bf16[16,128,512]{2,1,0:T(8,128)(2,1)S(1)} %bitcast.4, bf16[64,3072]{1,0:T(8,128)(2,1)S(1)} %collective-permute-done.8.refs_1_, ...), custom_call_target="tpu_custom_call" | custom-call | flops 536870912 | bytes 2097152 | tf_op jit(solution)/shard_map/pallas_call | solution.py:215
  35.2 2.0 %collective-permute-start.12 = (bf16[16,1024]{1,0:T(8,128)(2,1)S(1)}, bf16[16,1024]{1,0:T(8,128)(2,1)S(1)}, u32[]{:S(2)}, u32[]{:S(2)}) collective-permute-start(bf16[16,1024]{1,0:T(8,128)(2,1)S(1)} %constant_dynamic-update-slice_fusion.refs_0_), channel_id=1, source_target_pairs={{0,12},{1,13},{2,14},{3,15},{4,8},{5,9},{6,10},{7,11},{8,4},{9,5},... | collective-permute-start | bytes 98312 | tf_op jit(solution)/shard_map/ppermute | solution.py:17
  37.2 2.4 %collective-permute-start.10 = (bf16[16,1024]{1,0:T(8,128)(2,1)S(1)}, bf16[16,1024]{1,0:T(8,128)(2,1)S(1)}, u32[]{:S(2)}, u32[]{:S(2)}) collective-permute-start(bf16[16,1024]{1,0:T(8,128)(2,1)S(1)} %constant_dynamic-update-slice_fusion.refs_0_), channel_id=1, source_target_pairs={{0,4},{1,5},{2,6},{3,7},{4,0},{5,1},{6,2},{7,3},{8,12},{9,13},{10,... | collective-permute-start | bytes 98312 | tf_op jit(solution)/shard_map/ppermute | solution.py:17
  39.6 1.4 %collective-permute-done.12.refs_3_ = bf16[16,1024]{1,0:T(8,128)(2,1)S(1)} collective-permute-done((bf16[16,1024]{1,0:T(8,128)(2,1)S(1)}, bf16[16,1024]{1,0:T(8,128)(2,1)S(1)}, u32[]{:S(2)}, u32[]{:S(2)}) %collective-permute-start.12) | collective-permute-done | bytes 32800 | tf_op jit(solution)/shard_map/ppermute | solution.py:17
  41.1 1.0 %collective-permute-done.11.refs_2_ = bf16[16,1024]{1,0:T(8,128)(2,1)S(1)} collective-permute-done((bf16[16,1024]{1,0:T(8,128)(2,1)S(1)}, bf16[16,1024]{1,0:T(8,128)(2,1)S(1)}, u32[]{:S(2)}, u32[]{:S(2)}) %collective-permute-start.11) | collective-permute-done | bytes 32800 | tf_op jit(solution)/shard_map/ppermute | solution.py:17
  42.0 0.5 shard_map.50
  42.5 11.4 %all_to_all.5.field_ref = bf16[16,16,256]{2,1,0:T(8,128)(2,1)S(1)} all-to-all(bf16[16,16,256]{2,1,0:T(8,128)(2,1)S(1)} %shard_map.50), channel_id=1, replica_groups=mesh['grp'=2,'row'=16] {'row'}, dimensions={0} | all-to-all | bytes 262144 | tf_op jit(solution)/shard_map/all_to_all | solution.py:380
  53.9 3.4 %shard_map.51 = bf16[16,512,128]{2,1,0:T(8,128)(2,1)} custom-call(s32[1]{0:T(128)} %bitcast.index_ref, bf16[16,16,256]{2,1,0:T(8,128)(2,1)S(1)} %all_to_all.5.field_ref, bf16[512,512]{1,0:T(8,128)(2,1)S(1)} %get-tuple-element.47.refs_0_, bf16[256,512]{1,0:T(8,128)(2,1)S(1)} %get-tuple-element.48.refs_1_, bf16[256,512]{1,0:T(8,128)(2,1)S(1)} %get-tuple-element.49.refs_2_, ...), custom_call_target="tpu_custom_call" | custom-call | flops 2147483648 | bytes 2097152 | tf_op jit(solution)/shard_map/pallas_call | solution.py:322
  (14 shorter events, 0.0 us)
Async XLA Ops:
  0.0 12.7 %copy-start.1 = (bf16[64,128]{1,0:T(8,128)(2,1)S(1)}, bf16[64,128]{1,0:T(8,128)(2,1)}, u32[]{:S(2)}) copy-start(bf16[64,128]{1,0:T(8,128)(2,1)} %param.5) | copy-start | bytes 49156
  0.0 12.7 %copy-start = (bf16[64,1024]{1,0:T(8,128)(2,1)S(1)}, bf16[64,1024]{1,0:T(8,128)(2,1)}, u32[]{:S(2)}) copy-start(bf16[64,1024]{1,0:T(8,128)(2,1)} %param.7) | copy-start | bytes 393220
  0.0 11.5 %collective-permute-start = (bf16[64,128]{1,0:T(8,128)(2,1)}, bf16[64,128]{1,0:T(8,128)(2,1)S(1)}, u32[]{:S(2)}, u32[]{:S(2)}) collective-permute-start(bf16[64,128]{1,0:T(8,128)(2,1)} %param.5), channel_id=1, source_target_pairs={{0,8},{1,9},{2,10},{3,11},{4,12},{5,13},{6,14},{7,15},{8,0},{9,1},... | collective-permute-start | bytes 49160 | tf_op jit(solution)/shard_map/ppermute | solution.py:17
  5.0 12.7 %collective-permute-start.7 = (bf16[64,1024]{1,0:T(8,128)(2,1)S(1)}, bf16[64,1024]{1,0:T(8,128)(2,1)S(1)}, u32[]{:S(2)}, u32[]{:S(2)}) collective-permute-start(bf16[64,1024]{1,0:T(8,128)(2,1)S(1)} %constant_dynamic-slice_fusion.7), channel_id=1, source_target_pairs={{0,14},{1,15},{2,12},{3,13},{4,10},{5,11},{6,8},{7,9},{8,6},{9,7},... | collective-permute-start | bytes 393224 | tf_op jit(solution)/shard_map/ppermute | solution.py:17
  9.1 10.7 %collective-permute-start.6 = (bf16[64,1024]{1,0:T(8,128)(2,1)S(1)}, bf16[64,1024]{1,0:T(8,128)(2,1)S(1)}, u32[]{:S(2)}, u32[]{:S(2)}) collective-permute-start(bf16[64,1024]{1,0:T(8,128)(2,1)S(1)} %get-tuple-element.53), channel_id=1, source_target_pairs={{0,12},{1,13},{2,14},{3,15},{4,8},{5,9},{6,10},{7,11},{8,4},{9,5},... | collective-permute-start | bytes 393224 | tf_op jit(solution)/shard_map/ppermute | solution.py:17
  13.5 18.2 %collective-permute-start.1 = (bf16[64,2304]{1,0:T(8,128)(2,1)}, bf16[64,2304]{1,0:T(8,128)(2,1)S(1)}, u32[]{:S(2)}, u32[]{:S(2)}) collective-permute-start(bf16[64,2304]{1,0:T(8,128)(2,1)} %get-tuple-element.60), channel_id=1, source_target_pairs={{0,2},{1,3},{2,0},{3,1},{4,6},{5,7},{6,4},{7,5},{8,10},{9,11},{10,... | collective-permute-start | bytes 884744 | tf_op jit(solution)/shard_map/ppermute | solution.py:17
  14.7 16.9 %collective-permute-start.3 = (bf16[64,1280]{1,0:T(8,128)(2,1)}, bf16[64,1280]{1,0:T(8,128)(2,1)S(1)}, u32[]{:S(2)}, u32[]{:S(2)}) collective-permute-start(bf16[64,1280]{1,0:T(8,128)(2,1)} %get-tuple-element.62), channel_id=1, source_target_pairs={{0,6},{1,7},{2,4},{3,5},{4,2},{5,3},{6,0},{7,1},{8,14},{9,15},{10,... | collective-permute-start | bytes 491528 | tf_op jit(solution)/shard_map/ppermute | solution.py:17
  15.5 16.2 %collective-permute-start.2 = (bf16[64,1280]{1,0:T(8,128)(2,1)}, bf16[64,1280]{1,0:T(8,128)(2,1)S(1)}, u32[]{:S(2)}, u32[]{:S(2)}) collective-permute-start(bf16[64,1280]{1,0:T(8,128)(2,1)} %get-tuple-element.63), channel_id=1, source_target_pairs={{0,4},{1,5},{2,6},{3,7},{4,0},{5,1},{6,2},{7,3},{8,12},{9,13},{10,... | collective-permute-start | bytes 491528 | tf_op jit(solution)/shard_map/ppermute | solution.py:17
  17.7 12.8 %collective-permute-start.5 = (bf16[64,1024]{1,0:T(8,128)(2,1)}, bf16[64,1024]{1,0:T(8,128)(2,1)S(1)}, u32[]{:S(2)}, u32[]{:S(2)}) collective-permute-start(bf16[64,1024]{1,0:T(8,128)(2,1)} %get-tuple-element.54), channel_id=1, source_target_pairs={{0,10},{1,11},{2,8},{3,9},{4,14},{5,15},{6,12},{7,13},{8,2},{9,3},... | collective-permute-start | bytes 393224 | tf_op jit(solution)/shard_map/ppermute | solution.py:17
  19.8 11.8 %collective-permute-start.4 = (bf16[64,1024]{1,0:T(8,128)(2,1)}, bf16[64,1024]{1,0:T(8,128)(2,1)S(1)}, u32[]{:S(2)}, u32[]{:S(2)}) collective-permute-start(bf16[64,1024]{1,0:T(8,128)(2,1)} %get-tuple-element.55), channel_id=1, source_target_pairs={{0,8},{1,9},{2,10},{3,11},{4,12},{5,13},{6,14},{7,15},{8,0},{9,1},... | collective-permute-start | bytes 393224 | tf_op jit(solution)/shard_map/ppermute | solution.py:17
  31.7 1.9 %collective-permute-start.8 = (bf16[64,3072]{1,0:T(8,128)(2,1)S(1)}, bf16[64,3072]{1,0:T(8,128)(2,1)S(1)}, u32[]{:S(2)}, u32[]{:S(2)}) collective-permute-start(bf16[64,3072]{1,0:T(8,128)(2,1)S(1)} %get-tuple-element.43), channel_id=1, source_target_pairs={{0,1},{1,0},{2,3},{3,2},{4,5},{5,4},{6,7},{7,6},{8,9},{9,8},{10,11... | collective-permute-start | bytes 1179656 | tf_op jit(solution)/shard_map/ppermute | solution.py:17
  31.8 2.6 %collective-permute-start.9 = (bf16[64,4096]{1,0:T(8,128)(2,1)S(1)}, bf16[64,4096]{1,0:T(8,128)(2,1)S(1)}, u32[]{:S(2)}, u32[]{:S(2)}) collective-permute-start(bf16[64,4096]{1,0:T(8,128)(2,1)S(1)} %get-tuple-element.45), channel_id=1, source_target_pairs={{0,1},{1,0},{2,3},{3,2},{4,5},{5,4},{6,7},{7,6},{8,9},{9,8},{10,11... | collective-permute-start | bytes 1572872 | tf_op jit(solution)/shard_map/ppermute | solution.py:17
  35.2 5.9 %collective-permute-start.12 = (bf16[16,1024]{1,0:T(8,128)(2,1)S(1)}, bf16[16,1024]{1,0:T(8,128)(2,1)S(1)}, u32[]{:S(2)}, u32[]{:S(2)}) collective-permute-start(bf16[16,1024]{1,0:T(8,128)(2,1)S(1)} %constant_dynamic-update-slice_fusion.refs_0_), channel_id=1, source_target_pairs={{0,12},{1,13},{2,14},{3,15},{4,8},{5,9},{6,10},{7,11},{8,4},{9,5},... | collective-permute-start | bytes 98312 | tf_op jit(solution)/shard_map/ppermute | solution.py:17
  37.2 4.8 %collective-permute-start.11 = (bf16[16,1024]{1,0:T(8,128)(2,1)S(1)}, bf16[16,1024]{1,0:T(8,128)(2,1)S(1)}, u32[]{:S(2)}, u32[]{:S(2)}) collective-permute-start(bf16[16,1024]{1,0:T(8,128)(2,1)S(1)} %constant_dynamic-update-slice_fusion.refs_0_), channel_id=1, source_target_pairs={{0,8},{1,9},{2,10},{3,11},{4,12},{5,13},{6,14},{7,15},{8,0},{9,1},... | collective-permute-start | bytes 98312 | tf_op jit(solution)/shard_map/ppermute | solution.py:17
  37.2 4.8 %collective-permute-start.10 = (bf16[16,1024]{1,0:T(8,128)(2,1)S(1)}, bf16[16,1024]{1,0:T(8,128)(2,1)S(1)}, u32[]{:S(2)}, u32[]{:S(2)}) collective-permute-start(bf16[16,1024]{1,0:T(8,128)(2,1)S(1)} %constant_dynamic-update-slice_fusion.refs_0_), channel_id=1, source_target_pairs={{0,4},{1,5},{2,6},{3,7},{4,0},{5,1},{6,2},{7,3},{8,12},{9,13},{10,... | collective-permute-start | bytes 98312 | tf_op jit(solution)/shard_map/ppermute | solution.py:17

commit v5 on v4

--- a/solution.py
+++ b/solution.py
@@ -243,13 +243,18 @@
             total = term if total is None else total + term
         place = pl.ds(pl.multiple_of((chip ^ k) * pair, pair), pair)
         held_ref[:, place] = turned(total, core == 1)
-    density = held_ref[...].astype(jnp.bfloat16)
+    total = held_ref[...]
+    high = total.astype(jnp.bfloat16)
+    low = (total - high.astype(jnp.float32)).astype(jnp.bfloat16)
+    density = jnp.concatenate([high, low], axis=0)
+    batch = high.shape[0]
     for k in range(near):
         slab = screened[k]
         at = start + k * points
         both = [slab[:, slab.shape[1] - points :], forwarded[:, at : at + points]]
         both = jnp.concatenate(both, axis=0)
         partial = lax.dot_general(density, both, NT, preferred_element_type=jnp.float32)
+        partial = partial[:batch] + partial[batch:]
         place = pl.ds(pl.multiple_of(((chip % near) ^ k) * pair, pair), pair)
         partial = turned(partial, core == 1).astype(out_ref.dtype)
         for target in range(out_ref.shape[0]):

time: 57.6 us -> 57.6 us (level)
  no operation moved by 1% of the time
where the time goes in v5:
time: 57.6 us; the launch traced here: 57.3 us
  starting transfers between devices  20.4 us (35%)
  blocking collectives  11.4 us (20%)
  waiting for transfers between devices  10.4 us (18%)
  Pallas kernels  6.81 us (12%)
  local copies, waits for them, and re-layouts  6.66 us (12%)
  other arithmetic  1.5 us (3%)
    ppermute x13, starting transfers between devices, swap(): return lax.ppermute(x, AXIS, [(i, i ^ bits) for i in range(size)])  20.4 us
    all_to_all x1, blocking collectives, body_slabs(): field = lax.all_to_all(field, AXIS, split_axis=0, concat_axis=0, tiled=True)  11.4 us
    ppermute x13, waiting for transfers between devices, swap(): return lax.ppermute(x, AXIS, [(i, i ^ bits) for i in range(size)])  10.4 us
    dynamic_slice x3, local copies, waits for them, and re-layouts, columns(): lax.dynamic_slice_in_dim(x, (index // 2 ^ k) * 2 * width, 2 * width, 1)  3.79 us
    pallas_call x1, Pallas kernels, project(): pl.pallas_call(functools.partial(project_kernel, parts=len(conds), span=s...  3.42 us
    unnamed x7, local copies, waits for them, and re-layouts  2.87 us
    pallas_call x3, Pallas kernels, density_part(): pl.pallas_call(functools.partial(density_part_kernel, straight=straight),...  2.83 us
    concatenate x2, other arithmetic, body_slabs(): close.append(jnp.concatenate(parts, axis=1))  1.5 us
  transfers between devices with their start and end apart: 13, of which 4 were waited for; matrix products, arithmetic and copies ran while one was open for 14% of the time, Pallas kernels for 4%

profile of v5, /device:TPU:0, one launch (start us, length us, event | category | flops | bytes accessed | tf_op | source)
XLA Modules:
  0.0 57.3 jit_solution(6892114386502633670)
XLA Ops:
  0.0 4.0 %collective-permute-start = (bf16[64,128]{1,0:T(8,128)(2,1)}, bf16[64,128]{1,0:T(8,128)(2,1)S(1)}, u32[]{:S(2)}, u32[]{:S(2)}) collective-permute-start(bf16[64,128]{1,0:T(8,128)(2,1)} %param.5), channel_id=1, source_target_pairs={{0,8},{1,9},{2,10},{3,11},{4,12},{5,13},{6,14},{7,15},{8,0},{9,1},... | collective-permute-start | bytes 49160 | tf_op jit(solution)/shard_map/ppermute | solution.py:17
  4.0 0.9 %constant_dynamic-slice_fusion.7 = bf16[64,1024]{1,0:T(8,128)(2,1)S(1)} fusion(bf16[64,8192]{1,0:T(8,128)(2,1)} %param.6, s32[]{:T(128)S(6)} %select_n.37), kind=kLoop, calls=%fused_computation.20 | loop fusion | bytes 262148 | tf_op jit(solution)/shard_map/dynamic_slice | solution.py:358
  5.0 2.4 %collective-permute-start.7 = (bf16[64,1024]{1,0:T(8,128)(2,1)S(1)}, bf16[64,1024]{1,0:T(8,128)(2,1)S(1)}, u32[]{:S(2)}, u32[]{:S(2)}) collective-permute-start(bf16[64,1024]{1,0:T(8,128)(2,1)S(1)} %constant_dynamic-slice_fusion.7), channel_id=1, source_target_pairs={{0,14},{1,15},{2,12},{3,13},{4,10},{5,11},{6,8},{7,9},{8,6},{9,7},... | collective-permute-start | bytes 393224 | tf_op jit(solution)/shard_map/ppermute | solution.py:17
  7.3 1.7 %constant_dynamic-slice_fusion = (bf16[64,1024]{1,0:T(8,128)(2,1)S(1)}, bf16[64,1024]{1,0:T(8,128)(2,1)}, bf16[64,1024]{1,0:T(8,128)(2,1)}) fusion(bf16[64,8192]{1,0:T(8,128)(2,1)} %param.6, s32[]{:T(128)S(6)} %select_n.44, s32[]{:T(128)S(6)} %select_n.43, s32[]{:T(128)S(6)} %select_n.42), kind=kLoop, calls=%fused_computation.13 | loop fusion | bytes 786444 | tf_op jit(solution)/shard_map/dynamic_slice | solution.py:358
  9.1 2.5 %collective-permute-start.6 = (bf16[64,1024]{1,0:T(8,128)(2,1)S(1)}, bf16[64,1024]{1,0:T(8,128)(2,1)S(1)}, u32[]{:S(2)}, u32[]{:S(2)}) collective-permute-start(bf16[64,1024]{1,0:T(8,128)(2,1)S(1)} %get-tuple-element.53), channel_id=1, source_target_pairs={{0,12},{1,13},{2,14},{3,15},{4,8},{5,9},{6,10},{7,11},{8,4},{9,5},... | collective-permute-start | bytes 393224 | tf_op jit(solution)/shard_map/ppermute | solution.py:17
  11.6 1.1 %constant_dynamic-slice_fusion.3 = (bf16[64,1024]{1,0:T(8,128)(2,1)S(1)}, bf16[64,1024]{1,0:T(8,128)(2,1)S(1)}, bf16[64,1024]{1,0:T(8,128)(2,1)S(1)}, bf16[64,1024]{1,0:T(8,128)(2,1)S(1)}) fusion(bf16[64,8192]{1,0:T(8,128)(2,1)} %param.6, s32[]{:T(128)S(6)} %select_n.41, s32[]{:T(128)S(6)} %select_n.40, s32[]{:T(128)S(6)} %select_n.39, s32[]{:T(128)S(6)} %select_n.38), kind=kLoop, calls=%fused_computation.16 | loop fusion | bytes 1048592 | tf_op jit(solution)/shard_map/dynamic_slice | solution.py:358
  12.7 0.8 %pad_maximum_fusion.4 = (bf16[64,2304]{1,0:T(8,128)(2,1)}, bf16[64,2304]{1,0:T(8,128)(2,1)S(1)}) fusion(bf16[64,1024]{1,0:T(8,128)(2,1)S(1)} %copy-done, bf16[64,128]{1,0:T(8,128)(2,1)S(1)} %collective-permute-done, bf16[64,128]{1,0:T(8,128)(2,1)S(1)} %copy-done.1, bf16[64,1024]{1,0:T(8,128)(2,1)S(1)} %get-tuple-element.58, ...), kind=kLoop, calls=%fused_computation.4 | loop fusion | flops 1916928 | bytes 1015808 | tf_op jit(solution)/shard_map/concatenate | solution.py:369
  13.5 0.5 collective-permute-start.1
  14.0 0.7 %pad_maximum_fusion.6 = (bf16[64,1280]{1,0:T(8,128)(2,1)}, bf16[64,1280]{1,0:T(8,128)(2,1)}) fusion(bf16[64,128]{1,0:T(8,128)(2,1)S(1)} %collective-permute-done, bf16[64,128]{1,0:T(8,128)(2,1)S(1)} %copy-done.1, bf16[64,1024]{1,0:T(8,128)(2,1)S(1)} %get-tuple-element.56, bf16[64,1024]{1,0:T(8,128)(2,1)S(1)} %get-tuple-element.57), kind=kLoop, calls=%fused_computation.6 | loop fusion | flops 819200 | bytes 622592 | tf_op jit(solution)/shard_map/concatenate | solution.py:369
  14.7 0.7 %collective-permute-start.3 = (bf16[64,1280]{1,0:T(8,128)(2,1)}, bf16[64,1280]{1,0:T(8,128)(2,1)S(1)}, u32[]{:S(2)}, u32[]{:S(2)}) collective-permute-start(bf16[64,1280]{1,0:T(8,128)(2,1)} %get-tuple-element.62), channel_id=1, source_target_pairs={{0,6},{1,7},{2,4},{3,5},{4,2},{5,3},{6,0},{7,1},{8,14},{9,15},{10,... | collective-permute-start | bytes 491528 | tf_op jit(solution)/shard_map/ppermute | solution.py:17
  15.5 2.2 %collective-permute-start.2 = (bf16[64,1280]{1,0:T(8,128)(2,1)}, bf16[64,1280]{1,0:T(8,128)(2,1)S(1)}, u32[]{:S(2)}, u32[]{:S(2)}) collective-permute-start(bf16[64,1280]{1,0:T(8,128)(2,1)} %get-tuple-element.63), channel_id=1, source_target_pairs={{0,4},{1,5},{2,6},{3,7},{4,0},{5,1},{6,2},{7,3},{8,12},{9,13},{10,... | collective-permute-start | bytes 491528 | tf_op jit(solution)/shard_map/ppermute | solution.py:17
  17.7 0.0 collective-permute-done.7.refs_8_.refs_7_
  17.7 2.1 %collective-permute-start.5 = (bf16[64,1024]{1,0:T(8,128)(2,1)}, bf16[64,1024]{1,0:T(8,128)(2,1)S(1)}, u32[]{:S(2)}, u32[]{:S(2)}) collective-permute-start(bf16[64,1024]{1,0:T(8,128)(2,1)} %get-tuple-element.54), channel_id=1, source_target_pairs={{0,10},{1,11},{2,8},{3,9},{4,14},{5,15},{6,12},{7,13},{8,2},{9,3},... | collective-permute-start | bytes 393224 | tf_op jit(solution)/shard_map/ppermute | solution.py:17
  19.8 0.0 collective-permute-done.6.refs_7_.refs_6_
  19.8 0.9 %collective-permute-start.4 = (bf16[64,1024]{1,0:T(8,128)(2,1)}, bf16[64,1024]{1,0:T(8,128)(2,1)S(1)}, u32[]{:S(2)}, u32[]{:S(2)}) collective-permute-start(bf16[64,1024]{1,0:T(8,128)(2,1)} %get-tuple-element.55), channel_id=1, source_target_pairs={{0,8},{1,9},{2,10},{3,11},{4,12},{5,13},{6,14},{7,15},{8,0},{9,1},... | collective-permute-start | bytes 393224 | tf_op jit(solution)/shard_map/ppermute | solution.py:17
  20.7 2.9 %copy.5 = bf16[16,512,128]{1,2,0:T(8,128)(2,1)S(1)} copy(bf16[16,512,128]{2,1,0:T(8,128)(2,1)} %param.4) | data formatting | bytes 4194304 | tf_op args[0]
  23.6 6.9 %collective-permute-done.5.refs_6_.refs_5_ = bf16[64,1024]{1,0:T(8,128)(2,1)S(1)} collective-permute-done((bf16[64,1024]{1,0:T(8,128)(2,1)}, bf16[64,1024]{1,0:T(8,128)(2,1)S(1)}, u32[]{:S(2)}, u32[]{:S(2)}) %collective-permute-start.5) | collective-permute-done | bytes 131104 | tf_op jit(solution)/shard_map/ppermute | solution.py:17
  30.5 1.1 %collective-permute-done.4.refs_5_.refs_4_ = bf16[64,1024]{1,0:T(8,128)(2,1)S(1)} collective-permute-done((bf16[64,1024]{1,0:T(8,128)(2,1)}, bf16[64,1024]{1,0:T(8,128)(2,1)S(1)}, u32[]{:S(2)}, u32[]{:S(2)}) %collective-permute-start.4) | collective-permute-done | bytes 131104 | tf_op jit(solution)/shard_map/ppermute | solution.py:17
  31.6 0.1 shard_map.47
  31.7 0.1 collective-permute-start.8
  31.8 0.5 collective-permute-start.9
  32.3 1.3 %shard_map.46 = (bf16[16,512]{1,0:T(8,128)(2,1)S(1)}, bf16[512,512]{1,0:T(8,128)(2,1)S(1)}, bf16[128,512]{1,0:T(8,128)(2,1)S(1)}) custom-call(s32[1]{0:T(128)} %bitcast.index_ref, bf16[16,128,512]{2,1,0:T(8,128)(2,1)S(1)} %bitcast.2, bf16[64,2304]{1,0:T(8,128)(2,1)S(1)} %get-tuple-element.34.refs_1_.refs_0_.refs_4_, ...), custom_call_target="tpu_custom_call" | custom-call | flops 1073741824 | bytes 2097152 | tf_op jit(solution)/shard_map/pallas_call | solution.py:215
  33.6 0.0 collective-permute-done.8.refs_1_
  33.6 0.8 %shard_map.48 = (bf16[16,256]{1,0:T(8,128)(2,1)S(1)}, bf16[256,512]{1,0:T(8,128)(2,1)S(1)}, bf16[128,256]{1,0:T(8,128)(2,1)S(1)}) custom-call(s32[1]{0:T(128)} %bitcast.index_ref, bf16[16,128,512]{2,1,0:T(8,128)(2,1)S(1)} %bitcast.3, bf16[64,3072]{1,0:T(8,128)(2,1)S(1)} %collective-permute-done.8.refs_1_), custom_call_target="tpu_custom_call" | custom-call | flops 536870912 | bytes 2097152 | tf_op jit(solution)/shard_map/pallas_call | solution.py:215
  34.4 0.8 %shard_map.49 = (bf16[16,256]{1,0:T(8,128)(2,1)S(1)}, bf16[256,512]{1,0:T(8,128)(2,1)S(1)}, bf16[128,256]{1,0:T(8,128)(2,1)S(1)}) custom-call(s32[1]{0:T(128)} %bitcast.index_ref, bf16[16,128,512]{2,1,0:T(8,128)(2,1)S(1)} %bitcast.4, bf16[64,3072]{1,0:T(8,128)(2,1)S(1)} %collective-permute-done.8.refs_1_, ...), custom_call_target="tpu_custom_call" | custom-call | flops 536870912 | bytes 2097152 | tf_op jit(solution)/shard_map/pallas_call | solution.py:215
  35.2 2.0 %collective-permute-start.12 = (bf16[16,1024]{1,0:T(8,128)(2,1)S(1)}, bf16[16,1024]{1,0:T(8,128)(2,1)S(1)}, u32[]{:S(2)}, u32[]{:S(2)}) collective-permute-start(bf16[16,1024]{1,0:T(8,128)(2,1)S(1)} %constant_dynamic-update-slice_fusion.refs_0_), channel_id=1, source_target_pairs={{0,12},{1,13},{2,14},{3,15},{4,8},{5,9},{6,10},{7,11},{8,4},{9,5},... | collective-permute-start | bytes 98312 | tf_op jit(solution)/shard_map/ppermute | solution.py:17
  37.2 2.4 %collective-permute-start.10 = (bf16[16,1024]{1,0:T(8,128)(2,1)S(1)}, bf16[16,1024]{1,0:T(8,128)(2,1)S(1)}, u32[]{:S(2)}, u32[]{:S(2)}) collective-permute-start(bf16[16,1024]{1,0:T(8,128)(2,1)S(1)} %constant_dynamic-update-slice_fusion.refs_0_), channel_id=1, source_target_pairs={{0,4},{1,5},{2,6},{3,7},{4,0},{5,1},{6,2},{7,3},{8,12},{9,13},{10,... | collective-permute-start | bytes 98312 | tf_op jit(solution)/shard_map/ppermute | solution.py:17
  39.6 1.4 %collective-permute-done.12.refs_3_ = bf16[16,1024]{1,0:T(8,128)(2,1)S(1)} collective-permute-done((bf16[16,1024]{1,0:T(8,128)(2,1)S(1)}, bf16[16,1024]{1,0:T(8,128)(2,1)S(1)}, u32[]{:S(2)}, u32[]{:S(2)}) %collective-permute-start.12) | collective-permute-done | bytes 32800 | tf_op jit(solution)/shard_map/ppermute | solution.py:17
  41.1 1.0 %collective-permute-done.11.refs_2_ = bf16[16,1024]{1,0:T(8,128)(2,1)S(1)} collective-permute-done((bf16[16,1024]{1,0:T(8,128)(2,1)S(1)}, bf16[16,1024]{1,0:T(8,128)(2,1)S(1)}, u32[]{:S(2)}, u32[]{:S(2)}) %collective-permute-start.11) | collective-permute-done | bytes 32800 | tf_op jit(solution)/shard_map/ppermute | solution.py:17
  42.0 0.5 shard_map.50
  42.5 11.4 %all_to_all.5.field_ref = bf16[16,16,256]{2,1,0:T(8,128)(2,1)S(1)} all-to-all(bf16[16,16,256]{2,1,0:T(8,128)(2,1)S(1)} %shard_map.50), channel_id=1, replica_groups=mesh['grp'=2,'row'=16] {'row'}, dimensions={0} | all-to-all | bytes 262144 | tf_op jit(solution)/shard_map/all_to_all | solution.py:385
  53.9 3.4 %shard_map.51 = bf16[16,512,128]{2,1,0:T(8,128)(2,1)} custom-call(s32[1]{0:T(128)} %bitcast.index_ref, bf16[16,16,256]{2,1,0:T(8,128)(2,1)S(1)} %all_to_all.5.field_ref, bf16[512,512]{1,0:T(8,128)(2,1)S(1)} %get-tuple-element.47.refs_0_, bf16[256,512]{1,0:T(8,128)(2,1)S(1)} %get-tuple-element.48.refs_1_, bf16[256,512]{1,0:T(8,128)(2,1)S(1)} %get-tuple-element.49.refs_2_, ...), custom_call_target="tpu_custom_call" | custom-call | flops 2147483648 | bytes 2097152 | tf_op jit(solution)/shard_map/pallas_call | solution.py:327
  (14 shorter events, 0.0 us)
Async XLA Ops:
  0.0 12.7 %copy-start.1 = (bf16[64,128]{1,0:T(8,128)(2,1)S(1)}, bf16[64,128]{1,0:T(8,128)(2,1)}, u32[]{:S(2)}) copy-start(bf16[64,128]{1,0:T(8,128)(2,1)} %param.5) | copy-start | bytes 49156
  0.0 12.7 %copy-start = (bf16[64,1024]{1,0:T(8,128)(2,1)S(1)}, bf16[64,1024]{1,0:T(8,128)(2,1)}, u32[]{:S(2)}) copy-start(bf16[64,1024]{1,0:T(8,128)(2,1)} %param.7) | copy-start | bytes 393220
  0.0 11.5 %collective-permute-start = (bf16[64,128]{1,0:T(8,128)(2,1)}, bf16[64,128]{1,0:T(8,128)(2,1)S(1)}, u32[]{:S(2)}, u32[]{:S(2)}) collective-permute-start(bf16[64,128]{1,0:T(8,128)(2,1)} %param.5), channel_id=1, source_target_pairs={{0,8},{1,9},{2,10},{3,11},{4,12},{5,13},{6,14},{7,15},{8,0},{9,1},... | collective-permute-start | bytes 49160 | tf_op jit(solution)/shard_map/ppermute | solution.py:17
  5.0 12.7 %collective-permute-start.7 = (bf16[64,1024]{1,0:T(8,128)(2,1)S(1)}, bf16[64,1024]{1,0:T(8,128)(2,1)S(1)}, u32[]{:S(2)}, u32[]{:S(2)}) collective-permute-start(bf16[64,1024]{1,0:T(8,128)(2,1)S(1)} %constant_dynamic-slice_fusion.7), channel_id=1, source_target_pairs={{0,14},{1,15},{2,12},{3,13},{4,10},{5,11},{6,8},{7,9},{8,6},{9,7},... | collective-permute-start | bytes 393224 | tf_op jit(solution)/shard_map/ppermute | solution.py:17
  9.1 10.7 %collective-permute-start.6 = (bf16[64,1024]{1,0:T(8,128)(2,1)S(1)}, bf16[64,1024]{1,0:T(8,128)(2,1)S(1)}, u32[]{:S(2)}, u32[]{:S(2)}) collective-permute-start(bf16[64,1024]{1,0:T(8,128)(2,1)S(1)} %get-tuple-element.53), channel_id=1, source_target_pairs={{0,12},{1,13},{2,14},{3,15},{4,8},{5,9},{6,10},{7,11},{8,4},{9,5},... | collective-permute-start | bytes 393224 | tf_op jit(solution)/shard_map/ppermute | solution.py:17
  13.5 18.2 %collective-permute-start.1 = (bf16[64,2304]{1,0:T(8,128)(2,1)}, bf16[64,2304]{1,0:T(8,128)(2,1)S(1)}, u32[]{:S(2)}, u32[]{:S(2)}) collective-permute-start(bf16[64,2304]{1,0:T(8,128)(2,1)} %get-tuple-element.60), channel_id=1, source_target_pairs={{0,2},{1,3},{2,0},{3,1},{4,6},{5,7},{6,4},{7,5},{8,10},{9,11},{10,... | collective-permute-start | bytes 884744 | tf_op jit(solution)/shard_map/ppermute | solution.py:17
  14.7 16.9 %collective-permute-start.3 = (bf16[64,1280]{1,0:T(8,128)(2,1)}, bf16[64,1280]{1,0:T(8,128)(2,1)S(1)}, u32[]{:S(2)}, u32[]{:S(2)}) collective-permute-start(bf16[64,1280]{1,0:T(8,128)(2,1)} %get-tuple-element.62), channel_id=1, source_target_pairs={{0,6},{1,7},{2,4},{3,5},{4,2},{5,3},{6,0},{7,1},{8,14},{9,15},{10,... | collective-permute-start | bytes 491528 | tf_op jit(solution)/shard_map/ppermute | solution.py:17
  15.5 16.2 %collective-permute-start.2 = (bf16[64,1280]{1,0:T(8,128)(2,1)}, bf16[64,1280]{1,0:T(8,128)(2,1)S(1)}, u32[]{:S(2)}, u32[]{:S(2)}) collective-permute-start(bf16[64,1280]{1,0:T(8,128)(2,1)} %get-tuple-element.63), channel_id=1, source_target_pairs={{0,4},{1,5},{2,6},{3,7},{4,0},{5,1},{6,2},{7,3},{8,12},{9,13},{10,... | collective-permute-start | bytes 491528 | tf_op jit(solution)/shard_map/ppermute | solution.py:17
  17.7 12.8 %collective-permute-start.5 = (bf16[64,1024]{1,0:T(8,128)(2,1)}, bf16[64,1024]{1,0:T(8,128)(2,1)S(1)}, u32[]{:S(2)}, u32[]{:S(2)}) collective-permute-start(bf16[64,1024]{1,0:T(8,128)(2,1)} %get-tuple-element.54), channel_id=1, source_target_pairs={{0,10},{1,11},{2,8},{3,9},{4,14},{5,15},{6,12},{7,13},{8,2},{9,3},... | collective-permute-start | bytes 393224 | tf_op jit(solution)/shard_map/ppermute | solution.py:17
  19.8 11.8 %collective-permute-start.4 = (bf16[64,1024]{1,0:T(8,128)(2,1)}, bf16[64,1024]{1,0:T(8,128)(2,1)S(1)}, u32[]{:S(2)}, u32[]{:S(2)}) collective-permute-start(bf16[64,1024]{1,0:T(8,128)(2,1)} %get-tuple-element.55), channel_id=1, source_target_pairs={{0,8},{1,9},{2,10},{3,11},{4,12},{5,13},{6,14},{7,15},{8,0},{9,1},... | collective-permute-start | bytes 393224 | tf_op jit(solution)/shard_map/ppermute | solution.py:17
  31.7 1.9 %collective-permute-start.8 = (bf16[64,3072]{1,0:T(8,128)(2,1)S(1)}, bf16[64,3072]{1,0:T(8,128)(2,1)S(1)}, u32[]{:S(2)}, u32[]{:S(2)}) collective-permute-start(bf16[64,3072]{1,0:T(8,128)(2,1)S(1)} %get-tuple-element.43), channel_id=1, source_target_pairs={{0,1},{1,0},{2,3},{3,2},{4,5},{5,4},{6,7},{7,6},{8,9},{9,8},{10,11... | collective-permute-start | bytes 1179656 | tf_op jit(solution)/shard_map/ppermute | solution.py:17
  31.8 2.6 %collective-permute-start.9 = (bf16[64,4096]{1,0:T(8,128)(2,1)S(1)}, bf16[64,4096]{1,0:T(8,128)(2,1)S(1)}, u32[]{:S(2)}, u32[]{:S(2)}) collective-permute-start(bf16[64,4096]{1,0:T(8,128)(2,1)S(1)} %get-tuple-element.45), channel_id=1, source_target_pairs={{0,1},{1,0},{2,3},{3,2},{4,5},{5,4},{6,7},{7,6},{8,9},{9,8},{10,11... | collective-permute-start | bytes 1572872 | tf_op jit(solution)/shard_map/ppermute | solution.py:17
  35.2 5.9 %collective-permute-start.12 = (bf16[16,1024]{1,0:T(8,128)(2,1)S(1)}, bf16[16,1024]{1,0:T(8,128)(2,1)S(1)}, u32[]{:S(2)}, u32[]{:S(2)}) collective-permute-start(bf16[16,1024]{1,0:T(8,128)(2,1)S(1)} %constant_dynamic-update-slice_fusion.refs_0_), channel_id=1, source_target_pairs={{0,12},{1,13},{2,14},{3,15},{4,8},{5,9},{6,10},{7,11},{8,4},{9,5},... | collective-permute-start | bytes 98312 | tf_op jit(solution)/shard_map/ppermute | solution.py:17
  37.2 4.8 %collective-permute-start.11 = (bf16[16,1024]{1,0:T(8,128)(2,1)S(1)}, bf16[16,1024]{1,0:T(8,128)(2,1)S(1)}, u32[]{:S(2)}, u32[]{:S(2)}) collective-permute-start(bf16[16,1024]{1,0:T(8,128)(2,1)S(1)} %constant_dynamic-update-slice_fusion.refs_0_), channel_id=1, source_target_pairs={{0,8},{1,9},{2,10},{3,11},{4,12},{5,13},{6,14},{7,15},{8,0},{9,1},... | collective-permute-start | bytes 98312 | tf_op jit(solution)/shard_map/ppermute | solution.py:17
  37.2 4.8 %collective-permute-start.10 = (bf16[16,1024]{1,0:T(8,128)(2,1)S(1)}, bf16[16,1024]{1,0:T(8,128)(2,1)S(1)}, u32[]{:S(2)}, u32[]{:S(2)}) collective-permute-start(bf16[16,1024]{1,0:T(8,128)(2,1)S(1)} %constant_dynamic-update-slice_fusion.refs_0_), channel_id=1, source_target_pairs={{0,4},{1,5},{2,6},{3,7},{4,0},{5,1},{6,2},{7,3},{8,12},{9,13},{10,... | collective-permute-start | bytes 98312 | tf_op jit(solution)/shard_map/ppermute | solution.py:17

commit v6 on v5

--- a/solution.py
+++ b/solution.py
@@ -256,12 +256,10 @@
         partial = lax.dot_general(density, both, NT, preferred_element_type=jnp.float32)
         partial = partial[:batch] + partial[batch:]
         place = pl.ds(pl.multiple_of(((chip % near) ^ k) * pair, pair), pair)
-        partial = turned(partial, core == 1).astype(out_ref.dtype)
-        for target in range(out_ref.shape[0]):
-            out_ref[target, :, place] = partial
-
-
-def field_of(index, densities, screened, forwarded, copies, start):
+        out_ref[:, place] = turned(partial, core == 1).astype(out_ref.dtype)
+
+
+def field_of(index, densities, screened, forwarded, start):
     batch, points = densities[0].shape
     near, rows = len(screened), screened[0].shape[0]
     whole = pl.BlockSpec(memory_space=VMEM)
@@ -270,7 +268,7 @@
         functools.partial(field_kernel, z_size=len(densities), near=near, start=start, rows=rows),
         in_specs=[pl.BlockSpec(memory_space=pltpu.SMEM)] + [whole] * (len(densities) + near + 1),
         out_specs=whole,
-        out_shape=jax.ShapeDtypeStruct((copies, batch, columns), jnp.bfloat16),
+        out_shape=jax.ShapeDtypeStruct((batch, columns), jnp.bfloat16),
         scratch_shapes=[pltpu.VMEM((batch, points), jnp.float32)],
         compiler_params=pltpu.CompilerParams(vmem_limit_bytes=16 << 20),
         cost_estimate=pl.CostEstimate(
@@ -279,19 +277,17 @@
     )(index, *densities, *screened, forwarded)
 
 
-def project_kernel(index_ref, field_ref, *refs, parts, span):
+def project_kernel(index_ref, *refs, layers, parts, span):
+    fields, refs = refs[:layers], refs[layers:]
     conds, vals = refs[:parts], refs[parts : 2 * parts]
     out_ref, pairs_ref, total_ref, sems = refs[2 * parts :]
-    size, batch, chunk = field_ref.shape
+    batch, chunk = fields[0].shape
     chips, _, pair = pairs_ref.shape
-    near = chunk // pair
-    q_size = 2 * near
-    valence = vals[0].shape[0]
+    near, valence = chunk // pair, vals[0].shape[0]
     chip, core = index_ref[0] // 2, index_ref[0] % 2
-    for layer in range(size // q_size):
-        field = sum(field_ref[layer * q_size + k].astype(jnp.float32) for k in range(q_size))
+    for layer, ref in enumerate(fields):
         for k in range(near):
-            pairs_ref[layer * near + k] = field[:, k * pair : (k + 1) * pair]
+            pairs_ref[(chip // near ^ layer) * near + k] = ref[:, k * pair : (k + 1) * pair].astype(jnp.float32)
     both = [turned(pairs_ref[chip ^ k], core == 1) for k in range(chips)]
     halves = [x[:, : pair // 2] for x in both] + [x[:, pair // 2 :] for x in both]
     field = jnp.concatenate(halves, axis=1)
@@ -318,15 +314,15 @@
         copy.wait()
 
 
-def project(index, field, conds, vals):
-    size, batch, _ = field.shape
+def project(index, fields, conds, vals, size):
+    batch = fields[0].shape[0]
     points, width = sum(cond.shape[0] for cond in conds), conds[0].shape[1]
     valence, span = vals[0].shape[0], math.gcd(batch, 4)
     whole = pl.BlockSpec(memory_space=VMEM)
     shape = (batch, width, valence)
     return pl.pallas_call(
-        functools.partial(project_kernel, parts=len(conds), span=span),
-        in_specs=[pl.BlockSpec(memory_space=pltpu.SMEM)] + [whole] * (1 + 2 * len(conds)),
+        functools.partial(project_kernel, layers=len(fields), parts=len(conds), span=span),
+        in_specs=[pl.BlockSpec(memory_space=pltpu.SMEM)] + [whole] * (len(fields) + 2 * len(conds)),
         out_specs=pl.BlockSpec(memory_space=pl.ANY),
         out_shape=jax.ShapeDtypeStruct(shape, jnp.bfloat16),
         scratch_shapes=[
@@ -340,7 +336,7 @@
             bytes_accessed=2 * batch * width * valence,
             transcendentals=0,
         ),
-    )(index, field, *conds, *vals)
+    )(index, *fields, *conds, *vals)
 
 
 def body_slabs(size, excitations, valence_orb, conduction_orb, screened):
@@ -381,9 +377,9 @@
     density = jnp.concatenate(density, axis=1)
 
     densities = exchange(density, q_size, z_size, size)
-    field = field_of(place, densities, slabs[:near], far_part, size, half * width)
-    field = lax.all_to_all(field, AXIS, split_axis=0, concat_axis=0, tiled=True)
-    return project(place, field, conds, vals)
+    partial = field_of(place, densities, slabs[:near], far_part, half * width)
+    field = sum(x.astype(jnp.float32) for x in exchange(partial, 1, q_size, size)).astype(jnp.bfloat16)
+    return project(place, exchange(field, q_size, z_size, size), conds, vals, size)
 
 
 def body(size, excitations, valence_orb, conduction_orb, screened):

time: 57.6 us -> 56.6 us (0.983)
  blocking collectives: 11.4 us -> 0 us
  starting transfers between devices: 20.4 us -> 26.7 us
  waiting for transfers between devices: 10.4 us -> 14.6 us
    all_to_all x1 -> x0, blocking collectives: 11.4 us -> none  [body_slabs(): field = lax.all_to_all(field, AXIS, split_axis=0, concat_axis=0, tiled=True)]
    ppermute x13 -> x19, starting transfers between devices: 20.4 us -> 26.7 us  [swap(): return lax.ppermute(x, AXIS, [(i, i ^ bits) for i in range(size)])]
    ppermute x13 -> x19, waiting for transfers between devices: 10.4 us -> 14.6 us  [swap(): return lax.ppermute(x, AXIS, [(i, i ^ bits) for i in range(size)])]
  transfers between devices with their start and end apart: 13 -> 19, of which waited for: 4 -> 9; matrix products, arithmetic and copies ran while one was open for 14% -> 14% of each run, Pallas kernels for 4% -> 4%
where the time goes in v6:
time: 56.6 us; the launch traced here: 56.4 us
  starting transfers between devices  26.7 us (47%)
  waiting for transfers between devices  14.6 us (26%)
  Pallas kernels  6.77 us (12%)
  local copies, waits for them, and re-layouts  6.68 us (12%)
  other arithmetic  1.52 us (3%)
    ppermute x19, starting transfers between devices, swap(): return lax.ppermute(x, AXIS, [(i, i ^ bits) for i in range(size)])  26.7 us
    ppermute x19, waiting for transfers between devices, swap(): return lax.ppermute(x, AXIS, [(i, i ^ bits) for i in range(size)])  14.6 us
    dynamic_slice x3, local copies, waits for them, and re-layouts, columns(): lax.dynamic_slice_in_dim(x, (index // 2 ^ k) * 2 * width, 2 * width, 1)  3.81 us
    pallas_call x1, Pallas kernels, project(): pl.pallas_call(functools.partial(project_kernel, layers=len(fields), part...  3.41 us
    unnamed x7, local copies, waits for them, and re-layouts  2.87 us
    pallas_call x3, Pallas kernels, density_part(): pl.pallas_call(functools.partial(density_part_kernel, straight=straight),...  2.83 us
    concatenate x2, other arithmetic, body_slabs(): close.append(jnp.concatenate(parts, axis=1))  1.51 us
  transfers between devices with their start and end apart: 19, of which 9 were waited for; matrix products, arithmetic and copies ran while one was open for 14% of the time, Pallas kernels for 4%

profile of v6, /device:TPU:0, one launch (start us, length us, event | category | flops | bytes accessed | tf_op | source)
XLA Modules:
  0.0 56.4 jit_solution(8876384560718581237)
XLA Ops:
  0.0 4.0 %collective-permute-start = (bf16[64,128]{1,0:T(8,128)(2,1)}, bf16[64,128]{1,0:T(8,128)(2,1)S(1)}, u32[]{:S(2)}, u32[]{:S(2)}) collective-permute-start(bf16[64,128]{1,0:T(8,128)(2,1)} %param.5), channel_id=1, source_target_pairs={{0,8},{1,9},{2,10},{3,11},{4,12},{5,13},{6,14},{7,15},{8,0},{9,1},... | collective-permute-start | bytes 49160 | tf_op jit(solution)/shard_map/ppermute | solution.py:17
  4.0 0.9 %constant_dynamic-slice_fusion.7 = bf16[64,1024]{1,0:T(8,128)(2,1)S(1)} fusion(bf16[64,8192]{1,0:T(8,128)(2,1)} %param.6, s32[]{:T(128)S(6)} %select_n.37), kind=kLoop, calls=%fused_computation.21 | loop fusion | bytes 262148 | tf_op jit(solution)/shard_map/dynamic_slice | solution.py:354
  5.0 2.4 %collective-permute-start.7 = (bf16[64,1024]{1,0:T(8,128)(2,1)S(1)}, bf16[64,1024]{1,0:T(8,128)(2,1)S(1)}, u32[]{:S(2)}, u32[]{:S(2)}) collective-permute-start(bf16[64,1024]{1,0:T(8,128)(2,1)S(1)} %constant_dynamic-slice_fusion.7), channel_id=1, source_target_pairs={{0,14},{1,15},{2,12},{3,13},{4,10},{5,11},{6,8},{7,9},{8,6},{9,7},... | collective-permute-start | bytes 393224 | tf_op jit(solution)/shard_map/ppermute | solution.py:17
  7.3 1.8 %constant_dynamic-slice_fusion = (bf16[64,1024]{1,0:T(8,128)(2,1)S(1)}, bf16[64,1024]{1,0:T(8,128)(2,1)}, bf16[64,1024]{1,0:T(8,128)(2,1)}) fusion(bf16[64,8192]{1,0:T(8,128)(2,1)} %param.6, s32[]{:T(128)S(6)} %select_n.44, s32[]{:T(128)S(6)} %select_n.43, s32[]{:T(128)S(6)} %select_n.42), kind=kLoop, calls=%fused_computation.14 | loop fusion | bytes 786444 | tf_op jit(solution)/shard_map/dynamic_slice | solution.py:354
  9.1 2.5 %collective-permute-start.6 = (bf16[64,1024]{1,0:T(8,128)(2,1)S(1)}, bf16[64,1024]{1,0:T(8,128)(2,1)S(1)}, u32[]{:S(2)}, u32[]{:S(2)}) collective-permute-start(bf16[64,1024]{1,0:T(8,128)(2,1)S(1)} %get-tuple-element.53), channel_id=1, source_target_pairs={{0,12},{1,13},{2,14},{3,15},{4,8},{5,9},{6,10},{7,11},{8,4},{9,5},... | collective-permute-start | bytes 393224 | tf_op jit(solution)/shard_map/ppermute | solution.py:17
  11.6 1.1 %constant_dynamic-slice_fusion.3 = (bf16[64,1024]{1,0:T(8,128)(2,1)S(1)}, bf16[64,1024]{1,0:T(8,128)(2,1)S(1)}, bf16[64,1024]{1,0:T(8,128)(2,1)S(1)}, bf16[64,1024]{1,0:T(8,128)(2,1)S(1)}) fusion(bf16[64,8192]{1,0:T(8,128)(2,1)} %param.6, s32[]{:T(128)S(6)} %select_n.41, s32[]{:T(128)S(6)} %select_n.40, s32[]{:T(128)S(6)} %select_n.39, s32[]{:T(128)S(6)} %select_n.38), kind=kLoop, calls=%fused_computation.17 | loop fusion | bytes 1048592 | tf_op jit(solution)/shard_map/dynamic_slice | solution.py:354
  12.7 0.8 %pad_maximum_fusion.4 = (bf16[64,2304]{1,0:T(8,128)(2,1)}, bf16[64,2304]{1,0:T(8,128)(2,1)S(1)}) fusion(bf16[64,1024]{1,0:T(8,128)(2,1)S(1)} %copy-done, bf16[64,128]{1,0:T(8,128)(2,1)S(1)} %collective-permute-done, bf16[64,128]{1,0:T(8,128)(2,1)S(1)} %copy-done.1, bf16[64,1024]{1,0:T(8,128)(2,1)S(1)} %get-tuple-element.58, ...), kind=kLoop, calls=%fused_computation.4 | loop fusion | flops 1916928 | bytes 1015808 | tf_op jit(solution)/shard_map/concatenate | solution.py:365
  14.0 0.8 %pad_maximum_fusion.6 = (bf16[64,1280]{1,0:T(8,128)(2,1)}, bf16[64,1280]{1,0:T(8,128)(2,1)}) fusion(bf16[64,128]{1,0:T(8,128)(2,1)S(1)} %collective-permute-done, bf16[64,128]{1,0:T(8,128)(2,1)S(1)} %copy-done.1, bf16[64,1024]{1,0:T(8,128)(2,1)S(1)} %get-tuple-element.56, bf16[64,1024]{1,0:T(8,128)(2,1)S(1)} %get-tuple-element.57), kind=kLoop, calls=%fused_computation.6 | loop fusion | flops 819200 | bytes 622592 | tf_op jit(solution)/shard_map/concatenate | solution.py:365
  14.7 0.7 %collective-permute-start.3 = (bf16[64,1280]{1,0:T(8,128)(2,1)}, bf16[64,1280]{1,0:T(8,128)(2,1)S(1)}, u32[]{:S(2)}, u32[]{:S(2)}) collective-permute-start(bf16[64,1280]{1,0:T(8,128)(2,1)} %get-tuple-element.62), channel_id=1, source_target_pairs={{0,6},{1,7},{2,4},{3,5},{4,2},{5,3},{6,0},{7,1},{8,14},{9,15},{10,... | collective-permute-start | bytes 491528 | tf_op jit(solution)/shard_map/ppermute | solution.py:17
  15.5 2.2 %collective-permute-start.2 = (bf16[64,1280]{1,0:T(8,128)(2,1)}, bf16[64,1280]{1,0:T(8,128)(2,1)S(1)}, u32[]{:S(2)}, u32[]{:S(2)}) collective-permute-start(bf16[64,1280]{1,0:T(8,128)(2,1)} %get-tuple-element.63), channel_id=1, source_target_pairs={{0,4},{1,5},{2,6},{3,7},{4,0},{5,1},{6,2},{7,3},{8,12},{9,13},{10,... | collective-permute-start | bytes 491528 | tf_op jit(solution)/shard_map/ppermute | solution.py:17
  17.7 2.0 %collective-permute-start.5 = (bf16[64,1024]{1,0:T(8,128)(2,1)}, bf16[64,1024]{1,0:T(8,128)(2,1)S(1)}, u32[]{:S(2)}, u32[]{:S(2)}) collective-permute-start(bf16[64,1024]{1,0:T(8,128)(2,1)} %get-tuple-element.54), channel_id=1, source_target_pairs={{0,10},{1,11},{2,8},{3,9},{4,14},{5,15},{6,12},{7,13},{8,2},{9,3},... | collective-permute-start | bytes 393224 | tf_op jit(solution)/shard_map/ppermute | solution.py:17
  19.8 0.9 %collective-permute-start.4 = (bf16[64,1024]{1,0:T(8,128)(2,1)}, bf16[64,1024]{1,0:T(8,128)(2,1)S(1)}, u32[]{:S(2)}, u32[]{:S(2)}) collective-permute-start(bf16[64,1024]{1,0:T(8,128)(2,1)} %get-tuple-element.55), channel_id=1, source_target_pairs={{0,8},{1,9},{2,10},{3,11},{4,12},{5,13},{6,14},{7,15},{8,0},{9,1},... | collective-permute-start | bytes 393224 | tf_op jit(solution)/shard_map/ppermute | solution.py:17
  20.7 2.9 %copy.5 = bf16[16,512,128]{1,2,0:T(8,128)(2,1)S(1)} copy(bf16[16,512,128]{2,1,0:T(8,128)(2,1)} %param.4) | data formatting | bytes 4194304 | tf_op args[0]
  23.6 6.9 %collective-permute-done.5.refs_6_.refs_5_ = bf16[64,1024]{1,0:T(8,128)(2,1)S(1)} collective-permute-done((bf16[64,1024]{1,0:T(8,128)(2,1)}, bf16[64,1024]{1,0:T(8,128)(2,1)S(1)}, u32[]{:S(2)}, u32[]{:S(2)}) %collective-permute-start.5) | collective-permute-done | bytes 131104 | tf_op jit(solution)/shard_map/ppermute | solution.py:17
  30.5 1.1 %collective-permute-done.4.refs_5_.refs_4_ = bf16[64,1024]{1,0:T(8,128)(2,1)S(1)} collective-permute-done((bf16[64,1024]{1,0:T(8,128)(2,1)}, bf16[64,1024]{1,0:T(8,128)(2,1)S(1)}, u32[]{:S(2)}, u32[]{:S(2)}) %collective-permute-start.4) | collective-permute-done | bytes 131104 | tf_op jit(solution)/shard_map/ppermute | solution.py:17
  32.3 1.3 %shard_map.46 = (bf16[16,512]{1,0:T(8,128)(2,1)S(1)}, bf16[512,512]{1,0:T(8,128)(2,1)S(1)}, bf16[128,512]{1,0:T(8,128)(2,1)S(1)}) custom-call(s32[1]{0:T(128)} %bitcast.index_ref, bf16[16,128,512]{2,1,0:T(8,128)(2,1)S(1)} %bitcast.2, bf16[64,2304]{1,0:T(8,128)(2,1)S(1)} %get-tuple-element.34.refs_1_.refs_0_.refs_4_, ...), custom_call_target="tpu_custom_call" | custom-call | flops 1073741824 | bytes 2097152 | tf_op jit(solution)/shard_map/pallas_call | solution.py:215
  33.6 0.8 %shard_map.48 = (bf16[16,256]{1,0:T(8,128)(2,1)S(1)}, bf16[256,512]{1,0:T(8,128)(2,1)S(1)}, bf16[128,256]{1,0:T(8,128)(2,1)S(1)}) custom-call(s32[1]{0:T(128)} %bitcast.index_ref, bf16[16,128,512]{2,1,0:T(8,128)(2,1)S(1)} %bitcast.3, bf16[64,3072]{1,0:T(8,128)(2,1)S(1)} %collective-permute-done.8.refs_1_), custom_call_target="tpu_custom_call" | custom-call | flops 536870912 | bytes 2097152 | tf_op jit(solution)/shard_map/pallas_call | solution.py:215
  34.4 0.8 %shard_map.49 = (bf16[16,256]{1,0:T(8,128)(2,1)S(1)}, bf16[256,512]{1,0:T(8,128)(2,1)S(1)}, bf16[128,256]{1,0:T(8,128)(2,1)S(1)}) custom-call(s32[1]{0:T(128)} %bitcast.index_ref, bf16[16,128,512]{2,1,0:T(8,128)(2,1)S(1)} %bitcast.4, bf16[64,3072]{1,0:T(8,128)(2,1)S(1)} %collective-permute-done.8.refs_1_, ...), custom_call_target="tpu_custom_call" | custom-call | flops 536870912 | bytes 2097152 | tf_op jit(solution)/shard_map/pallas_call | solution.py:215
  35.2 2.0 %collective-permute-start.12 = (bf16[16,1024]{1,0:T(8,128)(2,1)S(1)}, bf16[16,1024]{1,0:T(8,128)(2,1)S(1)}, u32[]{:S(2)}, u32[]{:S(2)}) collective-permute-start(bf16[16,1024]{1,0:T(8,128)(2,1)S(1)} %constant_dynamic-update-slice_fusion.refs_0_), channel_id=1, source_target_pairs={{0,12},{1,13},{2,14},{3,15},{4,8},{5,9},{6,10},{7,11},{8,4},{9,5},... | collective-permute-start | bytes 98312 | tf_op jit(solution)/shard_map/ppermute | solution.py:17
  37.2 2.4 %collective-permute-start.10 = (bf16[16,1024]{1,0:T(8,128)(2,1)S(1)}, bf16[16,1024]{1,0:T(8,128)(2,1)S(1)}, u32[]{:S(2)}, u32[]{:S(2)}) collective-permute-start(bf16[16,1024]{1,0:T(8,128)(2,1)S(1)} %constant_dynamic-update-slice_fusion.refs_0_), channel_id=1, source_target_pairs={{0,4},{1,5},{2,6},{3,7},{4,0},{5,1},{6,2},{7,3},{8,12},{9,13},{10,... | collective-permute-start | bytes 98312 | tf_op jit(solution)/shard_map/ppermute | solution.py:17
  39.6 1.4 %collective-permute-done.12.refs_3_ = bf16[16,1024]{1,0:T(8,128)(2,1)S(1)} collective-permute-done((bf16[16,1024]{1,0:T(8,128)(2,1)S(1)}, bf16[16,1024]{1,0:T(8,128)(2,1)S(1)}, u32[]{:S(2)}, u32[]{:S(2)}) %collective-permute-start.12) | collective-permute-done | bytes 32800 | tf_op jit(solution)/shard_map/ppermute | solution.py:17
  41.1 0.9 %collective-permute-done.11.refs_2_ = bf16[16,1024]{1,0:T(8,128)(2,1)S(1)} collective-permute-done((bf16[16,1024]{1,0:T(8,128)(2,1)S(1)}, bf16[16,1024]{1,0:T(8,128)(2,1)S(1)}, u32[]{:S(2)}, u32[]{:S(2)}) %collective-permute-start.11) | collective-permute-done | bytes 32800 | tf_op jit(solution)/shard_map/ppermute | solution.py:17
  42.5 1.0 %collective-permute-start.14 = (bf16[16,256]{1,0:T(8,128)(2,1)S(1)}, bf16[16,256]{1,0:T(8,128)(2,1)S(1)}, u32[]{:S(2)}, u32[]{:S(2)}) collective-permute-start(bf16[16,256]{1,0:T(8,128)(2,1)S(1)} %shard_map.50), channel_id=1, source_target_pairs={{0,2},{1,3},{2,0},{3,1},{4,6},{5,7},{6,4},{7,5},{8,10},{9,11},{10,... | collective-permute-start | bytes 24584 | tf_op jit(solution)/shard_map/ppermute | solution.py:17
  43.5 0.9 %collective-permute-start.13 = (bf16[16,256]{1,0:T(8,128)(2,1)S(1)}, bf16[16,256]{1,0:T(8,128)(2,1)S(1)}, u32[]{:S(2)}, u32[]{:S(2)}) collective-permute-start(bf16[16,256]{1,0:T(8,128)(2,1)S(1)} %shard_map.50), channel_id=1, source_target_pairs={{0,1},{1,0},{2,3},{3,2},{4,5},{5,4},{6,7},{7,6},{8,9},{9,8},{10,11... | collective-permute-start | bytes 24584 | tf_op jit(solution)/shard_map/ppermute | solution.py:17
  44.4 1.2 %collective-permute-done.15 = bf16[16,256]{1,0:T(8,128)(2,1)S(1)} collective-permute-done((bf16[16,256]{1,0:T(8,128)(2,1)S(1)}, bf16[16,256]{1,0:T(8,128)(2,1)S(1)}, u32[]{:S(2)}, u32[]{:S(2)}) %collective-permute-start.15) | collective-permute-done | bytes 8224 | tf_op jit(solution)/shard_map/ppermute | solution.py:17
  45.6 0.6 %collective-permute-done.14 = bf16[16,256]{1,0:T(8,128)(2,1)S(1)} collective-permute-done((bf16[16,256]{1,0:T(8,128)(2,1)S(1)}, bf16[16,256]{1,0:T(8,128)(2,1)S(1)}, u32[]{:S(2)}, u32[]{:S(2)}) %collective-permute-start.14) | collective-permute-done | bytes 8224 | tf_op jit(solution)/shard_map/ppermute | solution.py:17
  46.2 2.0 %collective-permute-start.18 = (bf16[16,256]{1,0:T(8,128)(2,1)S(1)}, bf16[16,256]{1,0:T(8,128)(2,1)S(1)}, u32[]{:S(2)}, u32[]{:S(2)}) collective-permute-start(bf16[16,256]{1,0:T(8,128)(2,1)S(1)} %add_convert_fusion.refs_0_), channel_id=1, source_target_pairs={{0,12},{1,13},{2,14},{3,15},{4,8},{5,9},{6,10},{7,11},{8,4},{9,5},... | collective-permute-start | bytes 24584 | tf_op jit(solution)/shard_map/ppermute | solution.py:17
  48.2 1.1 %collective-permute-start.17 = (bf16[16,256]{1,0:T(8,128)(2,1)S(1)}, bf16[16,256]{1,0:T(8,128)(2,1)S(1)}, u32[]{:S(2)}, u32[]{:S(2)}) collective-permute-start(bf16[16,256]{1,0:T(8,128)(2,1)S(1)} %add_convert_fusion.refs_0_), channel_id=1, source_target_pairs={{0,8},{1,9},{2,10},{3,11},{4,12},{5,13},{6,14},{7,15},{8,0},{9,1},... | collective-permute-start | bytes 24584 | tf_op jit(solution)/shard_map/ppermute | solution.py:17
  49.3 1.4 %collective-permute-start.16 = (bf16[16,256]{1,0:T(8,128)(2,1)S(1)}, bf16[16,256]{1,0:T(8,128)(2,1)S(1)}, u32[]{:S(2)}, u32[]{:S(2)}) collective-permute-start(bf16[16,256]{1,0:T(8,128)(2,1)S(1)} %add_convert_fusion.refs_0_), channel_id=1, source_target_pairs={{0,4},{1,5},{2,6},{3,7},{4,0},{5,1},{6,2},{7,3},{8,12},{9,13},{10,... | collective-permute-start | bytes 24584 | tf_op jit(solution)/shard_map/ppermute | solution.py:17
  50.7 1.1 %collective-permute-done.18.refs_3_ = bf16[16,256]{1,0:T(8,128)(2,1)S(1)} collective-permute-done((bf16[16,256]{1,0:T(8,128)(2,1)S(1)}, bf16[16,256]{1,0:T(8,128)(2,1)S(1)}, u32[]{:S(2)}, u32[]{:S(2)}) %collective-permute-start.18) | collective-permute-done | bytes 8224 | tf_op jit(solution)/shard_map/ppermute | solution.py:17
  51.7 1.1 %collective-permute-done.17.refs_2_ = bf16[16,256]{1,0:T(8,128)(2,1)S(1)} collective-permute-done((bf16[16,256]{1,0:T(8,128)(2,1)S(1)}, bf16[16,256]{1,0:T(8,128)(2,1)S(1)}, u32[]{:S(2)}, u32[]{:S(2)}) %collective-permute-start.17) | collective-permute-done | bytes 8224 | tf_op jit(solution)/shard_map/ppermute | solution.py:17
  53.0 3.4 %shard_map.51 = bf16[16,512,128]{2,1,0:T(8,128)(2,1)} custom-call(s32[1]{0:T(128)} %bitcast.index_ref, bf16[16,256]{1,0:T(8,128)(2,1)S(1)} %add_convert_fusion.refs_0_, bf16[16,256]{1,0:T(8,128)(2,1)S(1)} %collective-permute-done.16.refs_1_, bf16[16,256]{1,0:T(8,128)(2,1)S(1)} %collective-permute-done.17.refs_2_, ...), custom_call_target="tpu_custom_call" | custom-call | flops 2147483648 | bytes 2097152 | tf_op jit(solution)/shard_map/pallas_call | solution.py:323
  (26 shorter events, 1.8 us)
Async XLA Ops:
  0.0 12.7 %copy-start.1 = (bf16[64,128]{1,0:T(8,128)(2,1)S(1)}, bf16[64,128]{1,0:T(8,128)(2,1)}, u32[]{:S(2)}) copy-start(bf16[64,128]{1,0:T(8,128)(2,1)} %param.5) | copy-start | bytes 49156
  0.0 12.7 %copy-start = (bf16[64,1024]{1,0:T(8,128)(2,1)S(1)}, bf16[64,1024]{1,0:T(8,128)(2,1)}, u32[]{:S(2)}) copy-start(bf16[64,1024]{1,0:T(8,128)(2,1)} %param.7) | copy-start | bytes 393220
  0.0 11.6 %collective-permute-start = (bf16[64,128]{1,0:T(8,128)(2,1)}, bf16[64,128]{1,0:T(8,128)(2,1)S(1)}, u32[]{:S(2)}, u32[]{:S(2)}) collective-permute-start(bf16[64,128]{1,0:T(8,128)(2,1)} %param.5), channel_id=1, source_target_pairs={{0,8},{1,9},{2,10},{3,11},{4,12},{5,13},{6,14},{7,15},{8,0},{9,1},... | collective-permute-start | bytes 49160 | tf_op jit(solution)/shard_map/ppermute | solution.py:17
  5.0 12.8 %collective-permute-start.7 = (bf16[64,1024]{1,0:T(8,128)(2,1)S(1)}, bf16[64,1024]{1,0:T(8,128)(2,1)S(1)}, u32[]{:S(2)}, u32[]{:S(2)}) collective-permute-start(bf16[64,1024]{1,0:T(8,128)(2,1)S(1)} %constant_dynamic-slice_fusion.7), channel_id=1, source_target_pairs={{0,14},{1,15},{2,12},{3,13},{4,10},{5,11},{6,8},{7,9},{8,6},{9,7},... | collective-permute-start | bytes 393224 | tf_op jit(solution)/shard_map/ppermute | solution.py:17
  9.1 10.7 %collective-permute-start.6 = (bf16[64,1024]{1,0:T(8,128)(2,1)S(1)}, bf16[64,1024]{1,0:T(8,128)(2,1)S(1)}, u32[]{:S(2)}, u32[]{:S(2)}) collective-permute-start(bf16[64,1024]{1,0:T(8,128)(2,1)S(1)} %get-tuple-element.53), channel_id=1, source_target_pairs={{0,12},{1,13},{2,14},{3,15},{4,8},{5,9},{6,10},{7,11},{8,4},{9,5},... | collective-permute-start | bytes 393224 | tf_op jit(solution)/shard_map/ppermute | solution.py:17
  13.5 18.1 %collective-permute-start.1 = (bf16[64,2304]{1,0:T(8,128)(2,1)}, bf16[64,2304]{1,0:T(8,128)(2,1)S(1)}, u32[]{:S(2)}, u32[]{:S(2)}) collective-permute-start(bf16[64,2304]{1,0:T(8,128)(2,1)} %get-tuple-element.60), channel_id=1, source_target_pairs={{0,2},{1,3},{2,0},{3,1},{4,6},{5,7},{6,4},{7,5},{8,10},{9,11},{10,... | collective-permute-start | bytes 884744 | tf_op jit(solution)/shard_map/ppermute | solution.py:17
  14.7 16.9 %collective-permute-start.3 = (bf16[64,1280]{1,0:T(8,128)(2,1)}, bf16[64,1280]{1,0:T(8,128)(2,1)S(1)}, u32[]{:S(2)}, u32[]{:S(2)}) collective-permute-start(bf16[64,1280]{1,0:T(8,128)(2,1)} %get-tuple-element.62), channel_id=1, source_target_pairs={{0,6},{1,7},{2,4},{3,5},{4,2},{5,3},{6,0},{7,1},{8,14},{9,15},{10,... | collective-permute-start | bytes 491528 | tf_op jit(solution)/shard_map/ppermute | solution.py:17
  15.5 16.1 %collective-permute-start.2 = (bf16[64,1280]{1,0:T(8,128)(2,1)}, bf16[64,1280]{1,0:T(8,128)(2,1)S(1)}, u32[]{:S(2)}, u32[]{:S(2)}) collective-permute-start(bf16[64,1280]{1,0:T(8,128)(2,1)} %get-tuple-element.63), channel_id=1, source_target_pairs={{0,4},{1,5},{2,6},{3,7},{4,0},{5,1},{6,2},{7,3},{8,12},{9,13},{10,... | collective-permute-start | bytes 491528 | tf_op jit(solution)/shard_map/ppermute | solution.py:17
  17.7 12.7 %collective-permute-start.5 = (bf16[64,1024]{1,0:T(8,128)(2,1)}, bf16[64,1024]{1,0:T(8,128)(2,1)S(1)}, u32[]{:S(2)}, u32[]{:S(2)}) collective-permute-start(bf16[64,1024]{1,0:T(8,128)(2,1)} %get-tuple-element.54), channel_id=1, source_target_pairs={{0,10},{1,11},{2,8},{3,9},{4,14},{5,15},{6,12},{7,13},{8,2},{9,3},... | collective-permute-start | bytes 393224 | tf_op jit(solution)/shard_map/ppermute | solution.py:17
  19.8 11.8 %collective-permute-start.4 = (bf16[64,1024]{1,0:T(8,128)(2,1)}, bf16[64,1024]{1,0:T(8,128)(2,1)S(1)}, u32[]{:S(2)}, u32[]{:S(2)}) collective-permute-start(bf16[64,1024]{1,0:T(8,128)(2,1)} %get-tuple-element.55), channel_id=1, source_target_pairs={{0,8},{1,9},{2,10},{3,11},{4,12},{5,13},{6,14},{7,15},{8,0},{9,1},... | collective-permute-start | bytes 393224 | tf_op jit(solution)/shard_map/ppermute | solution.py:17
  31.7 1.9 %collective-permute-start.8 = (bf16[64,3072]{1,0:T(8,128)(2,1)S(1)}, bf16[64,3072]{1,0:T(8,128)(2,1)S(1)}, u32[]{:S(2)}, u32[]{:S(2)}) collective-permute-start(bf16[64,3072]{1,0:T(8,128)(2,1)S(1)} %get-tuple-element.43), channel_id=1, source_target_pairs={{0,1},{1,0},{2,3},{3,2},{4,5},{5,4},{6,7},{7,6},{8,9},{9,8},{10,11... | collective-permute-start | bytes 1179656 | tf_op jit(solution)/shard_map/ppermute | solution.py:17
  31.8 2.6 %collective-permute-start.9 = (bf16[64,4096]{1,0:T(8,128)(2,1)S(1)}, bf16[64,4096]{1,0:T(8,128)(2,1)S(1)}, u32[]{:S(2)}, u32[]{:S(2)}) collective-permute-start(bf16[64,4096]{1,0:T(8,128)(2,1)S(1)} %get-tuple-element.45), channel_id=1, source_target_pairs={{0,1},{1,0},{2,3},{3,2},{4,5},{5,4},{6,7},{7,6},{8,9},{9,8},{10,11... | collective-permute-start | bytes 1572872 | tf_op jit(solution)/shard_map/ppermute | solution.py:17
  35.2 5.9 %collective-permute-start.12 = (bf16[16,1024]{1,0:T(8,128)(2,1)S(1)}, bf16[16,1024]{1,0:T(8,128)(2,1)S(1)}, u32[]{:S(2)}, u32[]{:S(2)}) collective-permute-start(bf16[16,1024]{1,0:T(8,128)(2,1)S(1)} %constant_dynamic-update-slice_fusion.refs_0_), channel_id=1, source_target_pairs={{0,12},{1,13},{2,14},{3,15},{4,8},{5,9},{6,10},{7,11},{8,4},{9,5},... | collective-permute-start | bytes 98312 | tf_op jit(solution)/shard_map/ppermute | solution.py:17
  37.2 4.8 %collective-permute-start.11 = (bf16[16,1024]{1,0:T(8,128)(2,1)S(1)}, bf16[16,1024]{1,0:T(8,128)(2,1)S(1)}, u32[]{:S(2)}, u32[]{:S(2)}) collective-permute-start(bf16[16,1024]{1,0:T(8,128)(2,1)S(1)} %constant_dynamic-update-slice_fusion.refs_0_), channel_id=1, source_target_pairs={{0,8},{1,9},{2,10},{3,11},{4,12},{5,13},{6,14},{7,15},{8,0},{9,1},... | collective-permute-start | bytes 98312 | tf_op jit(solution)/shard_map/ppermute | solution.py:17
  37.2 4.8 %collective-permute-start.10 = (bf16[16,1024]{1,0:T(8,128)(2,1)S(1)}, bf16[16,1024]{1,0:T(8,128)(2,1)S(1)}, u32[]{:S(2)}, u32[]{:S(2)}) collective-permute-start(bf16[16,1024]{1,0:T(8,128)(2,1)S(1)} %constant_dynamic-update-slice_fusion.refs_0_), channel_id=1, source_target_pairs={{0,4},{1,5},{2,6},{3,7},{4,0},{5,1},{6,2},{7,3},{8,12},{9,13},{10,... | collective-permute-start | bytes 98312 | tf_op jit(solution)/shard_map/ppermute | solution.py:17
  42.5 3.1 %collective-permute-start.15 = (bf16[16,256]{1,0:T(8,128)(2,1)S(1)}, bf16[16,256]{1,0:T(8,128)(2,1)S(1)}, u32[]{:S(2)}, u32[]{:S(2)}) collective-permute-start(bf16[16,256]{1,0:T(8,128)(2,1)S(1)} %shard_map.50), channel_id=1, source_target_pairs={{0,3},{1,2},{2,1},{3,0},{4,7},{5,6},{6,5},{7,4},{8,11},{9,10},{10,... | collective-permute-start | bytes 24584 | tf_op jit(solution)/shard_map/ppermute | solution.py:17
  42.5 3.7 %collective-permute-start.14 = (bf16[16,256]{1,0:T(8,128)(2,1)S(1)}, bf16[16,256]{1,0:T(8,128)(2,1)S(1)}, u32[]{:S(2)}, u32[]{:S(2)}) collective-permute-start(bf16[16,256]{1,0:T(8,128)(2,1)S(1)} %shard_map.50), channel_id=1, source_target_pairs={{0,2},{1,3},{2,0},{3,1},{4,6},{5,7},{6,4},{7,5},{8,10},{9,11},{10,... | collective-permute-start | bytes 24584 | tf_op jit(solution)/shard_map/ppermute | solution.py:17
  43.5 2.7 %collective-permute-start.13 = (bf16[16,256]{1,0:T(8,128)(2,1)S(1)}, bf16[16,256]{1,0:T(8,128)(2,1)S(1)}, u32[]{:S(2)}, u32[]{:S(2)}) collective-permute-start(bf16[16,256]{1,0:T(8,128)(2,1)S(1)} %shard_map.50), channel_id=1, source_target_pairs={{0,1},{1,0},{2,3},{3,2},{4,5},{5,4},{6,7},{7,6},{8,9},{9,8},{10,11... | collective-permute-start | bytes 24584 | tf_op jit(solution)/shard_map/ppermute | solution.py:17
  46.2 5.5 %collective-permute-start.18 = (bf16[16,256]{1,0:T(8,128)(2,1)S(1)}, bf16[16,256]{1,0:T(8,128)(2,1)S(1)}, u32[]{:S(2)}, u32[]{:S(2)}) collective-permute-start(bf16[16,256]{1,0:T(8,128)(2,1)S(1)} %add_convert_fusion.refs_0_), channel_id=1, source_target_pairs={{0,12},{1,13},{2,14},{3,15},{4,8},{5,9},{6,10},{7,11},{8,4},{9,5},... | collective-permute-start | bytes 24584 | tf_op jit(solution)/shard_map/ppermute | solution.py:17
  48.2 4.6 %collective-permute-start.17 = (bf16[16,256]{1,0:T(8,128)(2,1)S(1)}, bf16[16,256]{1,0:T(8,128)(2,1)S(1)}, u32[]{:S(2)}, u32[]{:S(2)}) collective-permute-start(bf16[16,256]{1,0:T(8,128)(2,1)S(1)} %add_convert_fusion.refs_0_), channel_id=1, source_target_pairs={{0,8},{1,9},{2,10},{3,11},{4,12},{5,13},{6,14},{7,15},{8,0},{9,1},... | collective-permute-start | bytes 24584 | tf_op jit(solution)/shard_map/ppermute | solution.py:17
  49.3 3.7 %collective-permute-start.16 = (bf16[16,256]{1,0:T(8,128)(2,1)S(1)}, bf16[16,256]{1,0:T(8,128)(2,1)S(1)}, u32[]{:S(2)}, u32[]{:S(2)}) collective-permute-start(bf16[16,256]{1,0:T(8,128)(2,1)S(1)} %add_convert_fusion.refs_0_), channel_id=1, source_target_pairs={{0,4},{1,5},{2,6},{3,7},{4,0},{5,1},{6,2},{7,3},{8,12},{9,13},{10,... | collective-permute-start | bytes 24584 | tf_op jit(solution)/shard_map/ppermute | solution.py:17

commit v7 on v6

--- a/solution.py
+++ b/solution.py
@@ -354,7 +354,7 @@
         return lax.dynamic_slice_in_dim(x, (index // 2 ^ k) * 2 * width, 2 * width, 1)
 
     lead = columns(conduction_orb, chips - 1)
-    lead, conduction_orb = lax.optimization_barrier((lead, conduction_orb))
+    lead, conduction_orb, valence_orb = lax.optimization_barrier((lead, conduction_orb, valence_orb))
     far = [columns(conduction_orb, k) for k in range(half, chips - 1)] + [lead]
     far = [swap(far[k - half], 2 * k, size) for k in range(half, chips)]
     crossed = swap(valence_orb, 2 * half, size)

time: 56.6 us -> 56.8 us (level)
  transfers between devices with their start and end apart: 19 -> 19, of which waited for: 9 -> 8; matrix products, arithmetic and copies ran while one was open for 14% -> 13% of each run, Pallas kernels for 4% -> 4%
where the time goes in v7:
time: 56.8 us; the launch traced here: 56.5 us
  starting transfers between devices  26.8 us (47%)
  waiting for transfers between devices  14.6 us (26%)
  Pallas kernels  6.77 us (12%)
  local copies, waits for them, and re-layouts  6.71 us (12%)
  other arithmetic  1.52 us (3%)
    ppermute x19, starting transfers between devices, swap(): return lax.ppermute(x, AXIS, [(i, i ^ bits) for i in range(size)])  26.8 us
    ppermute x19, waiting for transfers between devices, swap(): return lax.ppermute(x, AXIS, [(i, i ^ bits) for i in range(size)])  14.6 us
    dynamic_slice x3, local copies, waits for them, and re-layouts, columns(): lax.dynamic_slice_in_dim(x, (index // 2 ^ k) * 2 * width, 2 * width, 1)  3.84 us
    pallas_call x1, Pallas kernels, project(): pl.pallas_call(functools.partial(project_kernel, layers=len(fields), part...  3.42 us
    unnamed x7, local copies, waits for them, and re-layouts  2.87 us
    pallas_call x3, Pallas kernels, density_part(): pl.pallas_call(functools.partial(density_part_kernel, straight=straight),...  2.82 us
    concatenate x2, other arithmetic, body_slabs(): close.append(jnp.concatenate(parts, axis=1))  1.51 us
  transfers between devices with their start and end apart: 19, of which 8 were waited for; matrix products, arithmetic and copies ran while one was open for 13% of the time, Pallas kernels for 4%

profile of v7, /device:TPU:0, one launch (start us, length us, event | category | flops | bytes accessed | tf_op | source)
XLA Modules:
  0.0 56.5 jit_solution(9319298273897922468)
XLA Ops:
  0.0 0.9 %constant_dynamic-slice_fusion.7 = bf16[64,1024]{1,0:T(8,128)(2,1)S(1)} fusion(bf16[64,8192]{1,0:T(8,128)(2,1)} %param.6, s32[]{:T(128)S(6)} %select_n.37), kind=kLoop, calls=%fused_computation.21 | loop fusion | bytes 262148 | tf_op jit(solution)/shard_map/dynamic_slice | solution.py:354
  1.0 4.1 %collective-permute-start = (bf16[64,128]{1,0:T(8,128)(2,1)}, bf16[64,128]{1,0:T(8,128)(2,1)S(1)}, u32[]{:S(2)}, u32[]{:S(2)}) collective-permute-start(bf16[64,128]{1,0:T(8,128)(2,1)} %param.5), channel_id=1, source_target_pairs={{0,8},{1,9},{2,10},{3,11},{4,12},{5,13},{6,14},{7,15},{8,0},{9,1},... | collective-permute-start | bytes 49160 | tf_op jit(solution)/shard_map/ppermute | solution.py:17
  5.1 2.3 %collective-permute-start.7 = (bf16[64,1024]{1,0:T(8,128)(2,1)S(1)}, bf16[64,1024]{1,0:T(8,128)(2,1)S(1)}, u32[]{:S(2)}, u32[]{:S(2)}) collective-permute-start(bf16[64,1024]{1,0:T(8,128)(2,1)S(1)} %constant_dynamic-slice_fusion.7), channel_id=1, source_target_pairs={{0,14},{1,15},{2,12},{3,13},{4,10},{5,11},{6,8},{7,9},{8,6},{9,7},... | collective-permute-start | bytes 393224 | tf_op jit(solution)/shard_map/ppermute | solution.py:17
  7.4 1.8 %constant_dynamic-slice_fusion = (bf16[64,1024]{1,0:T(8,128)(2,1)S(1)}, bf16[64,1024]{1,0:T(8,128)(2,1)}, bf16[64,1024]{1,0:T(8,128)(2,1)}) fusion(bf16[64,8192]{1,0:T(8,128)(2,1)} %param.6, s32[]{:T(128)S(6)} %select_n.44, s32[]{:T(128)S(6)} %select_n.43, s32[]{:T(128)S(6)} %select_n.42), kind=kLoop, calls=%fused_computation.14 | loop fusion | bytes 786444 | tf_op jit(solution)/shard_map/dynamic_slice | solution.py:354
  9.1 2.5 %collective-permute-start.6 = (bf16[64,1024]{1,0:T(8,128)(2,1)S(1)}, bf16[64,1024]{1,0:T(8,128)(2,1)S(1)}, u32[]{:S(2)}, u32[]{:S(2)}) collective-permute-start(bf16[64,1024]{1,0:T(8,128)(2,1)S(1)} %get-tuple-element.55), channel_id=1, source_target_pairs={{0,12},{1,13},{2,14},{3,15},{4,8},{5,9},{6,10},{7,11},{8,4},{9,5},... | collective-permute-start | bytes 393224 | tf_op jit(solution)/shard_map/ppermute | solution.py:17
  11.6 1.1 %constant_dynamic-slice_fusion.3 = (bf16[64,1024]{1,0:T(8,128)(2,1)S(1)}, bf16[64,1024]{1,0:T(8,128)(2,1)S(1)}, bf16[64,1024]{1,0:T(8,128)(2,1)S(1)}, bf16[64,1024]{1,0:T(8,128)(2,1)S(1)}) fusion(bf16[64,8192]{1,0:T(8,128)(2,1)} %param.6, s32[]{:T(128)S(6)} %select_n.41, s32[]{:T(128)S(6)} %select_n.40, s32[]{:T(128)S(6)} %select_n.39, s32[]{:T(128)S(6)} %select_n.38), kind=kLoop, calls=%fused_computation.17 | loop fusion | bytes 1048592 | tf_op jit(solution)/shard_map/dynamic_slice | solution.py:354
  12.8 0.8 %pad_maximum_fusion.4 = (bf16[64,2304]{1,0:T(8,128)(2,1)}, bf16[64,2304]{1,0:T(8,128)(2,1)S(1)}) fusion(bf16[64,1024]{1,0:T(8,128)(2,1)S(1)} %copy-done, bf16[64,128]{1,0:T(8,128)(2,1)S(1)} %collective-permute-done, bf16[64,128]{1,0:T(8,128)(2,1)S(1)} %copy-done.1, bf16[64,1024]{1,0:T(8,128)(2,1)S(1)} %get-tuple-element.60, ...), kind=kLoop, calls=%fused_computation.4 | loop fusion | flops 1916928 | bytes 1015808 | tf_op jit(solution)/shard_map/concatenate | solution.py:365
  14.0 0.8 %pad_maximum_fusion.6 = (bf16[64,1280]{1,0:T(8,128)(2,1)}, bf16[64,1280]{1,0:T(8,128)(2,1)}) fusion(bf16[64,128]{1,0:T(8,128)(2,1)S(1)} %collective-permute-done, bf16[64,128]{1,0:T(8,128)(2,1)S(1)} %copy-done.1, bf16[64,1024]{1,0:T(8,128)(2,1)S(1)} %get-tuple-element.58, bf16[64,1024]{1,0:T(8,128)(2,1)S(1)} %get-tuple-element.59), kind=kLoop, calls=%fused_computation.6 | loop fusion | flops 819200 | bytes 622592 | tf_op jit(solution)/shard_map/concatenate | solution.py:365
  14.8 0.7 %collective-permute-start.3 = (bf16[64,1280]{1,0:T(8,128)(2,1)}, bf16[64,1280]{1,0:T(8,128)(2,1)S(1)}, u32[]{:S(2)}, u32[]{:S(2)}) collective-permute-start(bf16[64,1280]{1,0:T(8,128)(2,1)} %get-tuple-element.64), channel_id=1, source_target_pairs={{0,6},{1,7},{2,4},{3,5},{4,2},{5,3},{6,0},{7,1},{8,14},{9,15},{10,... | collective-permute-start | bytes 491528 | tf_op jit(solution)/shard_map/ppermute | solution.py:17
  15.5 2.2 %collective-permute-start.2 = (bf16[64,1280]{1,0:T(8,128)(2,1)}, bf16[64,1280]{1,0:T(8,128)(2,1)S(1)}, u32[]{:S(2)}, u32[]{:S(2)}) collective-permute-start(bf16[64,1280]{1,0:T(8,128)(2,1)} %get-tuple-element.65), channel_id=1, source_target_pairs={{0,4},{1,5},{2,6},{3,7},{4,0},{5,1},{6,2},{7,3},{8,12},{9,13},{10,... | collective-permute-start | bytes 491528 | tf_op jit(solution)/shard_map/ppermute | solution.py:17
  17.8 2.4 %collective-permute-start.5 = (bf16[64,1024]{1,0:T(8,128)(2,1)}, bf16[64,1024]{1,0:T(8,128)(2,1)S(1)}, u32[]{:S(2)}, u32[]{:S(2)}) collective-permute-start(bf16[64,1024]{1,0:T(8,128)(2,1)} %get-tuple-element.56), channel_id=1, source_target_pairs={{0,10},{1,11},{2,8},{3,9},{4,14},{5,15},{6,12},{7,13},{8,2},{9,3},... | collective-permute-start | bytes 393224 | tf_op jit(solution)/shard_map/ppermute | solution.py:17
  20.2 0.6 %collective-permute-start.4 = (bf16[64,1024]{1,0:T(8,128)(2,1)}, bf16[64,1024]{1,0:T(8,128)(2,1)S(1)}, u32[]{:S(2)}, u32[]{:S(2)}) collective-permute-start(bf16[64,1024]{1,0:T(8,128)(2,1)} %get-tuple-element.57), channel_id=1, source_target_pairs={{0,8},{1,9},{2,10},{3,11},{4,12},{5,13},{6,14},{7,15},{8,0},{9,1},... | collective-permute-start | bytes 393224 | tf_op jit(solution)/shard_map/ppermute | solution.py:17
  20.8 2.9 %copy.5 = bf16[16,512,128]{1,2,0:T(8,128)(2,1)S(1)} copy(bf16[16,512,128]{2,1,0:T(8,128)(2,1)} %param.4) | data formatting | bytes 4194304 | tf_op args[0]
  23.7 7.4 %collective-permute-done.5.refs_6_.refs_5_ = bf16[64,1024]{1,0:T(8,128)(2,1)S(1)} collective-permute-done((bf16[64,1024]{1,0:T(8,128)(2,1)}, bf16[64,1024]{1,0:T(8,128)(2,1)S(1)}, u32[]{:S(2)}, u32[]{:S(2)}) %collective-permute-start.5) | collective-permute-done | bytes 131104 | tf_op jit(solution)/shard_map/ppermute | solution.py:17
  31.1 0.6 %collective-permute-done.4.refs_5_.refs_4_ = bf16[64,1024]{1,0:T(8,128)(2,1)S(1)} collective-permute-done((bf16[64,1024]{1,0:T(8,128)(2,1)}, bf16[64,1024]{1,0:T(8,128)(2,1)S(1)}, u32[]{:S(2)}, u32[]{:S(2)}) %collective-permute-start.4) | collective-permute-done | bytes 131104 | tf_op jit(solution)/shard_map/ppermute | solution.py:17
  32.3 1.3 %shard_map.46 = (bf16[16,512]{1,0:T(8,128)(2,1)S(1)}, bf16[512,512]{1,0:T(8,128)(2,1)S(1)}, bf16[128,512]{1,0:T(8,128)(2,1)S(1)}) custom-call(s32[1]{0:T(128)} %bitcast.index_ref, bf16[16,128,512]{2,1,0:T(8,128)(2,1)S(1)} %bitcast.2, bf16[64,2304]{1,0:T(8,128)(2,1)S(1)} %get-tuple-element.36.refs_1_.refs_0_.refs_4_, ...), custom_call_target="tpu_custom_call" | custom-call | flops 1073741824 | bytes 2097152 | tf_op jit(solution)/shard_map/pallas_call | solution.py:215
  33.7 0.8 %shard_map.48 = (bf16[16,256]{1,0:T(8,128)(2,1)S(1)}, bf16[256,512]{1,0:T(8,128)(2,1)S(1)}, bf16[128,256]{1,0:T(8,128)(2,1)S(1)}) custom-call(s32[1]{0:T(128)} %bitcast.index_ref, bf16[16,128,512]{2,1,0:T(8,128)(2,1)S(1)} %bitcast.3, bf16[64,3072]{1,0:T(8,128)(2,1)S(1)} %collective-permute-done.8.refs_1_), custom_call_target="tpu_custom_call" | custom-call | flops 536870912 | bytes 2097152 | tf_op jit(solution)/shard_map/pallas_call | solution.py:215
  34.4 0.7 %shard_map.49 = (bf16[16,256]{1,0:T(8,128)(2,1)S(1)}, bf16[256,512]{1,0:T(8,128)(2,1)S(1)}, bf16[128,256]{1,0:T(8,128)(2,1)S(1)}) custom-call(s32[1]{0:T(128)} %bitcast.index_ref, bf16[16,128,512]{2,1,0:T(8,128)(2,1)S(1)} %bitcast.4, bf16[64,3072]{1,0:T(8,128)(2,1)S(1)} %collective-permute-done.8.refs_1_, ...), custom_call_target="tpu_custom_call" | custom-call | flops 536870912 | bytes 2097152 | tf_op jit(solution)/shard_map/pallas_call | solution.py:215
  35.2 2.3 %collective-permute-start.12 = (bf16[16,1024]{1,0:T(8,128)(2,1)S(1)}, bf16[16,1024]{1,0:T(8,128)(2,1)S(1)}, u32[]{:S(2)}, u32[]{:S(2)}) collective-permute-start(bf16[16,1024]{1,0:T(8,128)(2,1)S(1)} %constant_dynamic-update-slice_fusion.refs_0_), channel_id=1, source_target_pairs={{0,12},{1,13},{2,14},{3,15},{4,8},{5,9},{6,10},{7,11},{8,4},{9,5},... | collective-permute-start | bytes 98312 | tf_op jit(solution)/shard_map/ppermute | solution.py:17
  37.5 2.2 %collective-permute-start.10 = (bf16[16,1024]{1,0:T(8,128)(2,1)S(1)}, bf16[16,1024]{1,0:T(8,128)(2,1)S(1)}, u32[]{:S(2)}, u32[]{:S(2)}) collective-permute-start(bf16[16,1024]{1,0:T(8,128)(2,1)S(1)} %constant_dynamic-update-slice_fusion.refs_0_), channel_id=1, source_target_pairs={{0,4},{1,5},{2,6},{3,7},{4,0},{5,1},{6,2},{7,3},{8,12},{9,13},{10,... | collective-permute-start | bytes 98312 | tf_op jit(solution)/shard_map/ppermute | solution.py:17
  39.7 1.3 %collective-permute-done.12.refs_3_ = bf16[16,1024]{1,0:T(8,128)(2,1)S(1)} collective-permute-done((bf16[16,1024]{1,0:T(8,128)(2,1)S(1)}, bf16[16,1024]{1,0:T(8,128)(2,1)S(1)}, u32[]{:S(2)}, u32[]{:S(2)}) %collective-permute-start.12) | collective-permute-done | bytes 32800 | tf_op jit(solution)/shard_map/ppermute | solution.py:17
  41.0 1.3 %collective-permute-done.11.refs_2_ = bf16[16,1024]{1,0:T(8,128)(2,1)S(1)} collective-permute-done((bf16[16,1024]{1,0:T(8,128)(2,1)S(1)}, bf16[16,1024]{1,0:T(8,128)(2,1)S(1)}, u32[]{:S(2)}, u32[]{:S(2)}) %collective-permute-start.11) | collective-permute-done | bytes 32800 | tf_op jit(solution)/shard_map/ppermute | solution.py:17
  43.1 0.8 %collective-permute-start.14 = (bf16[16,256]{1,0:T(8,128)(2,1)S(1)}, bf16[16,256]{1,0:T(8,128)(2,1)S(1)}, u32[]{:S(2)}, u32[]{:S(2)}) collective-permute-start(bf16[16,256]{1,0:T(8,128)(2,1)S(1)} %shard_map.50), channel_id=1, source_target_pairs={{0,2},{1,3},{2,0},{3,1},{4,6},{5,7},{6,4},{7,5},{8,10},{9,11},{10,... | collective-permute-start | bytes 24584 | tf_op jit(solution)/shard_map/ppermute | solution.py:17
  44.0 0.7 %collective-permute-start.13 = (bf16[16,256]{1,0:T(8,128)(2,1)S(1)}, bf16[16,256]{1,0:T(8,128)(2,1)S(1)}, u32[]{:S(2)}, u32[]{:S(2)}) collective-permute-start(bf16[16,256]{1,0:T(8,128)(2,1)S(1)} %shard_map.50), channel_id=1, source_target_pairs={{0,1},{1,0},{2,3},{3,2},{4,5},{5,4},{6,7},{7,6},{8,9},{9,8},{10,11... | collective-permute-start | bytes 24584 | tf_op jit(solution)/shard_map/ppermute | solution.py:17
  44.7 1.2 %collective-permute-done.15 = bf16[16,256]{1,0:T(8,128)(2,1)S(1)} collective-permute-done((bf16[16,256]{1,0:T(8,128)(2,1)S(1)}, bf16[16,256]{1,0:T(8,128)(2,1)S(1)}, u32[]{:S(2)}, u32[]{:S(2)}) %collective-permute-start.15) | collective-permute-done | bytes 8224 | tf_op jit(solution)/shard_map/ppermute | solution.py:17
  45.9 0.9 %collective-permute-done.14 = bf16[16,256]{1,0:T(8,128)(2,1)S(1)} collective-permute-done((bf16[16,256]{1,0:T(8,128)(2,1)S(1)}, bf16[16,256]{1,0:T(8,128)(2,1)S(1)}, u32[]{:S(2)}, u32[]{:S(2)}) %collective-permute-start.14) | collective-permute-done | bytes 8224 | tf_op jit(solution)/shard_map/ppermute | solution.py:17
  46.8 1.7 %collective-permute-start.18 = (bf16[16,256]{1,0:T(8,128)(2,1)S(1)}, bf16[16,256]{1,0:T(8,128)(2,1)S(1)}, u32[]{:S(2)}, u32[]{:S(2)}) collective-permute-start(bf16[16,256]{1,0:T(8,128)(2,1)S(1)} %add_convert_fusion.refs_0_), channel_id=1, source_target_pairs={{0,12},{1,13},{2,14},{3,15},{4,8},{5,9},{6,10},{7,11},{8,4},{9,5},... | collective-permute-start | bytes 24584 | tf_op jit(solution)/shard_map/ppermute | solution.py:17
  48.6 0.7 %collective-permute-start.17 = (bf16[16,256]{1,0:T(8,128)(2,1)S(1)}, bf16[16,256]{1,0:T(8,128)(2,1)S(1)}, u32[]{:S(2)}, u32[]{:S(2)}) collective-permute-start(bf16[16,256]{1,0:T(8,128)(2,1)S(1)} %add_convert_fusion.refs_0_), channel_id=1, source_target_pairs={{0,8},{1,9},{2,10},{3,11},{4,12},{5,13},{6,14},{7,15},{8,0},{9,1},... | collective-permute-start | bytes 24584 | tf_op jit(solution)/shard_map/ppermute | solution.py:17
  49.3 2.0 %collective-permute-start.16 = (bf16[16,256]{1,0:T(8,128)(2,1)S(1)}, bf16[16,256]{1,0:T(8,128)(2,1)S(1)}, u32[]{:S(2)}, u32[]{:S(2)}) collective-permute-start(bf16[16,256]{1,0:T(8,128)(2,1)S(1)} %add_convert_fusion.refs_0_), channel_id=1, source_target_pairs={{0,4},{1,5},{2,6},{3,7},{4,0},{5,1},{6,2},{7,3},{8,12},{9,13},{10,... | collective-permute-start | bytes 24584 | tf_op jit(solution)/shard_map/ppermute | solution.py:17
  51.3 1.1 %collective-permute-done.18.refs_3_ = bf16[16,256]{1,0:T(8,128)(2,1)S(1)} collective-permute-done((bf16[16,256]{1,0:T(8,128)(2,1)S(1)}, bf16[16,256]{1,0:T(8,128)(2,1)S(1)}, u32[]{:S(2)}, u32[]{:S(2)}) %collective-permute-start.18) | collective-permute-done | bytes 8224 | tf_op jit(solution)/shard_map/ppermute | solution.py:17
  52.3 0.8 %collective-permute-done.17.refs_2_ = bf16[16,256]{1,0:T(8,128)(2,1)S(1)} collective-permute-done((bf16[16,256]{1,0:T(8,128)(2,1)S(1)}, bf16[16,256]{1,0:T(8,128)(2,1)S(1)}, u32[]{:S(2)}, u32[]{:S(2)}) %collective-permute-start.17) | collective-permute-done | bytes 8224 | tf_op jit(solution)/shard_map/ppermute | solution.py:17
  53.1 3.4 %shard_map.51 = bf16[16,512,128]{2,1,0:T(8,128)(2,1)} custom-call(s32[1]{0:T(128)} %bitcast.index_ref, bf16[16,256]{1,0:T(8,128)(2,1)S(1)} %add_convert_fusion.refs_0_, bf16[16,256]{1,0:T(8,128)(2,1)S(1)} %collective-permute-done.16.refs_1_, bf16[16,256]{1,0:T(8,128)(2,1)S(1)} %collective-permute-done.17.refs_2_, ...), custom_call_target="tpu_custom_call" | custom-call | flops 2147483648 | bytes 2097152 | tf_op jit(solution)/shard_map/pallas_call | solution.py:323
  (26 shorter events, 2.0 us)
Async XLA Ops:
  0.0 12.7 %copy-start.1 = (bf16[64,128]{1,0:T(8,128)(2,1)S(1)}, bf16[64,128]{1,0:T(8,128)(2,1)}, u32[]{:S(2)}) copy-start(bf16[64,128]{1,0:T(8,128)(2,1)} %param.5) | copy-start | bytes 49156
  0.0 12.7 %copy-start = (bf16[64,1024]{1,0:T(8,128)(2,1)S(1)}, bf16[64,1024]{1,0:T(8,128)(2,1)}, u32[]{:S(2)}) copy-start(bf16[64,1024]{1,0:T(8,128)(2,1)} %param.7) | copy-start | bytes 393220
  1.0 10.6 %collective-permute-start = (bf16[64,128]{1,0:T(8,128)(2,1)}, bf16[64,128]{1,0:T(8,128)(2,1)S(1)}, u32[]{:S(2)}, u32[]{:S(2)}) collective-permute-start(bf16[64,128]{1,0:T(8,128)(2,1)} %param.5), channel_id=1, source_target_pairs={{0,8},{1,9},{2,10},{3,11},{4,12},{5,13},{6,14},{7,15},{8,0},{9,1},... | collective-permute-start | bytes 49160 | tf_op jit(solution)/shard_map/ppermute | solution.py:17
  5.1 12.7 %collective-permute-start.7 = (bf16[64,1024]{1,0:T(8,128)(2,1)S(1)}, bf16[64,1024]{1,0:T(8,128)(2,1)S(1)}, u32[]{:S(2)}, u32[]{:S(2)}) collective-permute-start(bf16[64,1024]{1,0:T(8,128)(2,1)S(1)} %constant_dynamic-slice_fusion.7), channel_id=1, source_target_pairs={{0,14},{1,15},{2,12},{3,13},{4,10},{5,11},{6,8},{7,9},{8,6},{9,7},... | collective-permute-start | bytes 393224 | tf_op jit(solution)/shard_map/ppermute | solution.py:17
  9.1 11.1 %collective-permute-start.6 = (bf16[64,1024]{1,0:T(8,128)(2,1)S(1)}, bf16[64,1024]{1,0:T(8,128)(2,1)S(1)}, u32[]{:S(2)}, u32[]{:S(2)}) collective-permute-start(bf16[64,1024]{1,0:T(8,128)(2,1)S(1)} %get-tuple-element.55), channel_id=1, source_target_pairs={{0,12},{1,13},{2,14},{3,15},{4,8},{5,9},{6,10},{7,11},{8,4},{9,5},... | collective-permute-start | bytes 393224 | tf_op jit(solution)/shard_map/ppermute | solution.py:17
  13.5 18.1 %collective-permute-start.1 = (bf16[64,2304]{1,0:T(8,128)(2,1)}, bf16[64,2304]{1,0:T(8,128)(2,1)S(1)}, u32[]{:S(2)}, u32[]{:S(2)}) collective-permute-start(bf16[64,2304]{1,0:T(8,128)(2,1)} %get-tuple-element.62), channel_id=1, source_target_pairs={{0,2},{1,3},{2,0},{3,1},{4,6},{5,7},{6,4},{7,5},{8,10},{9,11},{10,... | collective-permute-start | bytes 884744 | tf_op jit(solution)/shard_map/ppermute | solution.py:17
  14.8 16.9 %collective-permute-start.3 = (bf16[64,1280]{1,0:T(8,128)(2,1)}, bf16[64,1280]{1,0:T(8,128)(2,1)S(1)}, u32[]{:S(2)}, u32[]{:S(2)}) collective-permute-start(bf16[64,1280]{1,0:T(8,128)(2,1)} %get-tuple-element.64), channel_id=1, source_target_pairs={{0,6},{1,7},{2,4},{3,5},{4,2},{5,3},{6,0},{7,1},{8,14},{9,15},{10,... | collective-permute-start | bytes 491528 | tf_op jit(solution)/shard_map/ppermute | solution.py:17
  15.5 16.1 %collective-permute-start.2 = (bf16[64,1280]{1,0:T(8,128)(2,1)}, bf16[64,1280]{1,0:T(8,128)(2,1)S(1)}, u32[]{:S(2)}, u32[]{:S(2)}) collective-permute-start(bf16[64,1280]{1,0:T(8,128)(2,1)} %get-tuple-element.65), channel_id=1, source_target_pairs={{0,4},{1,5},{2,6},{3,7},{4,0},{5,1},{6,2},{7,3},{8,12},{9,13},{10,... | collective-permute-start | bytes 491528 | tf_op jit(solution)/shard_map/ppermute | solution.py:17
  17.8 13.3 %collective-permute-start.5 = (bf16[64,1024]{1,0:T(8,128)(2,1)}, bf16[64,1024]{1,0:T(8,128)(2,1)S(1)}, u32[]{:S(2)}, u32[]{:S(2)}) collective-permute-start(bf16[64,1024]{1,0:T(8,128)(2,1)} %get-tuple-element.56), channel_id=1, source_target_pairs={{0,10},{1,11},{2,8},{3,9},{4,14},{5,15},{6,12},{7,13},{8,2},{9,3},... | collective-permute-start | bytes 393224 | tf_op jit(solution)/shard_map/ppermute | solution.py:17
  20.2 11.5 %collective-permute-start.4 = (bf16[64,1024]{1,0:T(8,128)(2,1)}, bf16[64,1024]{1,0:T(8,128)(2,1)S(1)}, u32[]{:S(2)}, u32[]{:S(2)}) collective-permute-start(bf16[64,1024]{1,0:T(8,128)(2,1)} %get-tuple-element.57), channel_id=1, source_target_pairs={{0,8},{1,9},{2,10},{3,11},{4,12},{5,13},{6,14},{7,15},{8,0},{9,1},... | collective-permute-start | bytes 393224 | tf_op jit(solution)/shard_map/ppermute | solution.py:17
  31.7 1.9 %collective-permute-start.8 = (bf16[64,3072]{1,0:T(8,128)(2,1)S(1)}, bf16[64,3072]{1,0:T(8,128)(2,1)S(1)}, u32[]{:S(2)}, u32[]{:S(2)}) collective-permute-start(bf16[64,3072]{1,0:T(8,128)(2,1)S(1)} %get-tuple-element.45), channel_id=1, source_target_pairs={{0,1},{1,0},{2,3},{3,2},{4,5},{5,4},{6,7},{7,6},{8,9},{9,8},{10,11... | collective-permute-start | bytes 1179656 | tf_op jit(solution)/shard_map/ppermute | solution.py:17
  31.8 2.6 %collective-permute-start.9 = (bf16[64,4096]{1,0:T(8,128)(2,1)S(1)}, bf16[64,4096]{1,0:T(8,128)(2,1)S(1)}, u32[]{:S(2)}, u32[]{:S(2)}) collective-permute-start(bf16[64,4096]{1,0:T(8,128)(2,1)S(1)} %get-tuple-element.47), channel_id=1, source_target_pairs={{0,1},{1,0},{2,3},{3,2},{4,5},{5,4},{6,7},{7,6},{8,9},{9,8},{10,11... | collective-permute-start | bytes 1572872 | tf_op jit(solution)/shard_map/ppermute | solution.py:17
  35.2 5.8 %collective-permute-start.12 = (bf16[16,1024]{1,0:T(8,128)(2,1)S(1)}, bf16[16,1024]{1,0:T(8,128)(2,1)S(1)}, u32[]{:S(2)}, u32[]{:S(2)}) collective-permute-start(bf16[16,1024]{1,0:T(8,128)(2,1)S(1)} %constant_dynamic-update-slice_fusion.refs_0_), channel_id=1, source_target_pairs={{0,12},{1,13},{2,14},{3,15},{4,8},{5,9},{6,10},{7,11},{8,4},{9,5},... | collective-permute-start | bytes 98312 | tf_op jit(solution)/shard_map/ppermute | solution.py:17
  37.5 4.8 %collective-permute-start.11 = (bf16[16,1024]{1,0:T(8,128)(2,1)S(1)}, bf16[16,1024]{1,0:T(8,128)(2,1)S(1)}, u32[]{:S(2)}, u32[]{:S(2)}) collective-permute-start(bf16[16,1024]{1,0:T(8,128)(2,1)S(1)} %constant_dynamic-update-slice_fusion.refs_0_), channel_id=1, source_target_pairs={{0,8},{1,9},{2,10},{3,11},{4,12},{5,13},{6,14},{7,15},{8,0},{9,1},... | collective-permute-start | bytes 98312 | tf_op jit(solution)/shard_map/ppermute | solution.py:17
  37.5 4.8 %collective-permute-start.10 = (bf16[16,1024]{1,0:T(8,128)(2,1)S(1)}, bf16[16,1024]{1,0:T(8,128)(2,1)S(1)}, u32[]{:S(2)}, u32[]{:S(2)}) collective-permute-start(bf16[16,1024]{1,0:T(8,128)(2,1)S(1)} %constant_dynamic-update-slice_fusion.refs_0_), channel_id=1, source_target_pairs={{0,4},{1,5},{2,6},{3,7},{4,0},{5,1},{6,2},{7,3},{8,12},{9,13},{10,... | collective-permute-start | bytes 98312 | tf_op jit(solution)/shard_map/ppermute | solution.py:17
  42.8 3.1 %collective-permute-start.15 = (bf16[16,256]{1,0:T(8,128)(2,1)S(1)}, bf16[16,256]{1,0:T(8,128)(2,1)S(1)}, u32[]{:S(2)}, u32[]{:S(2)}) collective-permute-start(bf16[16,256]{1,0:T(8,128)(2,1)S(1)} %shard_map.50), channel_id=1, source_target_pairs={{0,3},{1,2},{2,1},{3,0},{4,7},{5,6},{6,5},{7,4},{8,11},{9,10},{10,... | collective-permute-start | bytes 24584 | tf_op jit(solution)/shard_map/ppermute | solution.py:17
  43.1 3.7 %collective-permute-start.14 = (bf16[16,256]{1,0:T(8,128)(2,1)S(1)}, bf16[16,256]{1,0:T(8,128)(2,1)S(1)}, u32[]{:S(2)}, u32[]{:S(2)}) collective-permute-start(bf16[16,256]{1,0:T(8,128)(2,1)S(1)} %shard_map.50), channel_id=1, source_target_pairs={{0,2},{1,3},{2,0},{3,1},{4,6},{5,7},{6,4},{7,5},{8,10},{9,11},{10,... | collective-permute-start | bytes 24584 | tf_op jit(solution)/shard_map/ppermute | solution.py:17
  44.0 2.9 %collective-permute-start.13 = (bf16[16,256]{1,0:T(8,128)(2,1)S(1)}, bf16[16,256]{1,0:T(8,128)(2,1)S(1)}, u32[]{:S(2)}, u32[]{:S(2)}) collective-permute-start(bf16[16,256]{1,0:T(8,128)(2,1)S(1)} %shard_map.50), channel_id=1, source_target_pairs={{0,1},{1,0},{2,3},{3,2},{4,5},{5,4},{6,7},{7,6},{8,9},{9,8},{10,11... | collective-permute-start | bytes 24584 | tf_op jit(solution)/shard_map/ppermute | solution.py:17
  46.8 5.5 %collective-permute-start.18 = (bf16[16,256]{1,0:T(8,128)(2,1)S(1)}, bf16[16,256]{1,0:T(8,128)(2,1)S(1)}, u32[]{:S(2)}, u32[]{:S(2)}) collective-permute-start(bf16[16,256]{1,0:T(8,128)(2,1)S(1)} %add_convert_fusion.refs_0_), channel_id=1, source_target_pairs={{0,12},{1,13},{2,14},{3,15},{4,8},{5,9},{6,10},{7,11},{8,4},{9,5},... | collective-permute-start | bytes 24584 | tf_op jit(solution)/shard_map/ppermute | solution.py:17
  48.6 4.5 %collective-permute-start.17 = (bf16[16,256]{1,0:T(8,128)(2,1)S(1)}, bf16[16,256]{1,0:T(8,128)(2,1)S(1)}, u32[]{:S(2)}, u32[]{:S(2)}) collective-permute-start(bf16[16,256]{1,0:T(8,128)(2,1)S(1)} %add_convert_fusion.refs_0_), channel_id=1, source_target_pairs={{0,8},{1,9},{2,10},{3,11},{4,12},{5,13},{6,14},{7,15},{8,0},{9,1},... | collective-permute-start | bytes 24584 | tf_op jit(solution)/shard_map/ppermute | solution.py:17
  49.3 3.8 %collective-permute-start.16 = (bf16[16,256]{1,0:T(8,128)(2,1)S(1)}, bf16[16,256]{1,0:T(8,128)(2,1)S(1)}, u32[]{:S(2)}, u32[]{:S(2)}) collective-permute-start(bf16[16,256]{1,0:T(8,128)(2,1)S(1)} %add_convert_fusion.refs_0_), channel_id=1, source_target_pairs={{0,4},{1,5},{2,6},{3,7},{4,0},{5,1},{6,2},{7,3},{8,12},{9,13},{10,... | collective-permute-start | bytes 24584 | tf_op jit(solution)/shard_map/ppermute | solution.py:17

commit v8 on v7

--- a/solution.py
+++ b/solution.py
@@ -354,7 +354,6 @@
         return lax.dynamic_slice_in_dim(x, (index // 2 ^ k) * 2 * width, 2 * width, 1)
 
     lead = columns(conduction_orb, chips - 1)
-    lead, conduction_orb, valence_orb = lax.optimization_barrier((lead, conduction_orb, valence_orb))
     far = [columns(conduction_orb, k) for k in range(half, chips - 1)] + [lead]
     far = [swap(far[k - half], 2 * k, size) for k in range(half, chips)]
     crossed = swap(valence_orb, 2 * half, size)

time: 56.8 us -> 56.4 us (level)
  starting transfers between devices: 26.8 us -> 28.1 us
  waiting for transfers between devices: 14.6 us -> 13.7 us
  local copies, waits for them, and re-layouts: 6.71 us -> 5.84 us
    ppermute x19, starting transfers between devices: 26.8 us -> 28.1 us  [swap(): return lax.ppermute(x, AXIS, [(i, i ^ bits) for i in range(size)])]
    ppermute x19, waiting for transfers between devices: 14.6 us -> 13.7 us  [swap(): return lax.ppermute(x, AXIS, [(i, i ^ bits) for i in range(size)])]
    dynamic_slice x3 -> x2, local copies, waits for them, and re-layouts: 3.84 us -> 2.97 us  [columns(): lax.dynamic_slice_in_dim(x, (index // 2 ^ k) * 2 * width, 2 * width, 1)]
  transfers between devices with their start and end apart: 19 -> 19, of which waited for: 8 -> 10; matrix products, arithmetic and copies ran while one was open for 13% -> 13% of each run, Pallas kernels for 4% -> 4%
where the time goes in v8:
time: 56.4 us; the launch traced here: 56.1 us
  starting transfers between devices  28.1 us (50%)
  waiting for transfers between devices  13.7 us (24%)
  Pallas kernels  6.77 us (12%)
  local copies, waits for them, and re-layouts  5.84 us (10%)
  other arithmetic  1.52 us (3%)
    ppermute x19, starting transfers between devices, swap(): return lax.ppermute(x, AXIS, [(i, i ^ bits) for i in range(size)])  28.1 us
    ppermute x19, waiting for transfers between devices, swap(): return lax.ppermute(x, AXIS, [(i, i ^ bits) for i in range(size)])  13.7 us
    pallas_call x1, Pallas kernels, project(): pl.pallas_call(functools.partial(project_kernel, layers=len(fields), part...  3.42 us
    dynamic_slice x2, local copies, waits for them, and re-layouts, columns(): lax.dynamic_slice_in_dim(x, (index // 2 ^ k) * 2 * width, 2 * width, 1)  2.97 us
    unnamed x7, local copies, waits for them, and re-layouts  2.87 us
    pallas_call x3, Pallas kernels, density_part(): pl.pallas_call(functools.partial(density_part_kernel, straight=straight),...  2.82 us
    concatenate x2, other arithmetic, body_slabs(): close.append(jnp.concatenate(parts, axis=1))  1.51 us
  transfers between devices with their start and end apart: 19, of which 10 were waited for; matrix products, arithmetic and copies ran while one was open for 13% of the time, Pallas kernels for 4%

profile of v8, /device:TPU:0, one launch (start us, length us, event | category | flops | bytes accessed | tf_op | source)
XLA Modules:
  0.0 56.1 jit_solution(2278447909289555105)
XLA Ops:
  0.0 4.0 %collective-permute-start = (bf16[64,128]{1,0:T(8,128)(2,1)}, bf16[64,128]{1,0:T(8,128)(2,1)S(1)}, u32[]{:S(2)}, u32[]{:S(2)}) collective-permute-start(bf16[64,128]{1,0:T(8,128)(2,1)} %param.5), channel_id=1, source_target_pairs={{0,8},{1,9},{2,10},{3,11},{4,12},{5,13},{6,14},{7,15},{8,0},{9,1},... | collective-permute-start | bytes 49160 | tf_op jit(solution)/shard_map/ppermute | solution.py:17
  4.0 1.8 %constant_dynamic-slice_fusion = (bf16[64,1024]{1,0:T(8,128)(2,1)S(1)}, bf16[64,1024]{1,0:T(8,128)(2,1)S(1)}, bf16[64,1024]{1,0:T(8,128)(2,1)}, bf16[64,1024]{1,0:T(8,128)(2,1)}) fusion(bf16[64,8192]{1,0:T(8,128)(2,1)} %param.6, s32[]{:T(128)S(6)} %select_n.44, s32[]{:T(128)S(6)} %select_n.42, s32[]{:T(128)S(6)} %select_n.41, s32[]{:T(128)S(6)} %select_n.43), kind=kLoop, calls=%fused_computation.14 | loop fusion | bytes 1048592 | tf_op jit(solution)/shard_map/dynamic_slice | solution.py:354
  5.9 2.3 %collective-permute-start.7 = (bf16[64,1024]{1,0:T(8,128)(2,1)S(1)}, bf16[64,1024]{1,0:T(8,128)(2,1)S(1)}, u32[]{:S(2)}, u32[]{:S(2)}) collective-permute-start(bf16[64,1024]{1,0:T(8,128)(2,1)S(1)} %get-tuple-element.49), channel_id=1, source_target_pairs={{0,14},{1,15},{2,12},{3,13},{4,10},{5,11},{6,8},{7,9},{8,6},{9,7},... | collective-permute-start | bytes 393224 | tf_op jit(solution)/shard_map/ppermute | solution.py:17
  8.2 1.6 %collective-permute-start.5 = (bf16[64,1024]{1,0:T(8,128)(2,1)S(1)}, bf16[64,1024]{1,0:T(8,128)(2,1)S(1)}, u32[]{:S(2)}, u32[]{:S(2)}) collective-permute-start(bf16[64,1024]{1,0:T(8,128)(2,1)S(1)} %get-tuple-element.50), channel_id=1, source_target_pairs={{0,10},{1,11},{2,8},{3,9},{4,14},{5,15},{6,12},{7,13},{8,2},{9,3},... | collective-permute-start | bytes 393224 | tf_op jit(solution)/shard_map/ppermute | solution.py:17
  9.8 1.1 %constant_dynamic-slice_fusion.4 = (bf16[64,1024]{1,0:T(8,128)(2,1)S(1)}, bf16[64,1024]{1,0:T(8,128)(2,1)S(1)}, bf16[64,1024]{1,0:T(8,128)(2,1)S(1)}, bf16[64,1024]{1,0:T(8,128)(2,1)S(1)}) fusion(bf16[64,8192]{1,0:T(8,128)(2,1)} %param.6, s32[]{:T(128)S(6)} %select_n.40, s32[]{:T(128)S(6)} %select_n.39, s32[]{:T(128)S(6)} %select_n.38, s32[]{:T(128)S(6)} %select_n.37), kind=kLoop, calls=%fused_computation.18 | loop fusion | bytes 1048592 | tf_op jit(solution)/shard_map/dynamic_slice | solution.py:354
  11.0 0.8 %pad_maximum_fusion.4 = (bf16[64,2304]{1,0:T(8,128)(2,1)}, bf16[64,2304]{1,0:T(8,128)(2,1)S(1)}) fusion(bf16[64,1024]{1,0:T(8,128)(2,1)S(1)} %copy-done, bf16[64,128]{1,0:T(8,128)(2,1)S(1)} %collective-permute-done, bf16[64,128]{1,0:T(8,128)(2,1)S(1)} %copy-done.1, bf16[64,1024]{1,0:T(8,128)(2,1)S(1)} %get-tuple-element.55, ...), kind=kLoop, calls=%fused_computation.4 | loop fusion | flops 1916928 | bytes 1015808 | tf_op jit(solution)/shard_map/concatenate | solution.py:364
  11.7 1.5 %collective-permute-start.1 = (bf16[64,2304]{1,0:T(8,128)(2,1)}, bf16[64,2304]{1,0:T(8,128)(2,1)S(1)}, u32[]{:S(2)}, u32[]{:S(2)}) collective-permute-start(bf16[64,2304]{1,0:T(8,128)(2,1)} %get-tuple-element.57), channel_id=1, source_target_pairs={{0,2},{1,3},{2,0},{3,1},{4,6},{5,7},{6,4},{7,5},{8,10},{9,11},{10,... | collective-permute-start | bytes 884744 | tf_op jit(solution)/shard_map/ppermute | solution.py:17
  13.2 0.8 %pad_maximum_fusion.6 = (bf16[64,1280]{1,0:T(8,128)(2,1)}, bf16[64,1280]{1,0:T(8,128)(2,1)}) fusion(bf16[64,128]{1,0:T(8,128)(2,1)S(1)} %collective-permute-done, bf16[64,128]{1,0:T(8,128)(2,1)S(1)} %copy-done.1, bf16[64,1024]{1,0:T(8,128)(2,1)S(1)} %get-tuple-element.53, bf16[64,1024]{1,0:T(8,128)(2,1)S(1)} %get-tuple-element.54), kind=kLoop, calls=%fused_computation.6 | loop fusion | flops 819200 | bytes 622592 | tf_op jit(solution)/shard_map/concatenate | solution.py:364
  14.0 1.3 %collective-permute-start.3 = (bf16[64,1280]{1,0:T(8,128)(2,1)}, bf16[64,1280]{1,0:T(8,128)(2,1)S(1)}, u32[]{:S(2)}, u32[]{:S(2)}) collective-permute-start(bf16[64,1280]{1,0:T(8,128)(2,1)} %get-tuple-element.59), channel_id=1, source_target_pairs={{0,6},{1,7},{2,4},{3,5},{4,2},{5,3},{6,0},{7,1},{8,14},{9,15},{10,... | collective-permute-start | bytes 491528 | tf_op jit(solution)/shard_map/ppermute | solution.py:17
  15.3 0.7 %collective-permute-start.2 = (bf16[64,1280]{1,0:T(8,128)(2,1)}, bf16[64,1280]{1,0:T(8,128)(2,1)S(1)}, u32[]{:S(2)}, u32[]{:S(2)}) collective-permute-start(bf16[64,1280]{1,0:T(8,128)(2,1)} %get-tuple-element.60), channel_id=1, source_target_pairs={{0,4},{1,5},{2,6},{3,7},{4,0},{5,1},{6,2},{7,3},{8,12},{9,13},{10,... | collective-permute-start | bytes 491528 | tf_op jit(solution)/shard_map/ppermute | solution.py:17
  16.0 4.5 %collective-permute-start.4 = (bf16[64,1024]{1,0:T(8,128)(2,1)}, bf16[64,1024]{1,0:T(8,128)(2,1)S(1)}, u32[]{:S(2)}, u32[]{:S(2)}) collective-permute-start(bf16[64,1024]{1,0:T(8,128)(2,1)} %get-tuple-element.51), channel_id=1, source_target_pairs={{0,8},{1,9},{2,10},{3,11},{4,12},{5,13},{6,14},{7,15},{8,0},{9,1},... | collective-permute-start | bytes 393224 | tf_op jit(solution)/shard_map/ppermute | solution.py:17
  20.5 1.7 %collective-permute-done.5.refs_6_.refs_5_ = bf16[64,1024]{1,0:T(8,128)(2,1)S(1)} collective-permute-done((bf16[64,1024]{1,0:T(8,128)(2,1)S(1)}, bf16[64,1024]{1,0:T(8,128)(2,1)S(1)}, u32[]{:S(2)}, u32[]{:S(2)}) %collective-permute-start.5) | collective-permute-done | bytes 131104 | tf_op jit(solution)/shard_map/ppermute | solution.py:17
  22.3 0.8 %collective-permute-start.6 = (bf16[64,1024]{1,0:T(8,128)(2,1)}, bf16[64,1024]{1,0:T(8,128)(2,1)S(1)}, u32[]{:S(2)}, u32[]{:S(2)}) collective-permute-start(bf16[64,1024]{1,0:T(8,128)(2,1)} %get-tuple-element.52), channel_id=1, source_target_pairs={{0,12},{1,13},{2,14},{3,15},{4,8},{5,9},{6,10},{7,11},{8,4},{9,5},... | collective-permute-start | bytes 393224 | tf_op jit(solution)/shard_map/ppermute | solution.py:17
  23.0 2.9 %copy.5 = bf16[16,512,128]{1,2,0:T(8,128)(2,1)S(1)} copy(bf16[16,512,128]{2,1,0:T(8,128)(2,1)} %param.4) | data formatting | bytes 4194304 | tf_op args[0]
  25.9 5.1 %collective-permute-done.4.refs_5_.refs_4_ = bf16[64,1024]{1,0:T(8,128)(2,1)S(1)} collective-permute-done((bf16[64,1024]{1,0:T(8,128)(2,1)}, bf16[64,1024]{1,0:T(8,128)(2,1)S(1)}, u32[]{:S(2)}, u32[]{:S(2)}) %collective-permute-start.4) | collective-permute-done | bytes 131104 | tf_op jit(solution)/shard_map/ppermute | solution.py:17
  31.7 1.3 %shard_map.46 = (bf16[16,512]{1,0:T(8,128)(2,1)S(1)}, bf16[512,512]{1,0:T(8,128)(2,1)S(1)}, bf16[128,512]{1,0:T(8,128)(2,1)S(1)}) custom-call(s32[1]{0:T(128)} %bitcast.index_ref, bf16[16,128,512]{2,1,0:T(8,128)(2,1)S(1)} %bitcast.2, bf16[64,2304]{1,0:T(8,128)(2,1)S(1)} %get-tuple-element.30.refs_1_.refs_0_.refs_4_, ...), custom_call_target="tpu_custom_call" | custom-call | flops 1073741824 | bytes 2097152 | tf_op jit(solution)/shard_map/pallas_call | solution.py:215
  33.0 0.8 %shard_map.48 = (bf16[16,256]{1,0:T(8,128)(2,1)S(1)}, bf16[256,512]{1,0:T(8,128)(2,1)S(1)}, bf16[128,256]{1,0:T(8,128)(2,1)S(1)}) custom-call(s32[1]{0:T(128)} %bitcast.index_ref, bf16[16,128,512]{2,1,0:T(8,128)(2,1)S(1)} %bitcast.3, bf16[64,3072]{1,0:T(8,128)(2,1)S(1)} %collective-permute-done.8.refs_1_), custom_call_target="tpu_custom_call" | custom-call | flops 536870912 | bytes 2097152 | tf_op jit(solution)/shard_map/pallas_call | solution.py:215
  33.8 0.8 %shard_map.49 = (bf16[16,256]{1,0:T(8,128)(2,1)S(1)}, bf16[256,512]{1,0:T(8,128)(2,1)S(1)}, bf16[128,256]{1,0:T(8,128)(2,1)S(1)}) custom-call(s32[1]{0:T(128)} %bitcast.index_ref, bf16[16,128,512]{2,1,0:T(8,128)(2,1)S(1)} %bitcast.4, bf16[64,3072]{1,0:T(8,128)(2,1)S(1)} %collective-permute-done.8.refs_1_, ...), custom_call_target="tpu_custom_call" | custom-call | flops 536870912 | bytes 2097152 | tf_op jit(solution)/shard_map/pallas_call | solution.py:215
  34.6 1.5 %collective-permute-start.12 = (bf16[16,1024]{1,0:T(8,128)(2,1)S(1)}, bf16[16,1024]{1,0:T(8,128)(2,1)S(1)}, u32[]{:S(2)}, u32[]{:S(2)}) collective-permute-start(bf16[16,1024]{1,0:T(8,128)(2,1)S(1)} %constant_dynamic-update-slice_fusion.refs_0_), channel_id=1, source_target_pairs={{0,12},{1,13},{2,14},{3,15},{4,8},{5,9},{6,10},{7,11},{8,4},{9,5},... | collective-permute-start | bytes 98312 | tf_op jit(solution)/shard_map/ppermute | solution.py:17
  36.1 2.4 %collective-permute-start.11 = (bf16[16,1024]{1,0:T(8,128)(2,1)S(1)}, bf16[16,1024]{1,0:T(8,128)(2,1)S(1)}, u32[]{:S(2)}, u32[]{:S(2)}) collective-permute-start(bf16[16,1024]{1,0:T(8,128)(2,1)S(1)} %constant_dynamic-update-slice_fusion.refs_0_), channel_id=1, source_target_pairs={{0,8},{1,9},{2,10},{3,11},{4,12},{5,13},{6,14},{7,15},{8,0},{9,1},... | collective-permute-start | bytes 98312 | tf_op jit(solution)/shard_map/ppermute | solution.py:17
  38.5 0.5 collective-permute-start.10
  39.0 1.6 %collective-permute-done.12.refs_3_ = bf16[16,1024]{1,0:T(8,128)(2,1)S(1)} collective-permute-done((bf16[16,1024]{1,0:T(8,128)(2,1)S(1)}, bf16[16,1024]{1,0:T(8,128)(2,1)S(1)}, u32[]{:S(2)}, u32[]{:S(2)}) %collective-permute-start.12) | collective-permute-done | bytes 32800 | tf_op jit(solution)/shard_map/ppermute | solution.py:17
  40.7 1.3 %collective-permute-done.11.refs_2_ = bf16[16,1024]{1,0:T(8,128)(2,1)S(1)} collective-permute-done((bf16[16,1024]{1,0:T(8,128)(2,1)S(1)}, bf16[16,1024]{1,0:T(8,128)(2,1)S(1)}, u32[]{:S(2)}, u32[]{:S(2)}) %collective-permute-start.11) | collective-permute-done | bytes 32800 | tf_op jit(solution)/shard_map/ppermute | solution.py:17
  41.9 0.5 collective-permute-done.10.refs_1_
  43.3 1.5 %collective-permute-start.13 = (bf16[16,256]{1,0:T(8,128)(2,1)S(1)}, bf16[16,256]{1,0:T(8,128)(2,1)S(1)}, u32[]{:S(2)}, u32[]{:S(2)}) collective-permute-start(bf16[16,256]{1,0:T(8,128)(2,1)S(1)} %shard_map.50), channel_id=1, source_target_pairs={{0,1},{1,0},{2,3},{3,2},{4,5},{5,4},{6,7},{7,6},{8,9},{9,8},{10,11... | collective-permute-start | bytes 24584 | tf_op jit(solution)/shard_map/ppermute | solution.py:17
  44.8 1.2 %collective-permute-done.15 = bf16[16,256]{1,0:T(8,128)(2,1)S(1)} collective-permute-done((bf16[16,256]{1,0:T(8,128)(2,1)S(1)}, bf16[16,256]{1,0:T(8,128)(2,1)S(1)}, u32[]{:S(2)}, u32[]{:S(2)}) %collective-permute-start.15) | collective-permute-done | bytes 8224 | tf_op jit(solution)/shard_map/ppermute | solution.py:17
  46.0 0.6 %collective-permute-done.14 = bf16[16,256]{1,0:T(8,128)(2,1)S(1)} collective-permute-done((bf16[16,256]{1,0:T(8,128)(2,1)S(1)}, bf16[16,256]{1,0:T(8,128)(2,1)S(1)}, u32[]{:S(2)}, u32[]{:S(2)}) %collective-permute-start.14) | collective-permute-done | bytes 8224 | tf_op jit(solution)/shard_map/ppermute | solution.py:17
  46.6 1.4 %collective-permute-start.18 = (bf16[16,256]{1,0:T(8,128)(2,1)S(1)}, bf16[16,256]{1,0:T(8,128)(2,1)S(1)}, u32[]{:S(2)}, u32[]{:S(2)}) collective-permute-start(bf16[16,256]{1,0:T(8,128)(2,1)S(1)} %add_convert_fusion.refs_0_), channel_id=1, source_target_pairs={{0,12},{1,13},{2,14},{3,15},{4,8},{5,9},{6,10},{7,11},{8,4},{9,5},... | collective-permute-start | bytes 24584 | tf_op jit(solution)/shard_map/ppermute | solution.py:17
  48.0 0.6 %collective-permute-start.17 = (bf16[16,256]{1,0:T(8,128)(2,1)S(1)}, bf16[16,256]{1,0:T(8,128)(2,1)S(1)}, u32[]{:S(2)}, u32[]{:S(2)}) collective-permute-start(bf16[16,256]{1,0:T(8,128)(2,1)S(1)} %add_convert_fusion.refs_0_), channel_id=1, source_target_pairs={{0,8},{1,9},{2,10},{3,11},{4,12},{5,13},{6,14},{7,15},{8,0},{9,1},... | collective-permute-start | bytes 24584 | tf_op jit(solution)/shard_map/ppermute | solution.py:17
  48.7 2.4 %collective-permute-start.16 = (bf16[16,256]{1,0:T(8,128)(2,1)S(1)}, bf16[16,256]{1,0:T(8,128)(2,1)S(1)}, u32[]{:S(2)}, u32[]{:S(2)}) collective-permute-start(bf16[16,256]{1,0:T(8,128)(2,1)S(1)} %add_convert_fusion.refs_0_), channel_id=1, source_target_pairs={{0,4},{1,5},{2,6},{3,7},{4,0},{5,1},{6,2},{7,3},{8,12},{9,13},{10,... | collective-permute-start | bytes 24584 | tf_op jit(solution)/shard_map/ppermute | solution.py:17
  51.1 1.1 %collective-permute-done.18.refs_3_ = bf16[16,256]{1,0:T(8,128)(2,1)S(1)} collective-permute-done((bf16[16,256]{1,0:T(8,128)(2,1)S(1)}, bf16[16,256]{1,0:T(8,128)(2,1)S(1)}, u32[]{:S(2)}, u32[]{:S(2)}) %collective-permute-start.18) | collective-permute-done | bytes 8224 | tf_op jit(solution)/shard_map/ppermute | solution.py:17
  52.7 3.4 %shard_map.51 = bf16[16,512,128]{2,1,0:T(8,128)(2,1)} custom-call(s32[1]{0:T(128)} %bitcast.index_ref, bf16[16,256]{1,0:T(8,128)(2,1)S(1)} %add_convert_fusion.refs_0_, bf16[16,256]{1,0:T(8,128)(2,1)S(1)} %collective-permute-done.16.refs_1_, bf16[16,256]{1,0:T(8,128)(2,1)S(1)} %collective-permute-done.17.refs_2_, ...), custom_call_target="tpu_custom_call" | custom-call | flops 2147483648 | bytes 2097152 | tf_op jit(solution)/shard_map/pallas_call | solution.py:323
  (25 shorter events, 2.2 us)
Async XLA Ops:
  0.0 11.0 %copy-start.1 = (bf16[64,128]{1,0:T(8,128)(2,1)S(1)}, bf16[64,128]{1,0:T(8,128)(2,1)}, u32[]{:S(2)}) copy-start(bf16[64,128]{1,0:T(8,128)(2,1)} %param.5) | copy-start | bytes 49156
  0.0 11.0 %copy-start = (bf16[64,1024]{1,0:T(8,128)(2,1)S(1)}, bf16[64,1024]{1,0:T(8,128)(2,1)}, u32[]{:S(2)}) copy-start(bf16[64,1024]{1,0:T(8,128)(2,1)} %param.7) | copy-start | bytes 393220
  0.0 9.8 %collective-permute-start = (bf16[64,128]{1,0:T(8,128)(2,1)}, bf16[64,128]{1,0:T(8,128)(2,1)S(1)}, u32[]{:S(2)}, u32[]{:S(2)}) collective-permute-start(bf16[64,128]{1,0:T(8,128)(2,1)} %param.5), channel_id=1, source_target_pairs={{0,8},{1,9},{2,10},{3,11},{4,12},{5,13},{6,14},{7,15},{8,0},{9,1},... | collective-permute-start | bytes 49160 | tf_op jit(solution)/shard_map/ppermute | solution.py:17
  5.9 10.1 %collective-permute-start.7 = (bf16[64,1024]{1,0:T(8,128)(2,1)S(1)}, bf16[64,1024]{1,0:T(8,128)(2,1)S(1)}, u32[]{:S(2)}, u32[]{:S(2)}) collective-permute-start(bf16[64,1024]{1,0:T(8,128)(2,1)S(1)} %get-tuple-element.49), channel_id=1, source_target_pairs={{0,14},{1,15},{2,12},{3,13},{4,10},{5,11},{6,8},{7,9},{8,6},{9,7},... | collective-permute-start | bytes 393224 | tf_op jit(solution)/shard_map/ppermute | solution.py:17
  8.2 14.1 %collective-permute-start.5 = (bf16[64,1024]{1,0:T(8,128)(2,1)S(1)}, bf16[64,1024]{1,0:T(8,128)(2,1)S(1)}, u32[]{:S(2)}, u32[]{:S(2)}) collective-permute-start(bf16[64,1024]{1,0:T(8,128)(2,1)S(1)} %get-tuple-element.50), channel_id=1, source_target_pairs={{0,10},{1,11},{2,8},{3,9},{4,14},{5,15},{6,12},{7,13},{8,2},{9,3},... | collective-permute-start | bytes 393224 | tf_op jit(solution)/shard_map/ppermute | solution.py:17
  11.7 19.3 %collective-permute-start.1 = (bf16[64,2304]{1,0:T(8,128)(2,1)}, bf16[64,2304]{1,0:T(8,128)(2,1)S(1)}, u32[]{:S(2)}, u32[]{:S(2)}) collective-permute-start(bf16[64,2304]{1,0:T(8,128)(2,1)} %get-tuple-element.57), channel_id=1, source_target_pairs={{0,2},{1,3},{2,0},{3,1},{4,6},{5,7},{6,4},{7,5},{8,10},{9,11},{10,... | collective-permute-start | bytes 884744 | tf_op jit(solution)/shard_map/ppermute | solution.py:17
  14.0 17.0 %collective-permute-start.3 = (bf16[64,1280]{1,0:T(8,128)(2,1)}, bf16[64,1280]{1,0:T(8,128)(2,1)S(1)}, u32[]{:S(2)}, u32[]{:S(2)}) collective-permute-start(bf16[64,1280]{1,0:T(8,128)(2,1)} %get-tuple-element.59), channel_id=1, source_target_pairs={{0,6},{1,7},{2,4},{3,5},{4,2},{5,3},{6,0},{7,1},{8,14},{9,15},{10,... | collective-permute-start | bytes 491528 | tf_op jit(solution)/shard_map/ppermute | solution.py:17
  15.3 15.7 %collective-permute-start.2 = (bf16[64,1280]{1,0:T(8,128)(2,1)}, bf16[64,1280]{1,0:T(8,128)(2,1)S(1)}, u32[]{:S(2)}, u32[]{:S(2)}) collective-permute-start(bf16[64,1280]{1,0:T(8,128)(2,1)} %get-tuple-element.60), channel_id=1, source_target_pairs={{0,4},{1,5},{2,6},{3,7},{4,0},{5,1},{6,2},{7,3},{8,12},{9,13},{10,... | collective-permute-start | bytes 491528 | tf_op jit(solution)/shard_map/ppermute | solution.py:17
  16.0 15.0 %collective-permute-start.4 = (bf16[64,1024]{1,0:T(8,128)(2,1)}, bf16[64,1024]{1,0:T(8,128)(2,1)S(1)}, u32[]{:S(2)}, u32[]{:S(2)}) collective-permute-start(bf16[64,1024]{1,0:T(8,128)(2,1)} %get-tuple-element.51), channel_id=1, source_target_pairs={{0,8},{1,9},{2,10},{3,11},{4,12},{5,13},{6,14},{7,15},{8,0},{9,1},... | collective-permute-start | bytes 393224 | tf_op jit(solution)/shard_map/ppermute | solution.py:17
  22.3 8.7 %collective-permute-start.6 = (bf16[64,1024]{1,0:T(8,128)(2,1)}, bf16[64,1024]{1,0:T(8,128)(2,1)S(1)}, u32[]{:S(2)}, u32[]{:S(2)}) collective-permute-start(bf16[64,1024]{1,0:T(8,128)(2,1)} %get-tuple-element.52), channel_id=1, source_target_pairs={{0,12},{1,13},{2,14},{3,15},{4,8},{5,9},{6,10},{7,11},{8,4},{9,5},... | collective-permute-start | bytes 393224 | tf_op jit(solution)/shard_map/ppermute | solution.py:17
  31.1 1.9 %collective-permute-start.8 = (bf16[64,3072]{1,0:T(8,128)(2,1)S(1)}, bf16[64,3072]{1,0:T(8,128)(2,1)S(1)}, u32[]{:S(2)}, u32[]{:S(2)}) collective-permute-start(bf16[64,3072]{1,0:T(8,128)(2,1)S(1)} %get-tuple-element.39), channel_id=1, source_target_pairs={{0,1},{1,0},{2,3},{3,2},{4,5},{5,4},{6,7},{7,6},{8,9},{9,8},{10,11... | collective-permute-start | bytes 1179656 | tf_op jit(solution)/shard_map/ppermute | solution.py:17
  31.2 2.6 %collective-permute-start.9 = (bf16[64,4096]{1,0:T(8,128)(2,1)S(1)}, bf16[64,4096]{1,0:T(8,128)(2,1)S(1)}, u32[]{:S(2)}, u32[]{:S(2)}) collective-permute-start(bf16[64,4096]{1,0:T(8,128)(2,1)S(1)} %get-tuple-element.41), channel_id=1, source_target_pairs={{0,1},{1,0},{2,3},{3,2},{4,5},{5,4},{6,7},{7,6},{8,9},{9,8},{10,11... | collective-permute-start | bytes 1572872 | tf_op jit(solution)/shard_map/ppermute | solution.py:17
  34.6 6.1 %collective-permute-start.12 = (bf16[16,1024]{1,0:T(8,128)(2,1)S(1)}, bf16[16,1024]{1,0:T(8,128)(2,1)S(1)}, u32[]{:S(2)}, u32[]{:S(2)}) collective-permute-start(bf16[16,1024]{1,0:T(8,128)(2,1)S(1)} %constant_dynamic-update-slice_fusion.refs_0_), channel_id=1, source_target_pairs={{0,12},{1,13},{2,14},{3,15},{4,8},{5,9},{6,10},{7,11},{8,4},{9,5},... | collective-permute-start | bytes 98312 | tf_op jit(solution)/shard_map/ppermute | solution.py:17
  36.1 5.8 %collective-permute-start.11 = (bf16[16,1024]{1,0:T(8,128)(2,1)S(1)}, bf16[16,1024]{1,0:T(8,128)(2,1)S(1)}, u32[]{:S(2)}, u32[]{:S(2)}) collective-permute-start(bf16[16,1024]{1,0:T(8,128)(2,1)S(1)} %constant_dynamic-update-slice_fusion.refs_0_), channel_id=1, source_target_pairs={{0,8},{1,9},{2,10},{3,11},{4,12},{5,13},{6,14},{7,15},{8,0},{9,1},... | collective-permute-start | bytes 98312 | tf_op jit(solution)/shard_map/ppermute | solution.py:17
  38.5 3.9 %collective-permute-start.10 = (bf16[16,1024]{1,0:T(8,128)(2,1)S(1)}, bf16[16,1024]{1,0:T(8,128)(2,1)S(1)}, u32[]{:S(2)}, u32[]{:S(2)}) collective-permute-start(bf16[16,1024]{1,0:T(8,128)(2,1)S(1)} %constant_dynamic-update-slice_fusion.refs_0_), channel_id=1, source_target_pairs={{0,4},{1,5},{2,6},{3,7},{4,0},{5,1},{6,2},{7,3},{8,12},{9,13},{10,... | collective-permute-start | bytes 98312 | tf_op jit(solution)/shard_map/ppermute | solution.py:17
  42.9 3.1 %collective-permute-start.15 = (bf16[16,256]{1,0:T(8,128)(2,1)S(1)}, bf16[16,256]{1,0:T(8,128)(2,1)S(1)}, u32[]{:S(2)}, u32[]{:S(2)}) collective-permute-start(bf16[16,256]{1,0:T(8,128)(2,1)S(1)} %shard_map.50), channel_id=1, source_target_pairs={{0,3},{1,2},{2,1},{3,0},{4,7},{5,6},{6,5},{7,4},{8,11},{9,10},{10,... | collective-permute-start | bytes 24584 | tf_op jit(solution)/shard_map/ppermute | solution.py:17
  42.9 3.7 %collective-permute-start.14 = (bf16[16,256]{1,0:T(8,128)(2,1)S(1)}, bf16[16,256]{1,0:T(8,128)(2,1)S(1)}, u32[]{:S(2)}, u32[]{:S(2)}) collective-permute-start(bf16[16,256]{1,0:T(8,128)(2,1)S(1)} %shard_map.50), channel_id=1, source_target_pairs={{0,2},{1,3},{2,0},{3,1},{4,6},{5,7},{6,4},{7,5},{8,10},{9,11},{10,... | collective-permute-start | bytes 24584 | tf_op jit(solution)/shard_map/ppermute | solution.py:17
  43.3 3.3 %collective-permute-start.13 = (bf16[16,256]{1,0:T(8,128)(2,1)S(1)}, bf16[16,256]{1,0:T(8,128)(2,1)S(1)}, u32[]{:S(2)}, u32[]{:S(2)}) collective-permute-start(bf16[16,256]{1,0:T(8,128)(2,1)S(1)} %shard_map.50), channel_id=1, source_target_pairs={{0,1},{1,0},{2,3},{3,2},{4,5},{5,4},{6,7},{7,6},{8,9},{9,8},{10,11... | collective-permute-start | bytes 24584 | tf_op jit(solution)/shard_map/ppermute | solution.py:17
  46.6 5.5 %collective-permute-start.18 = (bf16[16,256]{1,0:T(8,128)(2,1)S(1)}, bf16[16,256]{1,0:T(8,128)(2,1)S(1)}, u32[]{:S(2)}, u32[]{:S(2)}) collective-permute-start(bf16[16,256]{1,0:T(8,128)(2,1)S(1)} %add_convert_fusion.refs_0_), channel_id=1, source_target_pairs={{0,12},{1,13},{2,14},{3,15},{4,8},{5,9},{6,10},{7,11},{8,4},{9,5},... | collective-permute-start | bytes 24584 | tf_op jit(solution)/shard_map/ppermute | solution.py:17
  48.0 4.5 %collective-permute-start.17 = (bf16[16,256]{1,0:T(8,128)(2,1)S(1)}, bf16[16,256]{1,0:T(8,128)(2,1)S(1)}, u32[]{:S(2)}, u32[]{:S(2)}) collective-permute-start(bf16[16,256]{1,0:T(8,128)(2,1)S(1)} %add_convert_fusion.refs_0_), channel_id=1, source_target_pairs={{0,8},{1,9},{2,10},{3,11},{4,12},{5,13},{6,14},{7,15},{8,0},{9,1},... | collective-permute-start | bytes 24584 | tf_op jit(solution)/shard_map/ppermute | solution.py:17
  48.7 4.0 %collective-permute-start.16 = (bf16[16,256]{1,0:T(8,128)(2,1)S(1)}, bf16[16,256]{1,0:T(8,128)(2,1)S(1)}, u32[]{:S(2)}, u32[]{:S(2)}) collective-permute-start(bf16[16,256]{1,0:T(8,128)(2,1)S(1)} %add_convert_fusion.refs_0_), channel_id=1, source_target_pairs={{0,4},{1,5},{2,6},{3,7},{4,0},{5,1},{6,2},{7,3},{8,12},{9,13},{10,... | collective-permute-start | bytes 24584 | tf_op jit(solution)/shard_map/ppermute | solution.py:17
